TPU v7x, 32 devices: a whole 2x2x4 slice. The times are simulated.
32 devices in a mesh: seq: 8 (over y, x, core), head: 4 (over z).
Axes of the slice: x: 2, y: 2, z: 4, core: 2. Of those that a mesh axis runs over, the one named last changes fastest.
Arguments:
- inputs: bfloat16 [32, 512, 768], P('seq'), may hold values from -6 to 6
- out_grad: bfloat16 [32, 512, 768], P('seq'), may hold values from -16 to 16
- w_query: bfloat16 [768, 512], P(None, 'head'), may hold values from -0.21875 to 0.21875
- w_key: bfloat16 [768, 512], P(None, 'head'), may hold values from -0.21875 to 0.21875
- w_value: bfloat16 [768, 512], P(None, 'head'), may hold values from -0.21875 to 0.21875
- w_output: bfloat16 [512, 768], P('head'), may hold values from -0.25 to 0.25
Outputs:
- grad_inputs: bfloat16 [32, 512, 768], P('seq', 'head')
- grad_wq: float32 [768, 512], P(None, 'head')
- grad_wk: float32 [768, 512], P(None, 'head')
- grad_wv: float32 [768, 512], P(None, 'head')
- grad_wo: float32 [512, 768], P('head')
All inputs are finite; a program needn't handle non-finite values.
Results may differ from a plain program's by a relative error of at most 0.012.
Values may be sent and summed in bfloat16 or wider, within the bound.
No kernel may reach another device: no remote copies, remote signals or barrier semaphores. Data moves between devices by JAX's collectives and lax.ppermute only.
A program may use at most 64 MiB of HBM per device.

v0:
```python
import math

import jax
import jax.numpy as jnp
from jax import lax
from jax.sharding import PartitionSpec as P

HEAD_DIM = 64


def times_transpose(left, right):
    return lax.dot_general(
        left, right, (((1,), (1,)), ((), ())), preferred_element_type=jnp.float32
    )


def first_contract(left, right):
    return lax.dot_general(
        left, right, (((0,), (0,)), ((), ())), preferred_element_type=jnp.float32
    )


def softmax_rows(logits):
    exponent = jnp.exp(logits)
    attn_probs = exponent / jnp.sum(exponent, axis=2, keepdims=True)
    return (attn_probs, attn_probs.astype(jnp.bfloat16))


def score_grad(attn_probs, grad_probs, logit_scale):
    row_inner = jnp.sum(attn_probs * grad_probs, axis=2, keepdims=True)
    return (logit_scale * attn_probs * (grad_probs - row_inner)).astype(jnp.bfloat16)


def body(inputs, out_grad, w_query, w_key, w_value, w_output):
    row_count, col_count, model_width = inputs.shape
    local_width = w_query.shape[1]
    head_count = local_width // HEAD_DIM
    all_rows = row_count * lax.axis_size("seq")
    logit_scale = 1.0 / (math.sqrt(HEAD_DIM) * math.sqrt(all_rows))
    inv_root = 1.0 / math.sqrt(all_rows * col_count)
    shape_heads = (row_count, col_count, head_count, HEAD_DIM)
    full_query, full_key, full_value = (
        lax.all_gather(w_query, "head", axis=1, tiled=True),
        lax.all_gather(w_key, "head", axis=1, tiled=True),
        lax.all_gather(w_value, "head", axis=1, tiled=True),
    )
    flat_in = inputs.reshape(-1, model_width)
    flat_grad = out_grad.reshape(-1, model_width)
    query_proj = jnp.dot(flat_in, w_query, preferred_element_type=jnp.float32).astype(jnp.bfloat16)
    key_proj = jnp.dot(flat_in, w_key, preferred_element_type=jnp.float32).astype(jnp.bfloat16)
    value_proj = jnp.dot(flat_in, w_value, preferred_element_type=jnp.float32).astype(jnp.bfloat16)
    grad_att = times_transpose(flat_grad, w_output).astype(jnp.bfloat16)
    query_four = query_proj.reshape(shape_heads)
    key_four = key_proj.reshape(shape_heads)
    value_four = value_proj.reshape(shape_heads)
    grad_four = grad_att.reshape(shape_heads)
    part_logits = jnp.einsum(
        "rihe,rjhe->hij", query_four, key_four, preferred_element_type=jnp.float32
    )
    part_probs = jnp.einsum(
        "rihe,rjhe->hij", grad_four, value_four, preferred_element_type=jnp.float32
    )
    summed = lax.psum(part_logits, "seq")
    attn_probs, probs_low = softmax_rows(logit_scale * summed)
    grad_probs = lax.psum(part_probs, "seq")
    grad_logits = score_grad(attn_probs, grad_probs, logit_scale)
    attended = jnp.einsum(
        "hij,rjhe->rihe", probs_low, value_four, preferred_element_type=jnp.float32
    )
    attended = attended.astype(jnp.bfloat16).reshape(-1, local_width)
    part_wo = first_contract(attended, flat_grad)
    grad_value = jnp.einsum(
        "hij,rihe->rjhe", probs_low, grad_four, preferred_element_type=jnp.float32
    )
    grad_query = jnp.einsum(
        "hij,rjhe->rihe", grad_logits, key_four, preferred_element_type=jnp.float32
    )
    grad_key = jnp.einsum(
        "hij,rihe->rjhe", grad_logits, query_four, preferred_element_type=jnp.float32
    )
    flat_q = grad_query.astype(jnp.bfloat16).reshape(-1, local_width)
    flat_k = grad_key.astype(jnp.bfloat16).reshape(-1, local_width)
    flat_v = grad_value.astype(jnp.bfloat16).reshape(-1, local_width)
    three_q = flat_q.reshape(row_count, col_count, local_width)
    three_k = flat_k.reshape(row_count, col_count, local_width)
    three_v = flat_v.reshape(row_count, col_count, local_width)
    moved_q, moved_k, moved_v = (
        lax.all_to_all(three_q, "head", split_axis=1, concat_axis=2, tiled=True),
        lax.all_to_all(three_k, "head", split_axis=1, concat_axis=2, tiled=True),
        lax.all_to_all(three_v, "head", split_axis=1, concat_axis=2, tiled=True),
    )
    block_cols = moved_q.shape[1]
    full_width = moved_q.shape[2]
    block_in = times_transpose(moved_q.reshape(-1, full_width), full_query)
    block_in = block_in + times_transpose(moved_k.reshape(-1, full_width), full_key)
    block_in = block_in + times_transpose(moved_v.reshape(-1, full_width), full_value)
    grad_inputs = block_in.astype(jnp.bfloat16).reshape(row_count, block_cols, model_width)
    part_wq = first_contract(flat_in, flat_q)
    part_wk = first_contract(flat_in, flat_k)
    part_wv = first_contract(flat_in, flat_v)
    sum_wq, sum_wk, sum_wv, sum_wo = lax.psum((part_wq, part_wk, part_wv, part_wo), "seq")
    return (grad_inputs, sum_wq * inv_root, sum_wk * inv_root, sum_wv * inv_root, sum_wo * inv_root)


def solution(mesh):
    return jax.shard_map(
        body,
        mesh=mesh,
        in_specs=(
            P("seq", None, None),
            P("seq", None, None),
            P(None, "head"),
            P(None, "head"),
            P(None, "head"),
            P("head", None),
        ),
        out_specs=(
            P("seq", "head", None),
            P(None, "head"),
            P(None, "head"),
            P(None, "head"),
            P("head", None),
        ),
        check_vma=False,
    )
```

profile of v0, /device:TPU:0, one launch (start us, length us, event | category | flops | bytes accessed | tf_op | source)
XLA Modules:
  0.0 298.2 jit_solution(11326383675340243878)
XLA Ops:
  9.1 2.7 convolution_convert_fusion.2
  11.8 3.2 %reshape.76 = bf16[4,512,2,64]{3,2,1,0:T(2,128)(2,1)} reshape(bf16[2048,128]{1,0:T(8,128)(2,1)} %convolution_convert_fusion.2) | data formatting | bytes 1048576 | tf_op jit(solution)/shard_map/reshape | solution.py:53
  15.0 3.6 %copy.49 = bf16[4,512,2,64]{1,3,0,2:T(8,128)(2,1)} copy(bf16[4,512,2,64]{3,2,1,0:T(2,128)(2,1)} %reshape.76) | data formatting | bytes 1048576 | tf_op jit(solution)/shard_map/reshape | solution.py:53
  20.3 3.2 %reshape.75 = bf16[4,512,2,64]{3,2,1,0:T(2,128)(2,1)} reshape(bf16[2048,128]{1,0:T(8,128)(2,1)} %convolution_convert_fusion.3) | data formatting | bytes 1048576 | tf_op jit(solution)/shard_map/reshape | solution.py:54
  23.5 3.5 %copy.55 = bf16[4,512,2,64]{1,3,0,2:T(8,128)(2,1)} copy(bf16[4,512,2,64]{3,2,1,0:T(2,128)(2,1)} %reshape.75) | data formatting | bytes 1048576 | tf_op jit(solution)/shard_map/reshape | solution.py:54
  28.9 3.2 %reshape.78 = bf16[4,512,2,64]{3,2,1,0:T(2,128)(2,1)} reshape(bf16[2048,128]{1,0:T(8,128)(2,1)} %convolution_convert_fusion) | data formatting | bytes 1048576 | tf_op jit(solution)/shard_map/reshape | solution.py:55
  32.1 3.5 %copy.54 = bf16[4,512,2,64]{1,3,0,2:T(8,128)(2,1)} copy(bf16[4,512,2,64]{3,2,1,0:T(2,128)(2,1)} %reshape.78) | data formatting | bytes 1048576 | tf_op jit(solution)/shard_map/reshape | solution.py:55
  35.6 3.7 %convolution_convert_fusion.1 = bf16[2048,128]{1,0:T(8,128)(2,1)} fusion(bf16[2048,768]{1,0:T(8,128)(2,1)} %bitcast.123, bf16[128,768]{1,0:T(8,128)(2,1)S(1)} %copy-done.17), kind=kOutput, calls=%fused_computation.2 | convolution fusion | flops 402915328 | bytes 3866624 | tf_op jit(solution)/shard_map/dot_general | solution.py:12
  39.3 3.2 %reshape.77 = bf16[4,512,2,64]{3,2,1,0:T(2,128)(2,1)} reshape(bf16[2048,128]{1,0:T(8,128)(2,1)} %convolution_convert_fusion.1) | data formatting | bytes 1048576 | tf_op jit(solution)/shard_map/reshape | solution.py:56
  42.5 3.5 %copy.53 = bf16[4,512,2,64]{1,3,0,2:T(8,128)(2,1)} copy(bf16[4,512,2,64]{3,2,1,0:T(2,128)(2,1)} %reshape.77) | data formatting | bytes 1048576 | tf_op jit(solution)/shard_map/reshape | solution.py:56
  46.0 3.1 %convolution_bitcast_fusion.1 = f32[2,512,512]{2,1,0:T(8,128)} fusion(bf16[4,512,2,64]{1,3,0,2:T(8,128)(2,1)} %copy.49, bf16[4,512,2,64]{1,3,0,2:T(8,128)(2,1)} %copy.55), kind=kOutput, calls=%fused_computation.12 | convolution fusion | flops 268435456 | bytes 3145728 | tf_op jit(solution)/shard_map/rihe,rjhe->hij/dot_general | solution.py:57
  51.0 84.1 %all-reduce.7.cloned.1.call-done = (f32[2,512,512]{2,1,0:T(8,128)}, f32[2,512,512]{2,1,0:T(8,128)}) async-done(((f32[2,512,512]{2,1,0:T(8,128)}, f32[2,512,512]{2,1,0:T(8,128)}), (f32[2,512,512]{2,1,0:T(8,128)}, f32[2,512,512]{2,1,0:T(8,128)})) %all-reduce.7.cloned.1.call-update) | async-done | bytes 4194320 | tf_op jit(solution)/shard_map/psum | solution.py:65
  135.1 2.1 fusion.3
  137.3 2.5 fusion.21
  141.3 9.9 %fusion.23 = bf16[4,512,2,64]{1,3,0,2:T(8,128)(2,1)} fusion(bf16[4,512,2,64]{1,3,0,2:T(8,128)(2,1)} %copy.49, f32[2,512,512]{2,1,0:T(8,128)} %get-tuple-element.24, f32[2,512,512]{2,1,0:T(8,128)} %get-tuple-element.25, f32[2,512]{1,0:T(2,128)S(1)} %fusion.3), kind=kOutput, calls=%fused_computation.23 | convolution fusion | flops 273417728 | bytes 5246976 | tf_op jit(solution)/shard_map/hij,rihe->rjhe/dot_general | solution.py:78
  156.0 2.1 copy.61
  158.1 4.6 %all-to-all-start.1 = ((bf16[4,512,128]{2,0,1:T(4,128)(2,1)}), bf16[4,512,128]{2,0,1:T(4,128)(2,1)}, u32[]{:S(2)}, u32[]{:S(2)}) async-start(bf16[4,512,128]{2,0,1:T(4,128)(2,1)} %copy.61), calls=%async_computation.1 | async-start | bytes 1048576 | tf_op jit(solution)/shard_map/all_to_all | solution.py:89
  162.7 9.7 %fusion.26 = bf16[4,512,2,64]{1,3,0,2:T(8,128)(2,1)} fusion(bf16[4,512,2,64]{1,3,0,2:T(8,128)(2,1)} %copy.55, f32[2,512,512]{2,1,0:T(8,128)} %get-tuple-element.24, f32[2,512,512]{2,1,0:T(8,128)} %get-tuple-element.25, f32[2,512]{1,0:T(2,128)S(1)} %fusion.3), kind=kOutput, calls=%fused_computation.24 | convolution fusion | flops 273417728 | bytes 5246976 | tf_op jit(solution)/shard_map/hij,rjhe->rihe/dot_general | solution.py:75
  173.9 1.9 copy.56
  179.3 2.1 copy.57
  181.5 2.4 convolution_bitcast_fusion.4
  185.2 5.1 %all-to-all-start = ((bf16[4,512,128]{2,0,1:T(4,128)(2,1)}), bf16[4,512,128]{2,0,1:T(4,128)(2,1)}, u32[]{:S(2)}, u32[]{:S(2)}) async-start(bf16[4,512,128]{2,0,1:T(4,128)(2,1)} %copy.57), calls=%async_computation | async-start | bytes 1048576 | tf_op jit(solution)/shard_map/all_to_all | solution.py:88
  190.3 3.4 %fusion.53 = f32[128,768]{1,0:T(8,128)} fusion(bf16[2048,128]{0,1:T(8,128)(2,1)} %bitcast.135, bf16[2048,768]{1,0:T(8,128)(2,1)} %bitcast.124), kind=kOutput, calls=%fused_computation.50 | convolution fusion | flops 402653184 | bytes 4063232 | tf_op jit(solution)/shard_map/dot_general | solution.py:18
  193.8 26.9 %all_gather.10 = bf16[768,512]{1,0:T(8,128)(2,1)} all-gather(bf16[768,128]{1,0:T(8,128)(2,1)S(1)} %copy-done.11), channel_id=1, replica_groups=mesh['seq'=8,'head'=4] {'head'}, dimensions={1}, use_global_device_ids=true | all-gather | bytes 983040 | tf_op jit(solution)/shard_map/all_gather | solution.py:44
  220.7 22.1 %all_gather.9 = bf16[768,512]{1,0:T(8,128)(2,1)} all-gather(bf16[768,128]{1,0:T(8,128)(2,1)S(1)} %copy-done.12), channel_id=1, replica_groups=mesh['seq'=8,'head'=4] {'head'}, dimensions={1}, use_global_device_ids=true | all-gather | bytes 983040 | tf_op jit(solution)/shard_map/all_gather | solution.py:43
  243.5 2.1 copy.65
  245.7 4.1 %all-to-all-start.2 = ((bf16[4,512,128]{2,0,1:T(4,128)(2,1)}), bf16[4,512,128]{2,0,1:T(4,128)(2,1)}, u32[]{:S(2)}, u32[]{:S(2)}) async-start(bf16[4,512,128]{2,0,1:T(4,128)(2,1)} %copy.65), calls=%async_computation.2 | async-start | bytes 1048576 | tf_op jit(solution)/shard_map/all_to_all | solution.py:90
  249.8 23.4 %all_gather.11 = bf16[768,512]{1,0:T(8,128)(2,1)} all-gather(bf16[768,128]{1,0:T(8,128)(2,1)S(1)} %copy-done.14), channel_id=1, replica_groups=mesh['seq'=8,'head'=4] {'head'}, dimensions={1}, use_global_device_ids=true | all-gather | bytes 983040 | tf_op jit(solution)/shard_map/all_gather | solution.py:45
  273.3 1.9 broadcast_multiply_fusion.1
  275.2 1.9 copy.73
  279.9 2.3 copy.62
  282.2 2.2 copy.58
  (68 shorter events, 30.6 us)
Async XLA Ops:
  7.2 1.9 copy-start
  7.2 127.9 %all-reduce.7.cloned.1.call-start = ((), (), s32[]{:S(2)}) async-start(), calls=%async_computation.4 | async-start | bytes 8388608 | tf_op jit(solution)/shard_map/psum | solution.py:65
  11.8 6.8 %copy-start.11 = (bf16[768,128]{1,0:T(8,128)(2,1)S(1)}, bf16[768,128]{1,0:T(8,128)(2,1)}, u32[]{:S(2)}) copy-start(bf16[768,128]{1,0:T(8,128)(2,1)} %param.9) | copy-start | bytes 589828
  20.3 6.7 %copy-start.13 = (bf16[768,128]{1,0:T(8,128)(2,1)S(1)}, bf16[768,128]{1,0:T(8,128)(2,1)}, u32[]{:S(2)}) copy-start(bf16[768,128]{1,0:T(8,128)(2,1)} %param.10) | copy-start | bytes 589828
  28.9 6.8 %copy-start.17 = (bf16[128,768]{1,0:T(8,128)(2,1)S(1)}, bf16[128,768]{1,0:T(8,128)(2,1)}, u32[]{:S(2)}) copy-start(bf16[128,768]{1,0:T(8,128)(2,1)} %param.11) | copy-start | bytes 589828
  46.0 3.1 %copy-start.6 = (bf16[4,512,2,64]{1,3,0,2:T(8,128)(2,1)S(1)}, bf16[4,512,2,64]{1,3,0,2:T(8,128)(2,1)}, u32[]{:S(2)}) copy-start(bf16[4,512,2,64]{1,3,0,2:T(8,128)(2,1)} %copy.54) | copy-start | bytes 1572868
  46.0 3.1 %copy-start.8 = (bf16[4,512,2,64]{1,3,0,2:T(8,128)(2,1)S(1)}, bf16[4,512,2,64]{1,3,0,2:T(8,128)(2,1)}, u32[]{:S(2)}) copy-start(bf16[4,512,2,64]{1,3,0,2:T(8,128)(2,1)} %copy.53) | copy-start | bytes 1572868
  135.1 2.2 copy-start.3
  137.3 2.6 copy-start.7
  158.1 27.1 %all-to-all-start.1 = ((bf16[4,512,128]{2,0,1:T(4,128)(2,1)}), bf16[4,512,128]{2,0,1:T(4,128)(2,1)}, u32[]{:S(2)}, u32[]{:S(2)}) async-start(bf16[4,512,128]{2,0,1:T(4,128)(2,1)} %copy.61), calls=%async_computation.1 | async-start | bytes 1048576 | tf_op jit(solution)/shard_map/all_to_all | solution.py:89
  172.4 4.3 %copy-start.4 = (bf16[4,512,2,64]{1,3,0,2:T(8,128)(2,1)S(1)}, bf16[4,512,2,64]{1,3,0,2:T(8,128)(2,1)}, u32[]{:S(2)}) copy-start(bf16[4,512,2,64]{1,3,0,2:T(8,128)(2,1)} %fusion.21) | copy-start | bytes 1572868
  173.9 4.1 %copy-start.15 = (bf16[4,512,2,64]{1,3,0,2:T(8,128)(2,1)S(1)}, bf16[4,512,2,64]{1,3,0,2:T(8,128)(2,1)}, u32[]{:S(2)}) copy-start(bf16[4,512,2,64]{1,3,0,2:T(8,128)(2,1)} %fusion.22) | copy-start | bytes 1572868
  181.5 2.4 copy-start.10
  185.2 60.4 %all-to-all-start = ((bf16[4,512,128]{2,0,1:T(4,128)(2,1)}), bf16[4,512,128]{2,0,1:T(4,128)(2,1)}, u32[]{:S(2)}, u32[]{:S(2)}) async-start(bf16[4,512,128]{2,0,1:T(4,128)(2,1)} %copy.57), calls=%async_computation | async-start | bytes 1048576 | tf_op jit(solution)/shard_map/all_to_all | solution.py:88
  190.3 82.9 %all-reduce.5.cloned.1.call-start = ((), (), s32[]{:S(2)}) async-start(), calls=%async_computation.3 | async-start | bytes 3145728 | tf_op jit(solution)/shard_map/psum | solution.py:101
  193.7 26.9 %copy-start.12 = (bf16[768,128]{1,0:T(8,128)(2,1)S(1)}, bf16[768,128]{1,0:T(8,128)(2,1)}, u32[]{:S(2)}) copy-start(bf16[768,128]{1,0:T(8,128)(2,1)} %param.8) | copy-start | bytes 589828
  193.8 49.0 %copy-start.5 = (bf16[4,512,2,64]{1,3,0,2:T(8,128)(2,1)S(1)}, bf16[4,512,2,64]{1,3,0,2:T(8,128)(2,1)}, u32[]{:S(2)}) copy-start(bf16[4,512,2,64]{1,3,0,2:T(8,128)(2,1)} %fusion.21) | copy-start | bytes 1572868
  220.7 29.2 %copy-start.14 = (bf16[768,128]{1,0:T(8,128)(2,1)S(1)}, bf16[768,128]{1,0:T(8,128)(2,1)}, u32[]{:S(2)}) copy-start(bf16[768,128]{1,0:T(8,128)(2,1)} %param.10) | copy-start | bytes 589828
  245.7 39.6 %all-to-all-start.2 = ((bf16[4,512,128]{2,0,1:T(4,128)(2,1)}), bf16[4,512,128]{2,0,1:T(4,128)(2,1)}, u32[]{:S(2)}, u32[]{:S(2)}) async-start(bf16[4,512,128]{2,0,1:T(4,128)(2,1)} %copy.65), calls=%async_computation.2 | async-start | bytes 1048576 | tf_op jit(solution)/shard_map/all_to_all | solution.py:90
  279.9 4.6 %copy-start.16 = (f32[128,768]{1,0:T(8,128)S(1)}, f32[128,768]{1,0:T(8,128)}, u32[]{:S(2)}) copy-start(f32[128,768]{1,0:T(8,128)} %get-tuple-element.23) | copy-start | bytes 1179652
  285.3 3.5 %copy-start.2 = (bf16[768,512]{1,0:T(8,128)(2,1)S(1)}, bf16[768,512]{1,0:T(8,128)(2,1)}, u32[]{:S(2)}) copy-start(bf16[768,512]{1,0:T(8,128)(2,1)} %all_gather.9) | copy-start | bytes 2359300
  285.3 3.5 %copy-start.9 = (bf16[4,4,128,128]{3,1,2,0:T(4,128)(2,1)S(1)}, bf16[4,4,128,128]{3,1,2,0:T(4,128)(2,1)}, u32[]{:S(2)}) copy-start(bf16[4,4,128,128]{3,1,2,0:T(4,128)(2,1)} %copy.58) | copy-start | bytes 1572868
  288.7 1.1 copy-start.1
Sparse Core Ops, SparseCore 0:
  51.1 83.9 all-reduce.6
  195.6 59.8 all-reduce.4
where the time goes:
time: 300 us; the launch traced here: 298 us
  waiting for transfers between devices  84.1 us (28%)
  blocking collectives  72.4 us (24%)
  local copies, waits for them, and re-layouts  56.8 us (19%)
  matrix products  51 us (17%)
  between operations  14.2 us (5%)
  starting transfers between devices  13.9 us (5%)
  other arithmetic  5.81 us (2%)
    psum x1, waiting for transfers between devices, body(): grad_probs = lax.psum(part_probs, 'seq')  84.1 us
    all_gather x1, blocking collectives, body(): lax.all_gather(w_key, 'head', axis=1, tiled=True)  26.9 us
    all_gather x1, blocking collectives, body(): lax.all_gather(w_value, 'head', axis=1, tiled=True)  23.4 us
    all_gather x1, blocking collectives, body(): lax.all_gather(w_query, 'head', axis=1, tiled=True)  22.1 us
    dot_general x1, matrix products, body(): jnp.einsum('hij,rihe->rjhe', grad_logits, query_four, preferred_element_t...  9.95 us
    dot_general x1, matrix products, body(): jnp.einsum('hij,rjhe->rihe', grad_logits, key_four, preferred_element_typ...  9.68 us
    unnamed x43, local copies, waits for them, and re-layouts  9.03 us
    dot_general x4, matrix products, first_contract(): lax.dot_general(left, right, (((0,), (0,)), ((), ())), preferred_element_...  8.47 us
  transfers between devices with their start and end apart: 5, of which 1 were waited for; matrix products, arithmetic and copies ran while one was open for 14% of the time, Pallas kernels for 0%

commit v1 on v0

v1 whole, which is shorter than its diff:
```python
import math
from functools import partial

import jax
import jax.numpy as jnp
from jax import lax
from jax.experimental import pallas as pl
from jax.experimental.pallas import tpu as pltpu
from jax.sharding import PartitionSpec as P

HEAD_DIM = 64
F32 = jnp.float32
BF16 = jnp.bfloat16
VMEM_BYTES = 40 * 1024 * 1024


def dot_nn(left, right):
    return lax.dot_general(left, right, (((1,), (0,)), ((), ())), preferred_element_type=F32)


def dot_nt(left, right):
    return lax.dot_general(left, right, (((1,), (1,)), ((), ())), preferred_element_type=F32)


def vmem_spec():
    return pl.BlockSpec(memory_space=pltpu.VMEM)


def smem_spec():
    return pl.BlockSpec(memory_space=pltpu.SMEM)


def call(kernel, outs, ins, scratch=(), flops=0, moved=0, name=None):
    return pl.pallas_call(
        kernel,
        out_shape=outs,
        in_specs=[smem_spec()] + [vmem_spec()] * (len(ins) - 1),
        out_specs=jax.tree.map(lambda _: vmem_spec(), outs),
        scratch_shapes=list(scratch),
        compiler_params=pltpu.CompilerParams(vmem_limit_bytes=VMEM_BYTES),
        cost_estimate=pl.CostEstimate(flops=flops, bytes_accessed=moved, transcendentals=0),
        name=name,
    )(*ins)


def front_kernel(place, x, og, wq, wk, wv, wo, wt, qt, kt, vt, gt, keep, give, qn, gn):
    step = pl.program_id(0)
    width = wq.shape[1]
    heads = width // HEAD_DIM
    pieces, piece_rows, _ = keep.shape
    cols = kt.shape[2]

    @pl.when(step == 0)
    def _():
        wt[0:width, :] = wq[...].T
        wt[width : 2 * width, :] = wk[...].T
        wt[2 * width : 3 * width, :] = wv[...].T

    three = dot_nt(wt[...], x[0]).astype(BF16)
    one = dot_nt(wo[...], og[0]).astype(BF16)
    rows = pl.ds(pl.multiple_of(step * HEAD_DIM, HEAD_DIM), HEAD_DIM)
    for h in range(heads):
        at = h * HEAD_DIM
        qt[h, rows, :] = three[at : at + HEAD_DIM]
        kt[h, rows, :] = three[width + at : width + at + HEAD_DIM]
        vt[h, rows, :] = three[2 * width + at : 2 * width + at + HEAD_DIM]
        gt[h, rows, :] = one[at : at + HEAD_DIM]

    @pl.when(step == pl.num_programs(0) - 1)
    def _():
        chip, core = place[0], place[1]
        for h in range(heads):
            qn[...] = qt[h].T
            gn[...] = gt[h].T
            for i in range(0, cols, piece_rows):
                shard = (h * cols + i) // piece_rows
                logits = dot_nn(qn[i : i + piece_rows, :], kt[h]).astype(BF16)
                probs = dot_nn(gn[i : i + piece_rows, :], vt[h]).astype(BF16)
                slot = jnp.bitwise_xor(chip, shard // 2)

                @pl.when(core == shard % 2)
                def _():
                    keep[slot, :, 0:cols] = logits
                    keep[slot, :, cols:] = probs

                @pl.when(core != shard % 2)
                def _():
                    give[slot, :, 0:cols] = logits
                    give[slot, :, cols:] = probs


def pair_kernel(place, keep, got, *outs):
    for k, out in enumerate(outs):
        out[...] = (keep[k].astype(F32) + got[k].astype(F32)).astype(out.dtype)


def score_kernel(logit_scale, place, *refs):
    *parts, out = refs
    cols = out.shape[1] // 2
    total = parts[0][...].astype(F32)
    for part in parts[1:]:
        total = total + part[...].astype(F32)
    exponent = jnp.exp(total[:, 0:cols] * logit_scale)
    probs = exponent / jnp.sum(exponent, axis=1, keepdims=True)
    grad = total[:, cols:]
    inner = jnp.sum(probs * grad, axis=1, keepdims=True)
    out[:, 0:cols] = probs.astype(BF16)
    out[:, cols:] = (logit_scale * probs * (grad - inner)).astype(BF16)


def grads_kernel(pieces, place, *refs):
    mine, other = refs[0:pieces], refs[pieces : 2 * pieces]
    qt, kt, vt, gt = refs[2 * pieces : 2 * pieces + 4]
    sends = refs[2 * pieces + 4 : -4]
    three, att, probs, grads = refs[-4:]
    heads, merged, cols = qt.shape
    rows = merged // HEAD_DIM
    width = heads * HEAD_DIM
    piece_rows = mine[0].shape[0]
    chip, core, zed = place[0], place[1], place[2]
    for k in range(pieces):
        base = 2 * jnp.bitwise_xor(chip, k)
        for side, part in ((core, mine[k]), (1 - core, other[k])):
            at = pl.ds(pl.multiple_of((base + side) * piece_rows, piece_rows), piece_rows)
            probs[at, :] = part[:, 0:cols]
            grads[at, :] = part[:, cols:]
    for h in range(heads):
        p = probs[h * cols : (h + 1) * cols, :]
        s = grads[h * cols : (h + 1) * cols, :]
        grad_q = dot_nt(kt[h], s).astype(BF16)
        grad_k = dot_nn(qt[h], s).astype(BF16)
        grad_v = dot_nn(gt[h], p).astype(BF16)
        attended = dot_nt(vt[h], p).astype(BF16)
        for r in range(rows):
            src = slice(r * HEAD_DIM, (r + 1) * HEAD_DIM)
            for t, value in enumerate((grad_q, grad_k, grad_v)):
                at = t * width + h * HEAD_DIM
                three[r, at : at + HEAD_DIM, :] = value[src]
            att[r, h * HEAD_DIM : (h + 1) * HEAD_DIM, :] = attended[src]
    block = cols // len(sends)
    for k, send in enumerate(sends):
        at = pl.multiple_of(jnp.bitwise_xor(zed, k) * block, block)
        for r in range(rows):
            send[:, r * block : (r + 1) * block] = three[r, :, pl.ds(at, block)]


def weights_kernel(place, x, og, three, att, keep, give, total):
    step = pl.program_id(0)
    depth = three.shape[1]
    pieces, piece_rows, _ = keep.shape

    @pl.when(step == 0)
    def _():
        total[...] = jnp.zeros_like(total)

    total[0:depth, :] += dot_nn(three[0], x[0])
    total[depth:, :] += dot_nn(att[0], og[0])

    @pl.when(step == pl.num_programs(0) - 1)
    def _():
        chip, core = place[0], place[1]
        for k in range(pieces):
            base = 2 * jnp.bitwise_xor(chip, k)
            mine = pl.ds(pl.multiple_of((base + core) * piece_rows, piece_rows), piece_rows)
            other = pl.ds(pl.multiple_of((base + 1 - core) * piece_rows, piece_rows), piece_rows)
            keep[k] = total[mine, :].astype(BF16)
            give[k] = total[other, :].astype(BF16)


def sum_kernel(scale, place, *refs):
    *parts, out = refs
    total = parts[0][...].astype(F32)
    for part in parts[1:]:
        total = total + part[...].astype(F32)
    out[...] = (total * scale).astype(out.dtype)


def unpack_kernel(pieces, place, *refs):
    mine, other = refs[0:pieces], refs[pieces : 2 * pieces]
    outs, full = refs[2 * pieces : -1], refs[-1]
    piece_rows = mine[0].shape[0]
    chip, core = place[0], place[1]
    for k in range(pieces):
        base = 2 * jnp.bitwise_xor(chip, k)
        for side, part in ((core, mine[k]), (1 - core, other[k])):
            at = pl.ds(pl.multiple_of((base + side) * piece_rows, piece_rows), piece_rows)
            full[at, :] = part[...].astype(F32)
    width = full.shape[0] // len(outs)
    for t, out in enumerate(outs[:-1]):
        out[...] = full[t * width : (t + 1) * width, :].T
    outs[-1][...] = full[(len(outs) - 1) * width :, :]


def inputs_kernel(count, place, *refs):
    sent = refs[0:count]
    mine, other = refs[count : 2 * count], refs[2 * count : 3 * count]
    out = refs[-1]
    rows, block, model = out.shape
    half = model // 2
    core = place[1]
    lefts = [part[...].T for part in sent]
    for side, parts in ((core, mine), (1 - core, other)):
        total = dot_nn(lefts[0], parts[0][...])
        for left, part in zip(lefts[1:], parts[1:]):
            total = total + dot_nn(left, part[...])
        total = total.astype(BF16)
        at = pl.ds(pl.multiple_of(side * half, 128), half)
        for r in range(rows):
            out[r, :, at] = total[r * block : (r + 1) * block]


def body(inputs, out_grad, w_query, w_key, w_value, w_output):
    rows, cols, model = inputs.shape
    width = w_query.shape[1]
    heads = width // HEAD_DIM
    merged = rows * HEAD_DIM
    seqs, zeds = lax.axis_size("seq"), lax.axis_size("head")
    pieces = seqs // 2
    all_rows = rows * seqs
    logit_scale = 1.0 / (math.sqrt(HEAD_DIM) * math.sqrt(all_rows))
    inv_root = 1.0 / math.sqrt(all_rows * cols)
    shard = heads * cols // seqs
    wide = 4 * width // seqs
    me = lax.axis_index("seq")
    zed = lax.axis_index("head")
    place = jnp.stack([me // 2, me % 2, zed]).astype(jnp.int32)

    def swap(value):
        return lax.ppermute(value, "seq", [(i, i ^ 1) for i in range(seqs)])

    def across(value, k):
        return lax.ppermute(value, "seq", [(i, i ^ (2 * k)) for i in range(seqs)])

    def along(value, k):
        return lax.ppermute(value, "head", [(i, i ^ k) for i in range(zeds)])

    def shape(*dims, dtype=BF16):
        return jax.ShapeDtypeStruct(dims, dtype)

    whole = lambda *dims: pl.BlockSpec(dims, lambda r: (0,) * len(dims))
    row = pl.BlockSpec((1, cols, model), lambda r: (r, 0, 0))
    wt, qt, kt, vt, gt, keep, give = pl.pallas_call(
        front_kernel,
        grid=(rows,),
        out_shape=(
            shape(3 * width, model),
            shape(heads, merged, cols),
            shape(heads, merged, cols),
            shape(heads, merged, cols),
            shape(heads, merged, cols),
            shape(pieces, shard, 2 * cols),
            shape(pieces, shard, 2 * cols),
        ),
        in_specs=[smem_spec(), row, row]
        + [whole(model, width)] * 3
        + [whole(width, model)],
        out_specs=[whole(3 * width, model)]
        + [whole(heads, merged, cols)] * 4
        + [whole(pieces, shard, 2 * cols)] * 2,
        scratch_shapes=[pltpu.VMEM((cols, merged), BF16)] * 2,
        compiler_params=pltpu.CompilerParams(vmem_limit_bytes=VMEM_BYTES),
        name="front",
    )(place, inputs, out_grad, w_query, w_key, w_value, w_output)

    half = model // 2
    my_half = lax.dynamic_slice_in_dim(wt, (me % 2) * half, half, axis=1)
    mine_w = [my_half] + [along(my_half, k) for k in range(1, zeds)]
    other_w = [swap(value) for value in mine_w]

    got = swap(give)
    paired = call(
        pair_kernel, [shape(shard, 2 * cols)] * pieces, (place, keep, got), name="pair"
    )
    parts = [paired[0]] + [across(paired[k], k) for k in range(1, pieces)]
    scored = call(
        partial(score_kernel, logit_scale), shape(shard, 2 * cols), (place, *parts), name="score"
    )
    mine = [scored] + [across(scored, k) for k in range(1, pieces)]
    other = [swap(value) for value in mine]

    block = cols // zeds
    *sends, three, att = call(
        partial(grads_kernel, pieces),
        [shape(3 * width, rows * block)] * zeds
        + [shape(rows, 3 * width, cols), shape(rows, width, cols)],
        (place, *mine, *other, qt, kt, vt, gt),
        scratch=[pltpu.VMEM((heads * cols, cols), BF16)] * 2,
        name="grads",
    )
    sent = [sends[0]] + [along(sends[k], k) for k in range(1, zeds)]

    keep_w, give_w = pl.pallas_call(
        weights_kernel,
        grid=(rows,),
        out_shape=(shape(pieces, wide, model), shape(pieces, wide, model)),
        in_specs=[
            smem_spec(),
            row,
            row,
            pl.BlockSpec((1, 3 * width, cols), lambda r: (r, 0, 0)),
            pl.BlockSpec((1, width, cols), lambda r: (r, 0, 0)),
        ],
        out_specs=[whole(pieces, wide, model)] * 2,
        scratch_shapes=[pltpu.VMEM((4 * width, model), F32)],
        compiler_params=pltpu.CompilerParams(vmem_limit_bytes=VMEM_BYTES),
        name="weights",
    )(place, inputs, out_grad, three, att)
    got_w = swap(give_w)
    paired_w = call(
        pair_kernel, [shape(wide, model)] * pieces, (place, keep_w, got_w), name="pair_w"
    )
    parts_w = [paired_w[0]] + [across(paired_w[k], k) for k in range(1, pieces)]
    summed = call(partial(sum_kernel, inv_root), shape(wide, model), (place, *parts_w), name="sum_w")
    mine_g = [summed] + [across(summed, k) for k in range(1, pieces)]
    other_g = [swap(value) for value in mine_g]
    grad_q, grad_k, grad_v, grad_o = call(
        partial(unpack_kernel, pieces),
        [shape(model, width, dtype=F32)] * 3 + [shape(width, model, dtype=F32)],
        (place, *mine_g, *other_g),
        scratch=[pltpu.VMEM((4 * width, model), F32)],
        name="unpack",
    )
    grad_inputs = call(
        partial(inputs_kernel, zeds),
        shape(rows, block, model),
        (place, *sent, *mine_w, *other_w),
        name="inputs",
    )
    return (grad_inputs, grad_q, grad_k, grad_v, grad_o)


def solution(mesh):
    return jax.shard_map(
        body,
        mesh=mesh,
        in_specs=(
            P("seq", None, None),
            P("seq", None, None),
            P(None, "head"),
            P(None, "head"),
            P(None, "head"),
            P("head", None),
        ),
        out_specs=(
            P("seq", "head", None),
            P(None, "head"),
            P(None, "head"),
            P(None, "head"),
            P("head", None),
        ),
        check_vma=False,
    )
```

time: 300 us -> 135 us (0.45)
  the two profiles are of different devices: /device:TPU:0 before, /device:TPU:8 now
where the time goes in v1:
time: 135 us; the launch traced here: 134 us
  waiting for transfers between devices  74.7 us (55%)
  starting transfers between devices  24.2 us (18%)
  Pallas kernels  20.2 us (15%)
  local copies, waits for them, and re-layouts  14.6 us (11%)
    ppermute x6, waiting for transfers between devices, along(): return lax.ppermute(value, 'head', [(i, i ^ k) for i in range(zeds)])  46.2 us
    ppermute x12, waiting for transfers between devices, across(): return lax.ppermute(value, 'seq', [(i, i ^ 2 * k) for i in range(seqs)])  25.6 us
    ppermute x12, starting transfers between devices, across(): return lax.ppermute(value, 'seq', [(i, i ^ 2 * k) for i in range(seqs)])  14.4 us
    unnamed x34, local copies, waits for them, and re-layouts  13.6 us
    pallas_call x7, Pallas kernels, call(): pl.pallas_call(kernel, out_shape=outs, in_specs=[smem_spec()] + [vmem_spe...  11.4 us
    ppermute x6, starting transfers between devices, along(): return lax.ppermute(value, 'head', [(i, i ^ k) for i in range(zeds)])  6.77 us
    pallas_call x1, Pallas kernels, body(): pl.pallas_call(front_kernel, grid=(rows,), out_shape=(shape(3 * width, mo...  5.68 us
    pallas_call x1, Pallas kernels, body(): pl.pallas_call(weights_kernel, grid=(rows,), out_shape=(shape(pieces, wid...  3.1 us
  transfers between devices with their start and end apart: 32, of which 12 were waited for; matrix products, arithmetic and copies ran while one was open for 1% of the time, Pallas kernels for 8%

profile of v1, /device:TPU:8, one launch (start us, length us, event | category | flops | bytes accessed | tf_op | source)
XLA Modules:
  0.0 134.5 jit_solution(7391133656696022595)
XLA Ops:
  0.7 1.9 %copy-done = bf16[4,512,768]{2,1,0:T(8,128)(2,1)S(1)} copy-done((bf16[4,512,768]{2,1,0:T(8,128)(2,1)S(1)}, bf16[4,512,768]{2,1,0:T(8,128)(2,1)}, u32[]{:S(2)}) %copy-start) | copy-done | bytes 3145752
  2.6 1.9 %copy-done.2 = bf16[4,512,768]{2,1,0:T(8,128)(2,1)S(1)} copy-done((bf16[4,512,768]{2,1,0:T(8,128)(2,1)S(1)}, bf16[4,512,768]{2,1,0:T(8,128)(2,1)}, u32[]{:S(2)}) %copy-start.2) | copy-done | bytes 3145752
  8.2 5.7 %front.1 = (bf16[384,768]{1,0:T(8,128)(2,1)S(1)}, bf16[2,256,512]{2,1,0:T(8,128)(2,1)S(1)}, bf16[2,256,512]{2,1,0:T(8,128)(2,1)S(1)}, bf16[2,256,512]{2,1,0:T(8,...) custom-call(s32[3]{0:T(128)S(1)} %pad_add_fusion.place, ...), custom_call_target="tpu_custom_call" | custom-call | tf_op jit(solution)/shard_map/front/pallas_call | solution.py:242
  14.0 2.6 %collective-permute-done.got = bf16[4,128,1024]{2,1,0:T(8,128)(2,1)S(1)} collective-permute-done((bf16[4,128,1024]{2,1,0:T(8,128)(2,1)S(1)}, bf16[4,128,1024]{2,1,0:T(8,128)(2,1)S(1)}, u32[]{:S(2)}, u32[]{:S(2)}) %collective-permute-start) | collective-permute-done | bytes 1048608 | tf_op jit(solution)/shard_map/ppermute | solution.py:229
  17.5 1.6 %collective-permute-start.1 = (bf16[128,1024]{1,0:T(8,128)(2,1)S(1)}, bf16[128,1024]{1,0:T(8,128)(2,1)S(1)}, u32[]{:S(2)}, u32[]{:S(2)}) collective-permute-start(bf16[128,1024]{1,0:T(8,128)(2,1)S(1)} %get-tuple-element.35), channel_id=1, source_target_pairs={{0,8},{4,12},{8,0},{12,4},{16,24},{20,28},{24,16},{28,20},{1,9},{5... | collective-permute-start | bytes 786440 | tf_op jit(solution)/shard_map/ppermute | solution.py:232
  19.0 1.5 %collective-permute-start.2 = (bf16[128,1024]{1,0:T(8,128)(2,1)S(1)}, bf16[128,1024]{1,0:T(8,128)(2,1)S(1)}, u32[]{:S(2)}, u32[]{:S(2)}) collective-permute-start(bf16[128,1024]{1,0:T(8,128)(2,1)S(1)} %get-tuple-element.36), channel_id=1, source_target_pairs={{0,16},{4,20},{8,24},{12,28},{16,0},{20,4},{24,8},{28,12},{1,17},{... | collective-permute-start | bytes 786440 | tf_op jit(solution)/shard_map/ppermute | solution.py:232
  21.0 5.7 %collective-permute-done.1.refs_1_ = bf16[128,1024]{1,0:T(8,128)(2,1)S(1)} collective-permute-done((bf16[128,1024]{1,0:T(8,128)(2,1)S(1)}, bf16[128,1024]{1,0:T(8,128)(2,1)S(1)}, u32[]{:S(2)}, u32[]{:S(2)}) %collective-permute-start.1) | collective-permute-done | bytes 262176 | tf_op jit(solution)/shard_map/ppermute | solution.py:232
  26.7 6.0 %collective-permute-done.2.refs_2_ = bf16[128,1024]{1,0:T(8,128)(2,1)S(1)} collective-permute-done((bf16[128,1024]{1,0:T(8,128)(2,1)S(1)}, bf16[128,1024]{1,0:T(8,128)(2,1)S(1)}, u32[]{:S(2)}, u32[]{:S(2)}) %collective-permute-start.2) | collective-permute-done | bytes 262176 | tf_op jit(solution)/shard_map/ppermute | solution.py:232
  33.5 1.6 %collective-permute-start.6 = (bf16[128,1024]{1,0:T(8,128)(2,1)S(1)}, bf16[128,1024]{1,0:T(8,128)(2,1)}, u32[]{:S(2)}, u32[]{:S(2)}) collective-permute-start(bf16[128,1024]{1,0:T(8,128)(2,1)S(1)} %score.1.refs_0_), channel_id=1, source_target_pairs={{0,24},{4,28},{8,16},{12,20},{16,8},{20,12},{24,0},{28,4},{1,25},{... | collective-permute-start | bytes 786440 | tf_op jit(solution)/shard_map/ppermute | solution.py:232
  35.1 1.5 %collective-permute-start.4 = (bf16[128,1024]{1,0:T(8,128)(2,1)S(1)}, bf16[128,1024]{1,0:T(8,128)(2,1)}, u32[]{:S(2)}, u32[]{:S(2)}) collective-permute-start(bf16[128,1024]{1,0:T(8,128)(2,1)S(1)} %score.1.refs_0_), channel_id=1, source_target_pairs={{0,8},{4,12},{8,0},{12,4},{16,24},{20,28},{24,16},{28,20},{1,9},{5... | collective-permute-start | bytes 786440 | tf_op jit(solution)/shard_map/ppermute | solution.py:232
  37.1 6.8 %collective-permute-done.6.refs_3_ = bf16[128,1024]{1,0:T(8,128)(2,1)} collective-permute-done((bf16[128,1024]{1,0:T(8,128)(2,1)S(1)}, bf16[128,1024]{1,0:T(8,128)(2,1)}, u32[]{:S(2)}, u32[]{:S(2)}) %collective-permute-start.6) | collective-permute-done | bytes 262176 | tf_op jit(solution)/shard_map/ppermute | solution.py:232
  43.9 3.6 %collective-permute-done.4.refs_1_ = bf16[128,1024]{1,0:T(8,128)(2,1)} collective-permute-done((bf16[128,1024]{1,0:T(8,128)(2,1)S(1)}, bf16[128,1024]{1,0:T(8,128)(2,1)}, u32[]{:S(2)}, u32[]{:S(2)}) %collective-permute-start.4) | collective-permute-done | bytes 262176 | tf_op jit(solution)/shard_map/ppermute | solution.py:232
  49.8 1.0 copy-done.5
  52.9 1.0 copy-done.11
  54.0 3.1 %grads.1 = (bf16[384,512]{1,0:T(8,128)(2,1)S(1)}, bf16[384,512]{1,0:T(8,128)(2,1)S(1)}, bf16[384,512]{1,0:T(8,128)(2,1)S(1)}, bf16[384,512]{1,0:T(8,128)(2,1)S(1...) custom-call(s32[3]{0:T(128)S(1)} %pad_add_fusion.place, bf16[128,1024]{1,0:T(8,128)(2,1)S(1)} %score.1.refs_0_, ...), custom_call_target="tpu_custom_call" | custom-call | tf_op jit(solution)/shard_map/grads/pallas_call | solution.py:34
  57.0 1.9 %copy-done.3 = bf16[4,512,768]{2,1,0:T(8,128)(2,1)S(1)} copy-done((bf16[4,512,768]{2,1,0:T(8,128)(2,1)S(1)}, bf16[4,512,768]{2,1,0:T(8,128)(2,1)}, u32[]{:S(2)}) %copy-start.3) | copy-done | bytes 3145752
  58.9 3.1 %weights.1 = (bf16[4,64,768]{2,1,0:T(8,128)(2,1)S(1)}, bf16[4,64,768]{2,1,0:T(8,128)(2,1)S(1)}) custom-call(s32[3]{0:T(128)S(1)} %pad_add_fusion.place, bf16[4,512,768]{2,1,0:T(8,128)(2,1)S(1)} %copy-done.1, bf16[4,512,768]{2,1,0:T(8,128)(2,1)S(1)} %copy-done.3, bf16[4,384,512]{2,1,0:T(8,128)(2,1)S(1)} %get-tuple-element.47.three, ...), custom_call_target="tpu_custom_call" | custom-call | tf_op jit(solution)/shard_map/weights/pallas_call | solution.py:292
  62.3 2.6 %collective-permute-start.15 = (bf16[384,384]{1,0:T(8,128)(2,1)S(1)}, bf16[384,384]{1,0:T(8,128)(2,1)S(1)}, u32[]{:S(2)}, u32[]{:S(2)}) collective-permute-start(bf16[384,384]{1,0:T(8,128)(2,1)S(1)} %constant_dynamic-slice_fusion.refs_4_), channel_id=1, source_target_pairs={{0,2},{1,3},{2,0},{3,1},{4,6},{5,7},{6,4},{7,5},{8,10},{9,11},{10,... | collective-permute-start | bytes 884744 | tf_op jit(solution)/shard_map/ppermute | solution.py:235
  66.3 1.1 collective-permute-start.22
  67.4 17.5 %collective-permute-done.15.refs_6_ = bf16[384,384]{1,0:T(8,128)(2,1)S(1)} collective-permute-done((bf16[384,384]{1,0:T(8,128)(2,1)S(1)}, bf16[384,384]{1,0:T(8,128)(2,1)S(1)}, u32[]{:S(2)}, u32[]{:S(2)}) %collective-permute-start.15) | collective-permute-done | bytes 294944 | tf_op jit(solution)/shard_map/ppermute | solution.py:235
  84.9 1.0 collective-permute-start.23
  86.0 5.4 %collective-permute-done.16.refs_7_ = bf16[384,384]{1,0:T(8,128)(2,1)S(1)} collective-permute-done((bf16[384,384]{1,0:T(8,128)(2,1)S(1)}, bf16[384,384]{1,0:T(8,128)(2,1)S(1)}, u32[]{:S(2)}, u32[]{:S(2)}) %collective-permute-start.16) | collective-permute-done | bytes 294944 | tf_op jit(solution)/shard_map/ppermute | solution.py:235
  91.4 3.1 %collective-permute-start.12 = (bf16[384,512]{1,0:T(8,128)(2,1)S(1)}, bf16[384,512]{1,0:T(8,128)(2,1)S(1)}, u32[]{:S(2)}, u32[]{:S(2)}) collective-permute-start(bf16[384,512]{1,0:T(8,128)(2,1)S(1)} %get-tuple-element.44), channel_id=1, source_target_pairs={{0,2},{1,3},{2,0},{3,1},{4,6},{5,7},{6,4},{7,5},{8,10},{9,11},{10,... | collective-permute-start | bytes 1179656 | tf_op jit(solution)/shard_map/ppermute | solution.py:235
  94.5 1.5 %collective-permute-start.24 = (bf16[64,768]{1,0:T(8,128)(2,1)S(1)}, bf16[64,768]{1,0:T(8,128)(2,1)S(1)}, u32[]{:S(2)}, u32[]{:S(2)}) collective-permute-start(bf16[64,768]{1,0:T(8,128)(2,1)S(1)} %get-tuple-element.54), channel_id=1, source_target_pairs={{0,24},{4,28},{8,16},{12,20},{16,8},{20,12},{24,0},{28,4},{1,25},{... | collective-permute-start | bytes 294920 | tf_op jit(solution)/shard_map/ppermute | solution.py:232
  96.6 3.5 %collective-permute-done.24.refs_3_ = bf16[64,768]{1,0:T(8,128)(2,1)S(1)} collective-permute-done((bf16[64,768]{1,0:T(8,128)(2,1)S(1)}, bf16[64,768]{1,0:T(8,128)(2,1)S(1)}, u32[]{:S(2)}, u32[]{:S(2)}) %collective-permute-start.24) | collective-permute-done | bytes 98336 | tf_op jit(solution)/shard_map/ppermute | solution.py:232
  102.1 1.1 collective-permute-start.26
  103.1 4.7 %collective-permute-done.11.refs_1_ = bf16[384,512]{1,0:T(8,128)(2,1)S(1)} collective-permute-done((bf16[384,512]{1,0:T(8,128)(2,1)S(1)}, bf16[384,512]{1,0:T(8,128)(2,1)S(1)}, u32[]{:S(2)}, u32[]{:S(2)}) %collective-permute-start.11) | collective-permute-done | bytes 393248 | tf_op jit(solution)/shard_map/ppermute | solution.py:235
  107.8 1.5 %collective-permute-start.27 = (bf16[64,768]{1,0:T(8,128)(2,1)S(1)}, bf16[64,768]{1,0:T(8,128)(2,1)S(1)}, u32[]{:S(2)}, u32[]{:S(2)}) collective-permute-start(bf16[64,768]{1,0:T(8,128)(2,1)S(1)} %sum_w.1.refs_0_), channel_id=1, source_target_pairs={{0,24},{4,28},{8,16},{12,20},{16,8},{20,12},{24,0},{28,4},{1,25},{... | collective-permute-start | bytes 294920 | tf_op jit(solution)/shard_map/ppermute | solution.py:232
  109.3 11.6 %collective-permute-done.12.refs_2_ = bf16[384,512]{1,0:T(8,128)(2,1)S(1)} collective-permute-done((bf16[384,512]{1,0:T(8,128)(2,1)S(1)}, bf16[384,512]{1,0:T(8,128)(2,1)S(1)}, u32[]{:S(2)}, u32[]{:S(2)}) %collective-permute-start.12) | collective-permute-done | bytes 393248 | tf_op jit(solution)/shard_map/ppermute | solution.py:235
  122.0 7.0 %collective-permute-done.13.refs_3_ = bf16[384,512]{1,0:T(8,128)(2,1)S(1)} collective-permute-done((bf16[384,512]{1,0:T(8,128)(2,1)S(1)}, bf16[384,512]{1,0:T(8,128)(2,1)S(1)}, u32[]{:S(2)}, u32[]{:S(2)}) %collective-permute-start.13) | collective-permute-done | bytes 393248 | tf_op jit(solution)/shard_map/ppermute | solution.py:235
  129.0 3.5 %inputs.1 = bf16[4,128,768]{2,1,0:T(8,128)(2,1)} custom-call(s32[3]{0:T(128)S(1)} %pad_add_fusion.place, bf16[384,512]{1,0:T(8,128)(2,1)S(1)} %get-tuple-element.42.refs_0_, bf16[384,512]{1,0:T(8,128)(2,1)S(1)} %collective-permute-done.11.refs_1_, bf16[384,512]{1,0:T(8,128)(2,1)S(1)} %collective-permute-done.12.refs_2_, ...), custom_call_target="tpu_custom_call" | custom-call | tf_op jit(solution)/shard_map/inputs/pallas_call | solution.py:34
  132.5 2.0 %unpack.1 = (f32[768,128]{1,0:T(8,128)}, f32[768,128]{1,0:T(8,128)}, f32[768,128]{1,0:T(8,128)}, f32[128,768]{1,0:T(8,128)}) custom-call(s32[3]{0:T(128)S(1)} %pad_add_fusion.place, bf16[64,768]{1,0:T(8,128)(2,1)S(1)} %sum_w.1.refs_0_, bf16[64,768]{1,0:T(8,128)(2,1)S(1)} %collective-permute-done.25.refs_1_, ...), custom_call_target="tpu_custom_call" | custom-call | tf_op jit(solution)/shard_map/unpack/pallas_call | solution.py:34
  (77 shorter events, 15.9 us)
Async XLA Ops:
  14.0 2.7 %collective-permute-start = (bf16[4,128,1024]{2,1,0:T(8,128)(2,1)S(1)}, bf16[4,128,1024]{2,1,0:T(8,128)(2,1)S(1)}, u32[]{:S(2)}, u32[]{:S(2)}) collective-permute-start(bf16[4,128,1024]{2,1,0:T(8,128)(2,1)S(1)} %get-tuple-element.33), channel_id=1, source_target_pairs={{0,4},{4,0},{8,12},{12,8},{16,20},{20,16},{24,28},{28,24},{1,5},{5... | collective-permute-start | bytes 3145736 | tf_op jit(solution)/shard_map/ppermute | solution.py:229
  17.5 9.2 %collective-permute-start.1 = (bf16[128,1024]{1,0:T(8,128)(2,1)S(1)}, bf16[128,1024]{1,0:T(8,128)(2,1)S(1)}, u32[]{:S(2)}, u32[]{:S(2)}) collective-permute-start(bf16[128,1024]{1,0:T(8,128)(2,1)S(1)} %get-tuple-element.35), channel_id=1, source_target_pairs={{0,8},{4,12},{8,0},{12,4},{16,24},{20,28},{24,16},{28,20},{1,9},{5... | collective-permute-start | bytes 786440 | tf_op jit(solution)/shard_map/ppermute | solution.py:232
  19.0 13.7 %collective-permute-start.2 = (bf16[128,1024]{1,0:T(8,128)(2,1)S(1)}, bf16[128,1024]{1,0:T(8,128)(2,1)S(1)}, u32[]{:S(2)}, u32[]{:S(2)}) collective-permute-start(bf16[128,1024]{1,0:T(8,128)(2,1)S(1)} %get-tuple-element.36), channel_id=1, source_target_pairs={{0,16},{4,20},{8,24},{12,28},{16,0},{20,4},{24,8},{28,12},{1,17},{... | collective-permute-start | bytes 786440 | tf_op jit(solution)/shard_map/ppermute | solution.py:232
  20.6 12.2 %collective-permute-start.3 = (bf16[128,1024]{1,0:T(8,128)(2,1)S(1)}, bf16[128,1024]{1,0:T(8,128)(2,1)S(1)}, u32[]{:S(2)}, u32[]{:S(2)}) collective-permute-start(bf16[128,1024]{1,0:T(8,128)(2,1)S(1)} %get-tuple-element.37), channel_id=1, source_target_pairs={{0,24},{4,28},{8,16},{12,20},{16,8},{20,12},{24,0},{28,4},{1,25},{... | collective-permute-start | bytes 786440 | tf_op jit(solution)/shard_map/ppermute | solution.py:232
  33.5 10.4 %collective-permute-start.6 = (bf16[128,1024]{1,0:T(8,128)(2,1)S(1)}, bf16[128,1024]{1,0:T(8,128)(2,1)}, u32[]{:S(2)}, u32[]{:S(2)}) collective-permute-start(bf16[128,1024]{1,0:T(8,128)(2,1)S(1)} %score.1.refs_0_), channel_id=1, source_target_pairs={{0,24},{4,28},{8,16},{12,20},{16,8},{20,12},{24,0},{28,4},{1,25},{... | collective-permute-start | bytes 786440 | tf_op jit(solution)/shard_map/ppermute | solution.py:232
  35.1 12.4 %collective-permute-start.4 = (bf16[128,1024]{1,0:T(8,128)(2,1)S(1)}, bf16[128,1024]{1,0:T(8,128)(2,1)}, u32[]{:S(2)}, u32[]{:S(2)}) collective-permute-start(bf16[128,1024]{1,0:T(8,128)(2,1)S(1)} %score.1.refs_0_), channel_id=1, source_target_pairs={{0,8},{4,12},{8,0},{12,4},{16,24},{20,28},{24,16},{28,20},{1,9},{5... | collective-permute-start | bytes 786440 | tf_op jit(solution)/shard_map/ppermute | solution.py:232
  36.6 10.9 %collective-permute-start.5 = (bf16[128,1024]{1,0:T(8,128)(2,1)S(1)}, bf16[128,1024]{1,0:T(8,128)(2,1)}, u32[]{:S(2)}, u32[]{:S(2)}) collective-permute-start(bf16[128,1024]{1,0:T(8,128)(2,1)S(1)} %score.1.refs_0_), channel_id=1, source_target_pairs={{0,16},{4,20},{8,24},{12,28},{16,0},{20,4},{24,8},{28,12},{1,17},{... | collective-permute-start | bytes 786440 | tf_op jit(solution)/shard_map/ppermute | solution.py:232
  37.1 12.6 %collective-permute-start.7 = (bf16[128,1024]{1,0:T(8,128)(2,1)S(1)}, bf16[128,1024]{1,0:T(8,128)(2,1)}, u32[]{:S(2)}, u32[]{:S(2)}) collective-permute-start(bf16[128,1024]{1,0:T(8,128)(2,1)S(1)} %score.1.refs_0_), channel_id=1, source_target_pairs={{0,4},{4,0},{8,12},{12,8},{16,20},{20,16},{24,28},{28,24},{1,5},{5... | collective-permute-start | bytes 786440 | tf_op jit(solution)/shard_map/ppermute | solution.py:229
  43.9 5.8 %collective-permute-start.10 = (bf16[128,1024]{1,0:T(8,128)(2,1)}, bf16[128,1024]{1,0:T(8,128)(2,1)}, u32[]{:S(2)}, u32[]{:S(2)}) collective-permute-start(bf16[128,1024]{1,0:T(8,128)(2,1)} %collective-permute-done.6.refs_3_), channel_id=1, source_target_pairs={{0,4},{4,0},{8,12},{12,8},{16,20},{20,16},{24,28},{28,24},{1,5},{5... | collective-permute-start | bytes 786440 | tf_op jit(solution)/shard_map/ppermute | solution.py:229
  47.5 2.1 %collective-permute-start.8 = (bf16[128,1024]{1,0:T(8,128)(2,1)}, bf16[128,1024]{1,0:T(8,128)(2,1)}, u32[]{:S(2)}, u32[]{:S(2)}) collective-permute-start(bf16[128,1024]{1,0:T(8,128)(2,1)} %collective-permute-done.4.refs_1_), channel_id=1, source_target_pairs={{0,4},{4,0},{8,12},{12,8},{16,20},{20,16},{24,28},{28,24},{1,5},{5... | collective-permute-start | bytes 786440 | tf_op jit(solution)/shard_map/ppermute | solution.py:229
  47.6 2.2 %collective-permute-start.9 = (bf16[128,1024]{1,0:T(8,128)(2,1)}, bf16[128,1024]{1,0:T(8,128)(2,1)}, u32[]{:S(2)}, u32[]{:S(2)}) collective-permute-start(bf16[128,1024]{1,0:T(8,128)(2,1)} %collective-permute-done.5.refs_2_), channel_id=1, source_target_pairs={{0,4},{4,0},{8,12},{12,8},{16,20},{20,16},{24,28},{28,24},{1,5},{5... | collective-permute-start | bytes 786440 | tf_op jit(solution)/shard_map/ppermute | solution.py:229
  49.1 16.0 %collective-permute-start.14 = (bf16[384,384]{1,0:T(8,128)(2,1)S(1)}, bf16[384,384]{1,0:T(8,128)(2,1)S(1)}, u32[]{:S(2)}, u32[]{:S(2)}) collective-permute-start(bf16[384,384]{1,0:T(8,128)(2,1)S(1)} %constant_dynamic-slice_fusion.refs_4_), channel_id=1, source_target_pairs={{0,1},{1,0},{2,3},{3,2},{4,5},{5,4},{6,7},{7,6},{8,9},{9,8},{10,11... | collective-permute-start | bytes 884744 | tf_op jit(solution)/shard_map/ppermute | solution.py:235
  62.0 3.6 %collective-permute-start.21 = (bf16[4,64,768]{2,1,0:T(8,128)(2,1)S(1)}, bf16[4,64,768]{2,1,0:T(8,128)(2,1)S(1)}, u32[]{:S(2)}, u32[]{:S(2)}) collective-permute-start(bf16[4,64,768]{2,1,0:T(8,128)(2,1)S(1)} %get-tuple-element.50), channel_id=1, source_target_pairs={{0,4},{4,0},{8,12},{12,8},{16,20},{20,16},{24,28},{28,24},{1,5},{5... | collective-permute-start | bytes 1179656 | tf_op jit(solution)/shard_map/ppermute | solution.py:229
  62.3 22.6 %collective-permute-start.15 = (bf16[384,384]{1,0:T(8,128)(2,1)S(1)}, bf16[384,384]{1,0:T(8,128)(2,1)S(1)}, u32[]{:S(2)}, u32[]{:S(2)}) collective-permute-start(bf16[384,384]{1,0:T(8,128)(2,1)S(1)} %constant_dynamic-slice_fusion.refs_4_), channel_id=1, source_target_pairs={{0,2},{1,3},{2,0},{3,1},{4,6},{5,7},{6,4},{7,5},{8,10},{9,11},{10,... | collective-permute-start | bytes 884744 | tf_op jit(solution)/shard_map/ppermute | solution.py:235
  64.9 26.5 %collective-permute-start.16 = (bf16[384,384]{1,0:T(8,128)(2,1)S(1)}, bf16[384,384]{1,0:T(8,128)(2,1)S(1)}, u32[]{:S(2)}, u32[]{:S(2)}) collective-permute-start(bf16[384,384]{1,0:T(8,128)(2,1)S(1)} %constant_dynamic-slice_fusion.refs_4_), channel_id=1, source_target_pairs={{0,3},{1,2},{2,1},{3,0},{4,7},{5,6},{6,5},{7,4},{8,11},{9,10},{10,... | collective-permute-start | bytes 884744 | tf_op jit(solution)/shard_map/ppermute | solution.py:235
  65.1 26.3 %collective-permute-start.17 = (bf16[384,384]{1,0:T(8,128)(2,1)S(1)}, bf16[384,384]{1,0:T(8,128)(2,1)S(1)}, u32[]{:S(2)}, u32[]{:S(2)}) collective-permute-start(bf16[384,384]{1,0:T(8,128)(2,1)S(1)} %constant_dynamic-slice_fusion.refs_4_), channel_id=1, source_target_pairs={{0,4},{4,0},{8,12},{12,8},{16,20},{20,16},{24,28},{28,24},{1,5},{5... | collective-permute-start | bytes 884744 | tf_op jit(solution)/shard_map/ppermute | solution.py:229
  65.1 29.4 %collective-permute-start.18 = (bf16[384,384]{1,0:T(8,128)(2,1)S(1)}, bf16[384,384]{1,0:T(8,128)(2,1)S(1)}, u32[]{:S(2)}, u32[]{:S(2)}) collective-permute-start(bf16[384,384]{1,0:T(8,128)(2,1)S(1)} %collective-permute-done.14.refs_5_), channel_id=1, source_target_pairs={{0,4},{4,0},{8,12},{12,8},{16,20},{20,16},{24,28},{28,24},{1,5},{5... | collective-permute-start | bytes 884744 | tf_op jit(solution)/shard_map/ppermute | solution.py:229
  66.3 29.8 %collective-permute-start.22 = (bf16[64,768]{1,0:T(8,128)(2,1)S(1)}, bf16[64,768]{1,0:T(8,128)(2,1)S(1)}, u32[]{:S(2)}, u32[]{:S(2)}) collective-permute-start(bf16[64,768]{1,0:T(8,128)(2,1)S(1)} %get-tuple-element.52), channel_id=1, source_target_pairs={{0,8},{4,12},{8,0},{12,4},{16,24},{20,28},{24,16},{28,20},{1,9},{5... | collective-permute-start | bytes 294920 | tf_op jit(solution)/shard_map/ppermute | solution.py:232
  84.9 11.1 %collective-permute-start.23 = (bf16[64,768]{1,0:T(8,128)(2,1)S(1)}, bf16[64,768]{1,0:T(8,128)(2,1)S(1)}, u32[]{:S(2)}, u32[]{:S(2)}) collective-permute-start(bf16[64,768]{1,0:T(8,128)(2,1)S(1)} %get-tuple-element.53), channel_id=1, source_target_pairs={{0,16},{4,20},{8,24},{12,28},{16,0},{20,4},{24,8},{28,12},{1,17},{... | collective-permute-start | bytes 294920 | tf_op jit(solution)/shard_map/ppermute | solution.py:232
  91.4 16.4 %collective-permute-start.11 = (bf16[384,512]{1,0:T(8,128)(2,1)S(1)}, bf16[384,512]{1,0:T(8,128)(2,1)S(1)}, u32[]{:S(2)}, u32[]{:S(2)}) collective-permute-start(bf16[384,512]{1,0:T(8,128)(2,1)S(1)} %get-tuple-element.43), channel_id=1, source_target_pairs={{0,1},{1,0},{2,3},{3,2},{4,5},{5,4},{6,7},{7,6},{8,9},{9,8},{10,11... | collective-permute-start | bytes 1179656 | tf_op jit(solution)/shard_map/ppermute | solution.py:235
  91.4 29.6 %collective-permute-start.12 = (bf16[384,512]{1,0:T(8,128)(2,1)S(1)}, bf16[384,512]{1,0:T(8,128)(2,1)S(1)}, u32[]{:S(2)}, u32[]{:S(2)}) collective-permute-start(bf16[384,512]{1,0:T(8,128)(2,1)S(1)} %get-tuple-element.44), channel_id=1, source_target_pairs={{0,2},{1,3},{2,0},{3,1},{4,6},{5,7},{6,4},{7,5},{8,10},{9,11},{10,... | collective-permute-start | bytes 1179656 | tf_op jit(solution)/shard_map/ppermute | solution.py:235
  94.5 5.5 %collective-permute-start.24 = (bf16[64,768]{1,0:T(8,128)(2,1)S(1)}, bf16[64,768]{1,0:T(8,128)(2,1)S(1)}, u32[]{:S(2)}, u32[]{:S(2)}) collective-permute-start(bf16[64,768]{1,0:T(8,128)(2,1)S(1)} %get-tuple-element.54), channel_id=1, source_target_pairs={{0,24},{4,28},{8,16},{12,20},{16,8},{20,12},{24,0},{28,4},{1,25},{... | collective-permute-start | bytes 294920 | tf_op jit(solution)/shard_map/ppermute | solution.py:232
  96.0 5.0 %collective-permute-start.19 = (bf16[384,384]{1,0:T(8,128)(2,1)S(1)}, bf16[384,384]{1,0:T(8,128)(2,1)S(1)}, u32[]{:S(2)}, u32[]{:S(2)}) collective-permute-start(bf16[384,384]{1,0:T(8,128)(2,1)S(1)} %collective-permute-done.15.refs_6_), channel_id=1, source_target_pairs={{0,4},{4,0},{8,12},{12,8},{16,20},{20,16},{24,28},{28,24},{1,5},{5... | collective-permute-start | bytes 884744 | tf_op jit(solution)/shard_map/ppermute | solution.py:229
  96.1 6.0 %collective-permute-start.20 = (bf16[384,384]{1,0:T(8,128)(2,1)S(1)}, bf16[384,384]{1,0:T(8,128)(2,1)S(1)}, u32[]{:S(2)}, u32[]{:S(2)}) collective-permute-start(bf16[384,384]{1,0:T(8,128)(2,1)S(1)} %collective-permute-done.16.refs_7_), channel_id=1, source_target_pairs={{0,4},{4,0},{8,12},{12,8},{16,20},{20,16},{24,28},{28,24},{1,5},{5... | collective-permute-start | bytes 884744 | tf_op jit(solution)/shard_map/ppermute | solution.py:229
  100.1 28.9 %collective-permute-start.13 = (bf16[384,512]{1,0:T(8,128)(2,1)S(1)}, bf16[384,512]{1,0:T(8,128)(2,1)S(1)}, u32[]{:S(2)}, u32[]{:S(2)}) collective-permute-start(bf16[384,512]{1,0:T(8,128)(2,1)S(1)} %get-tuple-element.45), channel_id=1, source_target_pairs={{0,3},{1,2},{2,1},{3,0},{4,7},{5,6},{6,5},{7,4},{8,11},{9,10},{10,... | collective-permute-start | bytes 1179656 | tf_op jit(solution)/shard_map/ppermute | solution.py:235
  101.0 20.0 %collective-permute-start.25 = (bf16[64,768]{1,0:T(8,128)(2,1)S(1)}, bf16[64,768]{1,0:T(8,128)(2,1)S(1)}, u32[]{:S(2)}, u32[]{:S(2)}) collective-permute-start(bf16[64,768]{1,0:T(8,128)(2,1)S(1)} %sum_w.1.refs_0_), channel_id=1, source_target_pairs={{0,8},{4,12},{8,0},{12,4},{16,24},{20,28},{24,16},{28,20},{1,9},{5... | collective-permute-start | bytes 294920 | tf_op jit(solution)/shard_map/ppermute | solution.py:232
  102.1 19.4 %collective-permute-start.26 = (bf16[64,768]{1,0:T(8,128)(2,1)S(1)}, bf16[64,768]{1,0:T(8,128)(2,1)S(1)}, u32[]{:S(2)}, u32[]{:S(2)}) collective-permute-start(bf16[64,768]{1,0:T(8,128)(2,1)S(1)} %sum_w.1.refs_0_), channel_id=1, source_target_pairs={{0,16},{4,20},{8,24},{12,28},{16,0},{20,4},{24,8},{28,12},{1,17},{... | collective-permute-start | bytes 294920 | tf_op jit(solution)/shard_map/ppermute | solution.py:232
  107.8 13.7 %collective-permute-start.27 = (bf16[64,768]{1,0:T(8,128)(2,1)S(1)}, bf16[64,768]{1,0:T(8,128)(2,1)S(1)}, u32[]{:S(2)}, u32[]{:S(2)}) collective-permute-start(bf16[64,768]{1,0:T(8,128)(2,1)S(1)} %sum_w.1.refs_0_), channel_id=1, source_target_pairs={{0,24},{4,28},{8,16},{12,20},{16,8},{20,12},{24,0},{28,4},{1,25},{... | collective-permute-start | bytes 294920 | tf_op jit(solution)/shard_map/ppermute | solution.py:232
  121.0 11.6 %collective-permute-start.28 = (bf16[64,768]{1,0:T(8,128)(2,1)S(1)}, bf16[64,768]{1,0:T(8,128)(2,1)S(1)}, u32[]{:S(2)}, u32[]{:S(2)}) collective-permute-start(bf16[64,768]{1,0:T(8,128)(2,1)S(1)} %sum_w.1.refs_0_), channel_id=1, source_target_pairs={{0,4},{4,0},{8,12},{12,8},{16,20},{20,16},{24,28},{28,24},{1,5},{5... | collective-permute-start | bytes 294920 | tf_op jit(solution)/shard_map/ppermute | solution.py:229
  121.0 11.6 %collective-permute-start.29 = (bf16[64,768]{1,0:T(8,128)(2,1)S(1)}, bf16[64,768]{1,0:T(8,128)(2,1)S(1)}, u32[]{:S(2)}, u32[]{:S(2)}) collective-permute-start(bf16[64,768]{1,0:T(8,128)(2,1)S(1)} %collective-permute-done.25.refs_1_), channel_id=1, source_target_pairs={{0,4},{4,0},{8,12},{12,8},{16,20},{20,16},{24,28},{28,24},{1,5},{5... | collective-permute-start | bytes 294920 | tf_op jit(solution)/shard_map/ppermute | solution.py:229
  121.5 11.0 %collective-permute-start.30 = (bf16[64,768]{1,0:T(8,128)(2,1)S(1)}, bf16[64,768]{1,0:T(8,128)(2,1)S(1)}, u32[]{:S(2)}, u32[]{:S(2)}) collective-permute-start(bf16[64,768]{1,0:T(8,128)(2,1)S(1)} %collective-permute-done.26.refs_2_), channel_id=1, source_target_pairs={{0,4},{4,0},{8,12},{12,8},{16,20},{20,16},{24,28},{28,24},{1,5},{5... | collective-permute-start | bytes 294920 | tf_op jit(solution)/shard_map/ppermute | solution.py:229
  121.6 11.0 %collective-permute-start.31 = (bf16[64,768]{1,0:T(8,128)(2,1)S(1)}, bf16[64,768]{1,0:T(8,128)(2,1)S(1)}, u32[]{:S(2)}, u32[]{:S(2)}) collective-permute-start(bf16[64,768]{1,0:T(8,128)(2,1)S(1)} %collective-permute-done.27.refs_3_), channel_id=1, source_target_pairs={{0,4},{4,0},{8,12},{12,8},{16,20},{20,16},{24,28},{28,24},{1,5},{5... | collective-permute-start | bytes 294920 | tf_op jit(solution)/shard_map/ppermute | solution.py:229
  (17 other events, 221.2 us)

commit v2 on v0

v2 whole, which is shorter than its diff:
```python
import math
from functools import partial

import jax
import jax.numpy as jnp
from jax import lax
from jax.experimental import pallas as pl
from jax.experimental.pallas import tpu as pltpu
from jax.sharding import PartitionSpec as P

HEAD_DIM = 64
F32 = jnp.float32
BF16 = jnp.bfloat16
VMEM_BYTES = 16 * 1024 * 1024
SHARERS = 4


def dot_nn(left, right):
    return lax.dot_general(left, right, (((1,), (0,)), ((), ())), preferred_element_type=F32)


def dot_nt(left, right):
    return lax.dot_general(left, right, (((1,), (1,)), ((), ())), preferred_element_type=F32)


def vmem_spec():
    return pl.BlockSpec(memory_space=pltpu.VMEM)


def smem_spec():
    return pl.BlockSpec(memory_space=pltpu.SMEM)


def hbm_spec():
    return pl.BlockSpec(memory_space=pltpu.HBM)


def any_spec():
    return pl.BlockSpec(memory_space=pl.ANY)


def call(kernel, outs, ins, hbm=0, held=(), out_specs=None, scratch=(), flops=0, moved=0, name=None):
    count = len(ins)

    def run(*refs):
        kernel(*refs[:count], *refs[count + len(held) :])

    place, far, near = ins[0], ins[1 : 1 + hbm], ins[1 + hbm :]
    return pl.pallas_call(
        run,
        out_shape=outs,
        in_specs=[smem_spec()]
        + [hbm_spec()] * len(far)
        + [vmem_spec()] * len(near)
        + [any_spec()] * len(held),
        out_specs=out_specs or jax.tree.map(lambda _: vmem_spec(), outs),
        scratch_shapes=list(scratch),
        compiler_params=pltpu.CompilerParams(vmem_limit_bytes=VMEM_BYTES),
        cost_estimate=pl.CostEstimate(flops=flops, bytes_accessed=moved, transcendentals=0),
        name=name,
    )(place, *[far_array(x) for x in far], *near, *held)


def far_array(x):
    return pltpu.with_memory_space_constraint(x, pltpu.HBM)


def fetch(pairs, sems):
    copies = [pltpu.make_async_copy(src, dst, sems.at[i]) for i, (src, dst) in enumerate(pairs)]
    for copy in copies:
        copy.start()
    return copies


def deal(chip, core, shard, keep, give, value, first=0):
    slot = jnp.bitwise_xor(chip, shard // 2)

    cols = pl.ds(first, value.shape[1])

    @pl.when(core == shard % 2)
    def _():
        keep[slot, :, cols] = value

    @pl.when(core != shard % 2)
    def _():
        give[slot, :, cols] = value


def scores(chip, core, left, right, turned, keep, give, first):
    heads, _, cols = left.shape
    piece_rows = keep.shape[1]
    for h in range(heads):
        turned[...] = left[h].T
        total = dot_nn(turned[...], right[h]).astype(BF16)
        for i in range(0, cols, piece_rows):
            deal(chip, core, (h * cols + i) // piece_rows, keep, give, total[i : i + piece_rows], first)


def front_kernel(
    place, x, og, wq, wk, wv, wo, qt, kt, vt, gt, keep, give, slab,
    rows_x, rows_og, three_w, held_wo, both, turned, sems,
):
    rows = x.shape[0]
    width = wq.shape[1]
    loads = [pltpu.make_async_copy(w, three_w.at[t], sems.at[2, t]) for t, w in enumerate((wq, wk, wv))]
    loads.append(pltpu.make_async_copy(wo, held_wo, sems.at[2, 3]))
    in_x = [pltpu.make_async_copy(x.at[r], rows_x.at[r], sems.at[0, r]) for r in range(rows)]
    in_og = [pltpu.make_async_copy(og.at[r], rows_og.at[r], sems.at[1, r]) for r in range(rows)]
    for copy in loads + in_x + in_og:
        copy.start()
    for copy in loads:
        copy.wait()
    depth = slab.shape[0]
    at = pl.ds(pl.multiple_of(place[3] * depth, depth), depth)
    for t in range(3):
        both[t * width : (t + 1) * width, :] = three_w[t].T
        slab[:, t * width : (t + 1) * width] = three_w[t, at, :]
    for r in range(rows):
        in_x[r].wait()
        three = dot_nt(both[...], rows_x[r]).astype(BF16)
        at = slice(r * HEAD_DIM, (r + 1) * HEAD_DIM)
        for t, out in enumerate((qt, kt, vt)):
            for h in range(width // HEAD_DIM):
                first = t * width + h * HEAD_DIM
                out[h, at, :] = three[first : first + HEAD_DIM]
    scores(place[0], place[1], qt, kt, turned, keep, give, 0)
    for r in range(rows):
        in_og[r].wait()
        grad = dot_nt(held_wo[...], rows_og[r]).astype(BF16)
        at = slice(r * HEAD_DIM, (r + 1) * HEAD_DIM)
        for h in range(width // HEAD_DIM):
            gt[h, at, :] = grad[h * HEAD_DIM : (h + 1) * HEAD_DIM]
    scores(place[0], place[1], gt, vt, turned, keep, give, kt.shape[2])


def pair_kernel(place, keep, got, *outs):
    for k in range(keep.shape[0]):
        outs[k][...] = (keep[k].astype(F32) + got[k].astype(F32)).astype(outs[k].dtype)


def pair_pass_kernel(place, keep, got, slab, *outs):
    pair_kernel(place, keep, got, *outs[:-1])
    outs[-1][...] = slab[...]


def added(parts, cols=slice(None)):
    total = parts[0][:, cols].astype(F32)
    for part in parts[1:]:
        total = total + part[:, cols].astype(F32)
    return total


def score_kernel(logit_scale, place, *refs):
    *parts, out = refs
    cols = out.shape[1] // 2
    exponent = jnp.exp(added(parts, slice(0, cols)) * logit_scale)
    probs = exponent / jnp.sum(exponent, axis=1, keepdims=True)
    out[:, 0:cols] = probs.astype(BF16)
    grad = added(parts, slice(cols, None))
    inner = jnp.sum(probs * grad, axis=1, keepdims=True)
    out[:, cols:] = (logit_scale * probs * (grad - inner)).astype(BF16)


def assemble(place, mine, other, full):
    piece_rows = mine[0].shape[0]
    for k in range(len(mine)):
        base = 2 * jnp.bitwise_xor(place[0], k)
        for side, part in ((place[1], mine[k]), (1 - place[1], other[k])):
            at = pl.ds(pl.multiple_of((base + side) * piece_rows, piece_rows), piece_rows)
            full[at, :] = part[...].astype(full.dtype)


def grads_kernel(pieces, zeds, place, *refs):
    mine, other = refs[0:pieces], refs[pieces : 2 * pieces]
    qt, kt, vt, gt = refs[2 * pieces : 2 * pieces + 4]
    slabs = refs[2 * pieces + 4 : 2 * pieces + 3 + zeds]
    send_far, four_far, packed, full, send, four, sems = refs[2 * pieces + 3 + zeds :]
    heads, _, cols = qt.shape
    rows, stacked, _ = four.shape
    width = stacked // 4
    block = cols // zeds
    assemble(place, mine, other, full)
    for h in range(heads):
        span = slice(h * cols, (h + 1) * cols)
        values = (
            dot_nt(kt[h], full[span, cols:]),
            dot_nn(qt[h], full[span, cols:]),
            dot_nn(gt[h], full[span, 0:cols]),
            dot_nt(vt[h], full[span, 0:cols]),
        )
        for t, value in enumerate(values):
            value = value.astype(BF16)
            at = slice(t * width + h * HEAD_DIM, t * width + (h + 1) * HEAD_DIM)
            for r in range(rows):
                four[r, at, :] = value[r * HEAD_DIM : (r + 1) * HEAD_DIM]
    copies = []
    for z in range(zeds):
        for r in range(rows):
            part = four[r, 0 : 3 * width, z * block : (z + 1) * block]
            send[z, :, r * block : (r + 1) * block] = part
        copies += fetch([(send.at[z], send_far.at[z])], sems.at[pl.ds(z, 1)])
    copies += fetch([(four, four_far)], sems.at[pl.ds(zeds, 1)])
    for k, slab in enumerate(slabs):
        packed[k] = slab[...]
    for copy in copies:
        copy.wait()


def weights_kernel(place, x_far, og_far, four_far, keep, give, x, og, four, total, sems):
    rows, stacked, _ = four.shape
    three = 3 * stacked // 4
    piece_rows = keep.shape[1]
    copies = [
        fetch([(four_far.at[r], four.at[r]), (x_far.at[r], x.at[r]), (og_far.at[r], og.at[r])], sems.at[r])
        for r in range(rows)
    ]
    for r in range(rows):
        for copy in copies[r]:
            copy.wait()
        upper = dot_nn(four[r, 0:three, :], x[r])
        lower = dot_nn(four[r, three:, :], og[r])
        if r == 0:
            total[0:three, :] = upper
            total[three:, :] = lower
        else:
            total[0:three, :] += upper
            total[three:, :] += lower
    for i in range(0, stacked, piece_rows):
        value = total[i : i + piece_rows, :].astype(BF16)
        deal(place[0], place[1], i // piece_rows, keep, give, value)


def sum_kernel(scale, place, *refs):
    *parts, out = refs
    out[...] = (added(parts) * scale).astype(out.dtype)


def unpack_kernel(pieces, place, *refs):
    mine, other = refs[0:pieces], refs[pieces : 2 * pieces]
    outs, full = refs[2 * pieces : -1], refs[-1]
    assemble(place, mine, other, full)
    width = full.shape[0] // len(outs)
    for t, out in enumerate(outs[:-1]):
        out[...] = full[t * width : (t + 1) * width, :].T
    outs[-1][...] = full[(len(outs) - 1) * width :, :]


def gather_weights_kernel(slabs, place, wq, wk, wv, *refs):
    mine, other, full = refs[0:slabs], refs[slabs : 2 * slabs], refs[-1]
    zeds, _, _ = full.shape
    width = wq.shape[1]
    depth = mine[0].shape[1]
    zed = place[2]
    for t, own in enumerate((wq, wk, wv)):
        full[zed, :, t * width : (t + 1) * width] = own[...]
    for k in range(slabs):
        base = 2 * jnp.bitwise_xor(place[3] // 2, k)
        for side, part in ((place[1], mine[k]), (1 - place[1], other[k])):
            at = pl.ds(pl.multiple_of((base + side) * depth, depth), depth)
            for z in range(1, zeds):
                full[jnp.bitwise_xor(zed, z), at, :] = part[z - 1]


def inputs_kernel(place, sent_far, full, out, sent, sems):
    rows, block, _ = out.shape
    zeds = sent.shape[0]
    copies = fetch([(sent_far.at[z], sent.at[z]) for z in range(zeds)], sems)
    copies[0].wait()
    value = dot_nt(sent[0].T, full[0])
    for z in range(1, zeds):
        copies[z].wait()
        value = value + dot_nt(sent[z].T, full[z])
    value = value.astype(BF16)
    for r in range(rows):
        out[r] = value[r * block : (r + 1) * block]


def body(inputs, out_grad, w_query, w_key, w_value, w_output):
    rows, cols, model = inputs.shape
    width = w_query.shape[1]
    heads = width // HEAD_DIM
    merged = rows * HEAD_DIM
    seqs, zeds = lax.axis_size("seq"), lax.axis_size("head")
    pieces = seqs // 2
    all_rows = rows * seqs
    logit_scale = 1.0 / (math.sqrt(HEAD_DIM) * math.sqrt(all_rows))
    inv_root = 1.0 / math.sqrt(all_rows * cols)
    shard = heads * cols // seqs
    wide = 4 * width // seqs
    block = cols // zeds
    sharers = min(seqs, SHARERS)
    depth = model // sharers
    me = lax.axis_index("seq")
    zed = lax.axis_index("head")
    place = jnp.stack([me // 2, me % 2, zed, me % sharers]).astype(jnp.int32)

    def swap(value):
        return lax.ppermute(value, "seq", [(i, i ^ 1) for i in range(seqs)])

    def across(value, k):
        return lax.ppermute(value, "seq", [(i, i ^ (2 * k)) for i in range(seqs)])

    def along(value, k):
        return lax.ppermute(value, "head", [(i, i ^ k) for i in range(zeds)])

    def shape(*dims, dtype=BF16):
        return jax.ShapeDtypeStruct(dims, dtype)

    def spread(paired):
        return [paired[0]] + [across(paired[k], k) for k in range(1, pieces)]

    def gathered(value, count):
        mine = [value] + [across(value, k) for k in range(1, count)]
        return mine, [swap(part) for part in mine]

    blocks = shape(heads, merged, cols)
    dealt = shape(pieces, shard, 2 * cols)
    rows_in = pltpu.VMEM((rows, cols, model), BF16)
    dot_flops = 2 * rows * cols * width * model
    score_flops = 2 * heads * cols * cols * merged

    qt, kt, vt, gt, keep, give, slab = call(
        front_kernel,
        (blocks,) * 4 + (dealt,) * 2 + (shape(depth, 3 * width),),
        (place, inputs, out_grad, w_query, w_key, w_value, w_output),
        hbm=6,
        scratch=[
            rows_in,
            rows_in,
            pltpu.VMEM((3, model, width), BF16),
            pltpu.VMEM((width, model), BF16),
            pltpu.VMEM((3 * width, model), BF16),
            pltpu.VMEM((cols, merged), BF16),
            pltpu.SemaphoreType.DMA((3, max(4, rows))),
        ],
        flops=4 * dot_flops + 2 * score_flops,
        name="front",
    )
    *paired, slab = call(
        pair_pass_kernel,
        [shape(shard, 2 * cols)] * pieces + [shape(*slab.shape)],
        (place, keep, swap(give), slab),
        name="pair_scores",
    )
    parts = spread(paired)
    slabs = [along(slab, k) for k in range(1, zeds)]
    scored = call(
        partial(score_kernel, logit_scale),
        shape(shard, 2 * cols),
        (place, *parts),
        held=slabs,
        name="score",
    )
    mine, other = gathered(scored, pieces)
    send, four, packed = call(
        partial(grads_kernel, pieces, zeds),
        (
            shape(zeds, 3 * width, rows * block),
            shape(rows, 4 * width, cols),
            shape(zeds - 1, depth, 3 * width),
        ),
        (place, *mine, *other, qt, kt, vt, gt, *slabs),
        out_specs=(hbm_spec(), hbm_spec(), vmem_spec()),
        scratch=[
            pltpu.VMEM((heads * cols, 2 * cols), BF16),
            pltpu.VMEM((zeds, 3 * width, rows * block), BF16),
            pltpu.VMEM((rows, 4 * width, cols), BF16),
            pltpu.SemaphoreType.DMA((zeds + 1,)),
        ],
        flops=4 * score_flops,
        name="grads",
    )
    sent = lax.all_to_all(send, "head", 0, 0, tiled=True)
    mine_w, other_w = gathered(packed, sharers // 2)

    keep, give = call(
        weights_kernel,
        [shape(pieces, wide, model)] * 2,
        (place, inputs, out_grad, four),
        hbm=3,
        scratch=[
            rows_in,
            rows_in,
            pltpu.VMEM((rows, 4 * width, cols), BF16),
            pltpu.VMEM((4 * width, model), F32),
            pltpu.SemaphoreType.DMA((rows, 3)),
        ],
        flops=4 * dot_flops,
        moved=inputs.size * 4,
        name="weights",
    )
    paired = call(
        pair_kernel, [shape(wide, model)] * pieces, (place, keep, swap(give)), name="pair_weights"
    )
    parts = spread(paired)
    full = call(
        partial(gather_weights_kernel, sharers // 2),
        shape(zeds, model, 3 * width),
        (place, w_query, w_key, w_value, *mine_w, *other_w),
        name="gather_weights",
    )
    total_w = call(
        partial(sum_kernel, inv_root),
        shape(wide, model),
        (place, *parts),
        held=(full,),
        name="sum_weights",
    )
    mine, other = gathered(total_w, pieces)
    grad_q, grad_k, grad_v, grad_o = call(
        partial(unpack_kernel, pieces),
        [shape(model, width, dtype=F32)] * 3 + [shape(width, model, dtype=F32)],
        (place, *mine, *other),
        scratch=[pltpu.VMEM((4 * width, model), F32)],
        name="unpack",
    )
    grad_inputs = call(
        inputs_kernel,
        shape(rows, block, model),
        (place, sent, full),
        hbm=1,
        scratch=[pltpu.VMEM((zeds, 3 * width, rows * block), BF16), pltpu.SemaphoreType.DMA((zeds,))],
        flops=3 * dot_flops,
        name="inputs",
    )
    return (grad_inputs, grad_q, grad_k, grad_v, grad_o)


def solution(mesh):
    return jax.shard_map(
        body,
        mesh=mesh,
        in_specs=(
            P("seq", None, None),
            P("seq", None, None),
            P(None, "head"),
            P(None, "head"),
            P(None, "head"),
            P("head", None),
        ),
        out_specs=(
            P("seq", "head", None),
            P(None, "head"),
            P(None, "head"),
            P(None, "head"),
            P("head", None),
        ),
        check_vma=False,
    )
```

time: 300 us -> 102 us (0.34)
  blocking collectives: 72.4 us -> 0 us
  local copies, waits for them, and re-layouts: 56.8 us -> 1.37 us
  matrix products: 51 us -> 0 us
  waiting for transfers between devices: 84.1 us -> 39.5 us
  Pallas kernels: 0 us -> 25.9 us
  starting transfers between devices: 13.9 us -> 33.8 us
  between operations: 14.2 us -> 0.95 us
  other arithmetic: 5.81 us -> 0.08 us
    psum x2 -> x0, waiting for transfers between devices: 84.1 us -> none  [the longest x1 84.1 us: body(): grad_probs = lax.psum(part_probs, 'seq')]
    all_gather x3 -> x0, blocking collectives: 72.4 us -> none  [the longest x1 26.9 us: body(): lax.all_gather(w_key, 'head', axis=1, tiled=True)]
    dot_general x17 -> x0, matrix products: 51 us -> none  [the longest x1 9.95 us: body(): jnp.einsum('hij,rihe->rjhe', grad_logits, query_four, preferred_element_t...]
    ppermute x0 -> x28, waiting for transfers between devices: none -> 34.5 us  [the longest x13 24.1 us: across(): return lax.ppermute(value, 'seq', [(i, i ^ 2 * k) for i in range(seqs)])]
    ppermute x0 -> x28, starting transfers between devices: none -> 29.5 us  [the longest x13 15.7 us: across(): return lax.ppermute(value, 'seq', [(i, i ^ 2 * k) for i in range(seqs)])]
    reshape x8 -> x0, local copies, waits for them, and re-layouts: 26.9 us -> none  [the longest x2 6.78 us: body(): query_four = query_proj.reshape(shape_heads)]
    pallas_call x0 -> x10, Pallas kernels: none -> 25.9 us  [call(): pl.pallas_call(run, out_shape=outs, in_specs=[smem_spec()] + [hbm_spec()]...]
    all_to_all x3 -> x1, starting transfers between devices: 13.8 us -> 4.34 us  [body(): sent = lax.all_to_all(send, 'head', 0, 0, tiled=True)]
  transfers between devices with their start and end apart: 5 -> 29, of which waited for: 1 -> 18; matrix products, arithmetic and copies ran while one was open for 14% -> 0% of each run, Pallas kernels for 0% -> 9%
where the time goes in v2:
time: 102 us
  waiting for transfers between devices  39.5 us (39%)
  starting transfers between devices  33.8 us (33%)
  Pallas kernels  25.9 us (25%)
  local copies, waits for them, and re-layouts  1.37 us (1%)
    pallas_call x10, Pallas kernels, call(): pl.pallas_call(run, out_shape=outs, in_specs=[smem_spec()] + [hbm_spec()]...  25.9 us
    ppermute x13, waiting for transfers between devices, across(): return lax.ppermute(value, 'seq', [(i, i ^ 2 * k) for i in range(seqs)])  24.1 us
    ppermute x13, starting transfers between devices, across(): return lax.ppermute(value, 'seq', [(i, i ^ 2 * k) for i in range(seqs)])  15.7 us
    ppermute x3, starting transfers between devices, along(): return lax.ppermute(value, 'head', [(i, i ^ k) for i in range(zeds)])  11.8 us
    ppermute x3, waiting for transfers between devices, along(): return lax.ppermute(value, 'head', [(i, i ^ k) for i in range(zeds)])  5.69 us
    all_to_all x1, waiting for transfers between devices, body(): sent = lax.all_to_all(send, 'head', 0, 0, tiled=True)  5.01 us
    ppermute x12, waiting for transfers between devices, swap(): return lax.ppermute(value, 'seq', [(i, i ^ 1) for i in range(seqs)])  4.72 us
    all_to_all x1, starting transfers between devices, body(): sent = lax.all_to_all(send, 'head', 0, 0, tiled=True)  4.34 us
  transfers between devices with their start and end apart: 29, of which 18 were waited for; matrix products, arithmetic and copies ran while one was open for 0% of the time, Pallas kernels for 9%

profile of v2, /device:TPU:0, one launch (start us, length us, event | category | flops | bytes accessed | tf_op | source)
XLA Modules:
  0.0 101.7 jit_solution(3824150919622581063)
XLA Ops:
  0.7 7.2 %front.1 = (bf16[2,256,512]{2,1,0:T(8,128)(2,1)S(1)}, bf16[2,256,512]{2,1,0:T(8,128)(2,1)S(1)}, bf16[2,256,512]{2,1,0:T(8,128)(2,1)S(1)}, bf16[2,256,512]{2,1,0:...) custom-call(s32[4]{0:T(128)S(1)} %pad_add_fusion.refs_0_, ...), custom_call_target="tpu_custom_call" | custom-call | flops 2147483648 | tf_op jit(solution)/shard_map/front/pallas_call | solution.py:49
  8.4 2.3 %collective-permute-done.refs_2_ = bf16[4,128,1024]{2,1,0:T(8,128)(2,1)S(1)} collective-permute-done((bf16[4,128,1024]{2,1,0:T(8,128)(2,1)S(1)}, bf16[4,128,1024]{2,1,0:T(8,128)(2,1)S(1)}, u32[]{:S(2)}, u32[]{:S(2)}) %collective-permute-start) | collective-permute-done | bytes 1048608 | tf_op jit(solution)/shard_map/ppermute | solution.py:298
  10.7 0.8 pair_scores.1
  11.5 5.0 %collective-permute-start.6 = (bf16[192,384]{1,0:T(8,128)(2,1)S(1)}, bf16[192,384]{1,0:T(8,128)(2,1)S(1)}, u32[]{:S(2)}, u32[]{:S(2)}) collective-permute-start(bf16[192,384]{1,0:T(8,128)(2,1)S(1)} %get-tuple-element.37), channel_id=1, source_target_pairs={{0,3},{1,2},{2,1},{3,0},{4,7},{5,6},{6,5},{7,4},{8,11},{9,10},{10,... | collective-permute-start | bytes 442376 | tf_op jit(solution)/shard_map/ppermute | solution.py:304
  16.5 1.5 %collective-permute-start.1 = (bf16[128,1024]{1,0:T(8,128)(2,1)S(1)}, bf16[128,1024]{1,0:T(8,128)(2,1)S(1)}, u32[]{:S(2)}, u32[]{:S(2)}) collective-permute-start(bf16[128,1024]{1,0:T(8,128)(2,1)S(1)} %get-tuple-element.34), channel_id=1, source_target_pairs={{0,8},{4,12},{8,0},{12,4},{16,24},{20,28},{24,16},{28,20},{1,9},{5... | collective-permute-start | bytes 786440 | tf_op jit(solution)/shard_map/ppermute | solution.py:301
  18.0 1.5 %collective-permute-start.2 = (bf16[128,1024]{1,0:T(8,128)(2,1)S(1)}, bf16[128,1024]{1,0:T(8,128)(2,1)S(1)}, u32[]{:S(2)}, u32[]{:S(2)}) collective-permute-start(bf16[128,1024]{1,0:T(8,128)(2,1)S(1)} %get-tuple-element.35), channel_id=1, source_target_pairs={{0,16},{4,20},{8,24},{12,28},{16,0},{20,4},{24,8},{28,12},{1,17},{... | collective-permute-start | bytes 786440 | tf_op jit(solution)/shard_map/ppermute | solution.py:301
  20.8 6.7 %collective-permute-start.4 = (bf16[192,384]{1,0:T(8,128)(2,1)S(1)}, bf16[192,384]{1,0:T(8,128)(2,1)S(1)}, u32[]{:S(2)}, u32[]{:S(2)}) collective-permute-start(bf16[192,384]{1,0:T(8,128)(2,1)S(1)} %get-tuple-element.37), channel_id=1, source_target_pairs={{0,1},{1,0},{2,3},{3,2},{4,5},{5,4},{6,7},{7,6},{8,9},{9,8},{10,11... | collective-permute-start | bytes 442376 | tf_op jit(solution)/shard_map/ppermute | solution.py:304
  27.5 1.9 %collective-permute-done.5.refs_6_.refs_14_ = bf16[192,384]{1,0:T(8,128)(2,1)S(1)} collective-permute-done((bf16[192,384]{1,0:T(8,128)(2,1)S(1)}, bf16[192,384]{1,0:T(8,128)(2,1)S(1)}, u32[]{:S(2)}, u32[]{:S(2)}) %collective-permute-start.5) | collective-permute-done | bytes 147488 | tf_op jit(solution)/shard_map/ppermute | solution.py:304
  29.4 3.0 %collective-permute-done.4.refs_5_.refs_13_ = bf16[192,384]{1,0:T(8,128)(2,1)S(1)} collective-permute-done((bf16[192,384]{1,0:T(8,128)(2,1)S(1)}, bf16[192,384]{1,0:T(8,128)(2,1)S(1)}, u32[]{:S(2)}, u32[]{:S(2)}) %collective-permute-start.4) | collective-permute-done | bytes 147488 | tf_op jit(solution)/shard_map/ppermute | solution.py:304
  32.5 0.8 score.1.refs_1_
  33.3 2.5 %collective-permute-start.9 = (bf16[128,1024]{1,0:T(8,128)(2,1)S(1)}, bf16[128,1024]{1,0:T(8,128)(2,1)S(1)}, u32[]{:S(2)}, u32[]{:S(2)}) collective-permute-start(bf16[128,1024]{1,0:T(8,128)(2,1)S(1)} %score.1.refs_1_), channel_id=1, source_target_pairs={{0,24},{4,28},{8,16},{12,20},{16,8},{20,12},{24,0},{28,4},{1,25},{... | collective-permute-start | bytes 786440 | tf_op jit(solution)/shard_map/ppermute | solution.py:301
  36.8 6.6 %collective-permute-done.9.refs_4_ = bf16[128,1024]{1,0:T(8,128)(2,1)S(1)} collective-permute-done((bf16[128,1024]{1,0:T(8,128)(2,1)S(1)}, bf16[128,1024]{1,0:T(8,128)(2,1)S(1)}, u32[]{:S(2)}, u32[]{:S(2)}) %collective-permute-start.9) | collective-permute-done | bytes 262176 | tf_op jit(solution)/shard_map/ppermute | solution.py:301
  43.4 4.6 %collective-permute-done.8.refs_3_ = bf16[128,1024]{1,0:T(8,128)(2,1)S(1)} collective-permute-done((bf16[128,1024]{1,0:T(8,128)(2,1)S(1)}, bf16[128,1024]{1,0:T(8,128)(2,1)S(1)}, u32[]{:S(2)}, u32[]{:S(2)}) %collective-permute-start.8) | collective-permute-done | bytes 262176 | tf_op jit(solution)/shard_map/ppermute | solution.py:301
  48.6 1.0 collective-permute-done.12.refs_7_
  49.9 3.3 %grads.1 = (bf16[4,384,512]{2,1,0:T(8,128)(2,1)}, bf16[4,512,512]{2,1,0:T(8,128)(2,1)S(1)}, bf16[3,192,384]{2,1,0:T(8,128)(2,1)S(1)}) custom-call(s32[4]{0:T(128)S(1)} %pad_add_fusion.refs_0_, bf16[128,1024]{1,0:T(8,128)(2,1)S(1)} %score.1.refs_1_, bf16[128,1024]{1,0:T(8,128)(2,1)S(1)} %collective-permute-done.7.refs_2_, ...), custom_call_target="tpu_custom_call" | custom-call | flops 1073741824 | tf_op jit(solution)/shard_map/grads/pallas_call | solution.py:49
  53.3 1.4 %copy-done = bf16[4,512,512]{2,1,0:T(8,128)(2,1)} copy-done((bf16[4,512,512]{2,1,0:T(8,128)(2,1)}, bf16[4,512,512]{2,1,0:T(8,128)(2,1)S(1)}, u32[]{:S(2)}) %copy-start) | copy-done | bytes 2097176
  54.6 4.3 %all-to-all-start = ((bf16[4,384,512]{2,1,0:T(8,128)(2,1)}), bf16[4,384,512]{2,1,0:T(8,128)(2,1)}, u32[]{:S(2)}, u32[]{:S(2)}) async-start(bf16[4,384,512]{2,1,0:T(8,128)(2,1)} %get-tuple-element.42), calls=%async_computation | async-start | bytes 3145728 | tf_op jit(solution)/shard_map/all_to_all | solution.py:373
  59.0 1.5 %collective-permute-start.14 = (bf16[3,192,384]{2,1,0:T(8,128)(2,1)S(1)}, bf16[3,192,384]{2,1,0:T(8,128)(2,1)S(1)}, u32[]{:S(2)}, u32[]{:S(2)}) collective-permute-start(bf16[3,192,384]{2,1,0:T(8,128)(2,1)S(1)} %get-tuple-element.43.refs_4_), channel_id=1, source_target_pairs={{0,8},{4,12},{8,0},{12,4},{16,24},{20,28},{24,16},{28,20},{1,9},{5... | collective-permute-start | bytes 1327112 | tf_op jit(solution)/shard_map/ppermute | solution.py:301
  60.5 4.9 %weights.1 = (bf16[4,64,768]{2,1,0:T(8,128)(2,1)S(1)}, bf16[4,64,768]{2,1,0:T(8,128)(2,1)S(1)}) custom-call(s32[4]{0:T(128)S(1)} %pad_add_fusion.refs_0_, bf16[4,512,768]{2,1,0:T(8,128)(2,1)} %refs_1_.5, bf16[4,512,768]{2,1,0:T(8,128)(2,1)} %refs_2_.5, bf16[4,512,512]{2,1,0:T(8,128)(2,1)} %copy-done), custom_call_target="tpu_custom_call" | custom-call | flops 1610612736 | bytes 6291456 | tf_op jit(solution)/shard_map/weights/pallas_call | solution.py:49
  66.0 5.2 %collective-permute-done.14.refs_5_ = bf16[3,192,384]{2,1,0:T(8,128)(2,1)S(1)} collective-permute-done((bf16[3,192,384]{2,1,0:T(8,128)(2,1)S(1)}, bf16[3,192,384]{2,1,0:T(8,128)(2,1)S(1)}, u32[]{:S(2)}, u32[]{:S(2)}) %collective-permute-start.14) | collective-permute-done | bytes 442400 | tf_op jit(solution)/shard_map/ppermute | solution.py:301
  71.9 1.5 %collective-permute-start.18 = (bf16[64,768]{1,0:T(8,128)(2,1)S(1)}, bf16[64,768]{1,0:T(8,128)(2,1)S(1)}, u32[]{:S(2)}, u32[]{:S(2)}) collective-permute-start(bf16[64,768]{1,0:T(8,128)(2,1)S(1)} %get-tuple-element.48), channel_id=1, source_target_pairs={{0,8},{4,12},{8,0},{12,4},{16,24},{20,28},{24,16},{28,20},{1,9},{5... | collective-permute-start | bytes 294920 | tf_op jit(solution)/shard_map/ppermute | solution.py:301
  73.4 0.8 collective-permute-start.19
  74.3 1.2 %collective-permute-start.20 = (bf16[64,768]{1,0:T(8,128)(2,1)S(1)}, bf16[64,768]{1,0:T(8,128)(2,1)S(1)}, u32[]{:S(2)}, u32[]{:S(2)}) collective-permute-start(bf16[64,768]{1,0:T(8,128)(2,1)S(1)} %get-tuple-element.50), channel_id=1, source_target_pairs={{0,24},{4,28},{8,16},{12,20},{16,8},{20,12},{24,0},{28,4},{1,25},{... | collective-permute-start | bytes 294920 | tf_op jit(solution)/shard_map/ppermute | solution.py:301
  75.5 0.8 gather_weights.1.refs_2_.refs_5_
  76.3 0.9 collective-permute-done.18.refs_2_
  77.2 3.3 %collective-permute-done.19.refs_3_ = bf16[64,768]{1,0:T(8,128)(2,1)S(1)} collective-permute-done((bf16[64,768]{1,0:T(8,128)(2,1)S(1)}, bf16[64,768]{1,0:T(8,128)(2,1)S(1)}, u32[]{:S(2)}, u32[]{:S(2)}) %collective-permute-start.19) | collective-permute-done | bytes 98336 | tf_op jit(solution)/shard_map/ppermute | solution.py:301
  81.1 1.6 %collective-permute-start.23 = (bf16[64,768]{1,0:T(8,128)(2,1)S(1)}, bf16[64,768]{1,0:T(8,128)(2,1)S(1)}, u32[]{:S(2)}, u32[]{:S(2)}) collective-permute-start(bf16[64,768]{1,0:T(8,128)(2,1)S(1)} %sum_weights.1.refs_1_), channel_id=1, source_target_pairs={{0,24},{4,28},{8,16},{12,20},{16,8},{20,12},{24,0},{28,4},{1,25},{... | collective-permute-start | bytes 294920 | tf_op jit(solution)/shard_map/ppermute | solution.py:301
  83.2 1.5 %collective-permute-start.21 = (bf16[64,768]{1,0:T(8,128)(2,1)S(1)}, bf16[64,768]{1,0:T(8,128)(2,1)S(1)}, u32[]{:S(2)}, u32[]{:S(2)}) collective-permute-start(bf16[64,768]{1,0:T(8,128)(2,1)S(1)} %sum_weights.1.refs_1_), channel_id=1, source_target_pairs={{0,8},{4,12},{8,0},{12,4},{16,24},{20,28},{24,16},{28,20},{1,9},{5... | collective-permute-start | bytes 294920 | tf_op jit(solution)/shard_map/ppermute | solution.py:301
  84.6 3.2 %collective-permute-done.23.refs_4_ = bf16[64,768]{1,0:T(8,128)(2,1)S(1)} collective-permute-done((bf16[64,768]{1,0:T(8,128)(2,1)S(1)}, bf16[64,768]{1,0:T(8,128)(2,1)S(1)}, u32[]{:S(2)}, u32[]{:S(2)}) %collective-permute-start.23) | collective-permute-done | bytes 98336 | tf_op jit(solution)/shard_map/ppermute | solution.py:301
  89.6 2.0 %unpack.1 = (f32[768,128]{1,0:T(8,128)}, f32[768,128]{1,0:T(8,128)}, f32[768,128]{1,0:T(8,128)}, f32[128,768]{1,0:T(8,128)}) custom-call(s32[4]{0:T(128)S(1)} %pad_add_fusion.refs_0_, bf16[64,768]{1,0:T(8,128)(2,1)S(1)} %sum_weights.1.refs_1_, bf16[64,768]{1,0:T(8,128)(2,1)S(1)} %collective-permute-done.21.refs_2_, ...), custom_call_target="tpu_custom_call" | custom-call | tf_op jit(solution)/shard_map/unpack/pallas_call | solution.py:49
  91.6 5.0 %all-to-all-done.refs_1_ = bf16[4,384,512]{2,1,0:T(8,128)(2,1)} async-done(((bf16[4,384,512]{2,1,0:T(8,128)(2,1)}), bf16[4,384,512]{2,1,0:T(8,128)(2,1)}, u32[]{:S(2)}, u32[]{:S(2)}) %all-to-all-start) | async-done | bytes 1572896 | tf_op jit(solution)/shard_map/all_to_all | solution.py:373
  96.6 4.9 %inputs.1 = bf16[4,128,768]{2,1,0:T(8,128)(2,1)} custom-call(s32[4]{0:T(128)S(1)} %pad_add_fusion.refs_0_, bf16[4,384,512]{2,1,0:T(8,128)(2,1)} %all-to-all-done.refs_1_, bf16[4,768,384]{2,1,0:T(8,128)(2,1)S(1)} %gather_weights.1.refs_2_.refs_5_), custom_call_target="tpu_custom_call" | custom-call | flops 1207959552 | tf_op jit(solution)/shard_map/inputs/pallas_call | solution.py:49
  (45 shorter events, 8.0 us)
Async XLA Ops:
  7.9 2.8 %collective-permute-start = (bf16[4,128,1024]{2,1,0:T(8,128)(2,1)S(1)}, bf16[4,128,1024]{2,1,0:T(8,128)(2,1)S(1)}, u32[]{:S(2)}, u32[]{:S(2)}) collective-permute-start(bf16[4,128,1024]{2,1,0:T(8,128)(2,1)S(1)} %get-tuple-element.31), channel_id=1, source_target_pairs={{0,4},{4,0},{8,12},{12,8},{16,20},{20,16},{24,28},{28,24},{1,5},{5... | collective-permute-start | bytes 3145736 | tf_op jit(solution)/shard_map/ppermute | solution.py:298
  11.5 9.3 %collective-permute-start.6 = (bf16[192,384]{1,0:T(8,128)(2,1)S(1)}, bf16[192,384]{1,0:T(8,128)(2,1)S(1)}, u32[]{:S(2)}, u32[]{:S(2)}) collective-permute-start(bf16[192,384]{1,0:T(8,128)(2,1)S(1)} %get-tuple-element.37), channel_id=1, source_target_pairs={{0,3},{1,2},{2,1},{3,0},{4,7},{5,6},{6,5},{7,4},{8,11},{9,10},{10,... | collective-permute-start | bytes 442376 | tf_op jit(solution)/shard_map/ppermute | solution.py:304
  16.5 15.9 %collective-permute-start.1 = (bf16[128,1024]{1,0:T(8,128)(2,1)S(1)}, bf16[128,1024]{1,0:T(8,128)(2,1)S(1)}, u32[]{:S(2)}, u32[]{:S(2)}) collective-permute-start(bf16[128,1024]{1,0:T(8,128)(2,1)S(1)} %get-tuple-element.34), channel_id=1, source_target_pairs={{0,8},{4,12},{8,0},{12,4},{16,24},{20,28},{24,16},{28,20},{1,9},{5... | collective-permute-start | bytes 786440 | tf_op jit(solution)/shard_map/ppermute | solution.py:301
  18.0 14.4 %collective-permute-start.2 = (bf16[128,1024]{1,0:T(8,128)(2,1)S(1)}, bf16[128,1024]{1,0:T(8,128)(2,1)S(1)}, u32[]{:S(2)}, u32[]{:S(2)}) collective-permute-start(bf16[128,1024]{1,0:T(8,128)(2,1)S(1)} %get-tuple-element.35), channel_id=1, source_target_pairs={{0,16},{4,20},{8,24},{12,28},{16,0},{20,4},{24,8},{28,12},{1,17},{... | collective-permute-start | bytes 786440 | tf_op jit(solution)/shard_map/ppermute | solution.py:301
  19.5 12.9 %collective-permute-start.3 = (bf16[128,1024]{1,0:T(8,128)(2,1)S(1)}, bf16[128,1024]{1,0:T(8,128)(2,1)S(1)}, u32[]{:S(2)}, u32[]{:S(2)}) collective-permute-start(bf16[128,1024]{1,0:T(8,128)(2,1)S(1)} %get-tuple-element.36), channel_id=1, source_target_pairs={{0,24},{4,28},{8,16},{12,20},{16,8},{20,12},{24,0},{28,4},{1,25},{... | collective-permute-start | bytes 786440 | tf_op jit(solution)/shard_map/ppermute | solution.py:301
  20.0 9.4 %collective-permute-start.5 = (bf16[192,384]{1,0:T(8,128)(2,1)S(1)}, bf16[192,384]{1,0:T(8,128)(2,1)S(1)}, u32[]{:S(2)}, u32[]{:S(2)}) collective-permute-start(bf16[192,384]{1,0:T(8,128)(2,1)S(1)} %get-tuple-element.37), channel_id=1, source_target_pairs={{0,2},{1,3},{2,0},{3,1},{4,6},{5,7},{6,4},{7,5},{8,10},{9,11},{10,... | collective-permute-start | bytes 442376 | tf_op jit(solution)/shard_map/ppermute | solution.py:304
  20.8 11.7 %collective-permute-start.4 = (bf16[192,384]{1,0:T(8,128)(2,1)S(1)}, bf16[192,384]{1,0:T(8,128)(2,1)S(1)}, u32[]{:S(2)}, u32[]{:S(2)}) collective-permute-start(bf16[192,384]{1,0:T(8,128)(2,1)S(1)} %get-tuple-element.37), channel_id=1, source_target_pairs={{0,1},{1,0},{2,3},{3,2},{4,5},{5,4},{6,7},{7,6},{8,9},{9,8},{10,11... | collective-permute-start | bytes 442376 | tf_op jit(solution)/shard_map/ppermute | solution.py:304
  33.3 10.2 %collective-permute-start.9 = (bf16[128,1024]{1,0:T(8,128)(2,1)S(1)}, bf16[128,1024]{1,0:T(8,128)(2,1)S(1)}, u32[]{:S(2)}, u32[]{:S(2)}) collective-permute-start(bf16[128,1024]{1,0:T(8,128)(2,1)S(1)} %score.1.refs_1_), channel_id=1, source_target_pairs={{0,24},{4,28},{8,16},{12,20},{16,8},{20,12},{24,0},{28,4},{1,25},{... | collective-permute-start | bytes 786440 | tf_op jit(solution)/shard_map/ppermute | solution.py:301
  35.8 12.3 %collective-permute-start.8 = (bf16[128,1024]{1,0:T(8,128)(2,1)S(1)}, bf16[128,1024]{1,0:T(8,128)(2,1)S(1)}, u32[]{:S(2)}, u32[]{:S(2)}) collective-permute-start(bf16[128,1024]{1,0:T(8,128)(2,1)S(1)} %score.1.refs_1_), channel_id=1, source_target_pairs={{0,16},{4,20},{8,24},{12,28},{16,0},{20,4},{24,8},{28,12},{1,17},{... | collective-permute-start | bytes 786440 | tf_op jit(solution)/shard_map/ppermute | solution.py:301
  36.3 11.9 %collective-permute-start.7 = (bf16[128,1024]{1,0:T(8,128)(2,1)S(1)}, bf16[128,1024]{1,0:T(8,128)(2,1)S(1)}, u32[]{:S(2)}, u32[]{:S(2)}) collective-permute-start(bf16[128,1024]{1,0:T(8,128)(2,1)S(1)} %score.1.refs_1_), channel_id=1, source_target_pairs={{0,8},{4,12},{8,0},{12,4},{16,24},{20,28},{24,16},{28,20},{1,9},{5... | collective-permute-start | bytes 786440 | tf_op jit(solution)/shard_map/ppermute | solution.py:301
  36.8 11.7 %collective-permute-start.10 = (bf16[128,1024]{1,0:T(8,128)(2,1)S(1)}, bf16[128,1024]{1,0:T(8,128)(2,1)S(1)}, u32[]{:S(2)}, u32[]{:S(2)}) collective-permute-start(bf16[128,1024]{1,0:T(8,128)(2,1)S(1)} %score.1.refs_1_), channel_id=1, source_target_pairs={{0,4},{4,0},{8,12},{12,8},{16,20},{20,16},{24,28},{28,24},{1,5},{5... | collective-permute-start | bytes 786440 | tf_op jit(solution)/shard_map/ppermute | solution.py:298
  43.4 5.1 %collective-permute-start.13 = (bf16[128,1024]{1,0:T(8,128)(2,1)S(1)}, bf16[128,1024]{1,0:T(8,128)(2,1)S(1)}, u32[]{:S(2)}, u32[]{:S(2)}) collective-permute-start(bf16[128,1024]{1,0:T(8,128)(2,1)S(1)} %collective-permute-done.9.refs_4_), channel_id=1, source_target_pairs={{0,4},{4,0},{8,12},{12,8},{16,20},{20,16},{24,28},{28,24},{1,5},{5... | collective-permute-start | bytes 786440 | tf_op jit(solution)/shard_map/ppermute | solution.py:298
  48.0 1.5 %collective-permute-start.12 = (bf16[128,1024]{1,0:T(8,128)(2,1)S(1)}, bf16[128,1024]{1,0:T(8,128)(2,1)S(1)}, u32[]{:S(2)}, u32[]{:S(2)}) collective-permute-start(bf16[128,1024]{1,0:T(8,128)(2,1)S(1)} %collective-permute-done.8.refs_3_), channel_id=1, source_target_pairs={{0,4},{4,0},{8,12},{12,8},{16,20},{20,16},{24,28},{28,24},{1,5},{5... | collective-permute-start | bytes 786440 | tf_op jit(solution)/shard_map/ppermute | solution.py:298
  48.1 1.8 %collective-permute-start.11 = (bf16[128,1024]{1,0:T(8,128)(2,1)S(1)}, bf16[128,1024]{1,0:T(8,128)(2,1)S(1)}, u32[]{:S(2)}, u32[]{:S(2)}) collective-permute-start(bf16[128,1024]{1,0:T(8,128)(2,1)S(1)} %collective-permute-done.7.refs_2_), channel_id=1, source_target_pairs={{0,4},{4,0},{8,12},{12,8},{16,20},{20,16},{24,28},{28,24},{1,5},{5... | collective-permute-start | bytes 786440 | tf_op jit(solution)/shard_map/ppermute | solution.py:298
  54.6 42.0 %all-to-all-start = ((bf16[4,384,512]{2,1,0:T(8,128)(2,1)}), bf16[4,384,512]{2,1,0:T(8,128)(2,1)}, u32[]{:S(2)}, u32[]{:S(2)}) async-start(bf16[4,384,512]{2,1,0:T(8,128)(2,1)} %get-tuple-element.42), calls=%async_computation | async-start | bytes 3145728 | tf_op jit(solution)/shard_map/all_to_all | solution.py:373
  59.0 12.3 %collective-permute-start.14 = (bf16[3,192,384]{2,1,0:T(8,128)(2,1)S(1)}, bf16[3,192,384]{2,1,0:T(8,128)(2,1)S(1)}, u32[]{:S(2)}, u32[]{:S(2)}) collective-permute-start(bf16[3,192,384]{2,1,0:T(8,128)(2,1)S(1)} %get-tuple-element.43.refs_4_), channel_id=1, source_target_pairs={{0,8},{4,12},{8,0},{12,4},{16,24},{20,28},{24,16},{28,20},{1,9},{5... | collective-permute-start | bytes 1327112 | tf_op jit(solution)/shard_map/ppermute | solution.py:301
  60.5 15.0 %copy-start.1 = (bf16[768,128]{1,0:T(8,128)(2,1)S(1)}, bf16[768,128]{1,0:T(8,128)(2,1)}, u32[]{:S(2)}) copy-start(bf16[768,128]{1,0:T(8,128)(2,1)} %refs_1_.4) | copy-start | bytes 589828
  60.5 15.0 %copy-start.2 = (bf16[768,128]{1,0:T(8,128)(2,1)S(1)}, bf16[768,128]{1,0:T(8,128)(2,1)}, u32[]{:S(2)}) copy-start(bf16[768,128]{1,0:T(8,128)(2,1)} %refs_2_.4) | copy-start | bytes 589828
  60.5 15.0 %copy-start.3 = (bf16[768,128]{1,0:T(8,128)(2,1)S(1)}, bf16[768,128]{1,0:T(8,128)(2,1)}, u32[]{:S(2)}) copy-start(bf16[768,128]{1,0:T(8,128)(2,1)} %refs_3_.3) | copy-start | bytes 589828
  65.4 5.8 %collective-permute-start.17 = (bf16[4,64,768]{2,1,0:T(8,128)(2,1)S(1)}, bf16[4,64,768]{2,1,0:T(8,128)(2,1)S(1)}, u32[]{:S(2)}, u32[]{:S(2)}) collective-permute-start(bf16[4,64,768]{2,1,0:T(8,128)(2,1)S(1)} %get-tuple-element.46), channel_id=1, source_target_pairs={{0,4},{4,0},{8,12},{12,8},{16,20},{20,16},{24,28},{28,24},{1,5},{5... | collective-permute-start | bytes 1179656 | tf_op jit(solution)/shard_map/ppermute | solution.py:298
  65.5 9.9 %collective-permute-start.15 = (bf16[3,192,384]{2,1,0:T(8,128)(2,1)S(1)}, bf16[3,192,384]{2,1,0:T(8,128)(2,1)S(1)}, u32[]{:S(2)}, u32[]{:S(2)}) collective-permute-start(bf16[3,192,384]{2,1,0:T(8,128)(2,1)S(1)} %get-tuple-element.43.refs_4_), channel_id=1, source_target_pairs={{0,4},{4,0},{8,12},{12,8},{16,20},{20,16},{24,28},{28,24},{1,5},{5... | collective-permute-start | bytes 1327112 | tf_op jit(solution)/shard_map/ppermute | solution.py:298
  71.2 4.2 %collective-permute-start.16 = (bf16[3,192,384]{2,1,0:T(8,128)(2,1)S(1)}, bf16[3,192,384]{2,1,0:T(8,128)(2,1)S(1)}, u32[]{:S(2)}, u32[]{:S(2)}) collective-permute-start(bf16[3,192,384]{2,1,0:T(8,128)(2,1)S(1)} %collective-permute-done.14.refs_5_), channel_id=1, source_target_pairs={{0,4},{4,0},{8,12},{12,8},{16,20},{20,16},{24,28},{28,24},{1,5},{5... | collective-permute-start | bytes 1327112 | tf_op jit(solution)/shard_map/ppermute | solution.py:298
  71.9 5.3 %collective-permute-start.18 = (bf16[64,768]{1,0:T(8,128)(2,1)S(1)}, bf16[64,768]{1,0:T(8,128)(2,1)S(1)}, u32[]{:S(2)}, u32[]{:S(2)}) collective-permute-start(bf16[64,768]{1,0:T(8,128)(2,1)S(1)} %get-tuple-element.48), channel_id=1, source_target_pairs={{0,8},{4,12},{8,0},{12,4},{16,24},{20,28},{24,16},{28,20},{1,9},{5... | collective-permute-start | bytes 294920 | tf_op jit(solution)/shard_map/ppermute | solution.py:301
  73.4 7.0 %collective-permute-start.19 = (bf16[64,768]{1,0:T(8,128)(2,1)S(1)}, bf16[64,768]{1,0:T(8,128)(2,1)S(1)}, u32[]{:S(2)}, u32[]{:S(2)}) collective-permute-start(bf16[64,768]{1,0:T(8,128)(2,1)S(1)} %get-tuple-element.49), channel_id=1, source_target_pairs={{0,16},{4,20},{8,24},{12,28},{16,0},{20,4},{24,8},{28,12},{1,17},{... | collective-permute-start | bytes 294920 | tf_op jit(solution)/shard_map/ppermute | solution.py:301
  74.3 6.2 %collective-permute-start.20 = (bf16[64,768]{1,0:T(8,128)(2,1)S(1)}, bf16[64,768]{1,0:T(8,128)(2,1)S(1)}, u32[]{:S(2)}, u32[]{:S(2)}) collective-permute-start(bf16[64,768]{1,0:T(8,128)(2,1)S(1)} %get-tuple-element.50), channel_id=1, source_target_pairs={{0,24},{4,28},{8,16},{12,20},{16,8},{20,12},{24,0},{28,4},{1,25},{... | collective-permute-start | bytes 294920 | tf_op jit(solution)/shard_map/ppermute | solution.py:301
  81.1 6.7 %collective-permute-start.23 = (bf16[64,768]{1,0:T(8,128)(2,1)S(1)}, bf16[64,768]{1,0:T(8,128)(2,1)S(1)}, u32[]{:S(2)}, u32[]{:S(2)}) collective-permute-start(bf16[64,768]{1,0:T(8,128)(2,1)S(1)} %sum_weights.1.refs_1_), channel_id=1, source_target_pairs={{0,24},{4,28},{8,16},{12,20},{16,8},{20,12},{24,0},{28,4},{1,25},{... | collective-permute-start | bytes 294920 | tf_op jit(solution)/shard_map/ppermute | solution.py:301
  82.6 5.4 %collective-permute-start.22 = (bf16[64,768]{1,0:T(8,128)(2,1)S(1)}, bf16[64,768]{1,0:T(8,128)(2,1)S(1)}, u32[]{:S(2)}, u32[]{:S(2)}) collective-permute-start(bf16[64,768]{1,0:T(8,128)(2,1)S(1)} %sum_weights.1.refs_1_), channel_id=1, source_target_pairs={{0,16},{4,20},{8,24},{12,28},{16,0},{20,4},{24,8},{28,12},{1,17},{... | collective-permute-start | bytes 294920 | tf_op jit(solution)/shard_map/ppermute | solution.py:301
  83.2 5.1 %collective-permute-start.21 = (bf16[64,768]{1,0:T(8,128)(2,1)S(1)}, bf16[64,768]{1,0:T(8,128)(2,1)S(1)}, u32[]{:S(2)}, u32[]{:S(2)}) collective-permute-start(bf16[64,768]{1,0:T(8,128)(2,1)S(1)} %sum_weights.1.refs_1_), channel_id=1, source_target_pairs={{0,8},{4,12},{8,0},{12,4},{16,24},{20,28},{24,16},{28,20},{1,9},{5... | collective-permute-start | bytes 294920 | tf_op jit(solution)/shard_map/ppermute | solution.py:301
  84.6 4.0 %collective-permute-start.24 = (bf16[64,768]{1,0:T(8,128)(2,1)S(1)}, bf16[64,768]{1,0:T(8,128)(2,1)S(1)}, u32[]{:S(2)}, u32[]{:S(2)}) collective-permute-start(bf16[64,768]{1,0:T(8,128)(2,1)S(1)} %sum_weights.1.refs_1_), channel_id=1, source_target_pairs={{0,4},{4,0},{8,12},{12,8},{16,20},{20,16},{24,28},{28,24},{1,5},{5... | collective-permute-start | bytes 294920 | tf_op jit(solution)/shard_map/ppermute | solution.py:298
  87.8 1.3 %collective-permute-start.27 = (bf16[64,768]{1,0:T(8,128)(2,1)S(1)}, bf16[64,768]{1,0:T(8,128)(2,1)S(1)}, u32[]{:S(2)}, u32[]{:S(2)}) collective-permute-start(bf16[64,768]{1,0:T(8,128)(2,1)S(1)} %collective-permute-done.23.refs_4_), channel_id=1, source_target_pairs={{0,4},{4,0},{8,12},{12,8},{16,20},{20,16},{24,28},{28,24},{1,5},{5... | collective-permute-start | bytes 294920 | tf_op jit(solution)/shard_map/ppermute | solution.py:298
  88.1 1.3 %collective-permute-start.26 = (bf16[64,768]{1,0:T(8,128)(2,1)S(1)}, bf16[64,768]{1,0:T(8,128)(2,1)S(1)}, u32[]{:S(2)}, u32[]{:S(2)}) collective-permute-start(bf16[64,768]{1,0:T(8,128)(2,1)S(1)} %collective-permute-done.22.refs_3_), channel_id=1, source_target_pairs={{0,4},{4,0},{8,12},{12,8},{16,20},{20,16},{24,28},{28,24},{1,5},{5... | collective-permute-start | bytes 294920 | tf_op jit(solution)/shard_map/ppermute | solution.py:298
  88.3 1.3 %collective-permute-start.25 = (bf16[64,768]{1,0:T(8,128)(2,1)S(1)}, bf16[64,768]{1,0:T(8,128)(2,1)S(1)}, u32[]{:S(2)}, u32[]{:S(2)}) collective-permute-start(bf16[64,768]{1,0:T(8,128)(2,1)S(1)} %collective-permute-done.21.refs_2_), channel_id=1, source_target_pairs={{0,4},{4,0},{8,12},{12,8},{16,20},{20,16},{24,28},{28,24},{1,5},{5... | collective-permute-start | bytes 294920 | tf_op jit(solution)/shard_map/ppermute | solution.py:298
  (1 other events, 1.4 us)

commit v3 on v2

--- a/solution.py
+++ b/solution.py
@@ -12,7 +12,7 @@
 F32 = jnp.float32
 BF16 = jnp.bfloat16
 VMEM_BYTES = 16 * 1024 * 1024
-SHARERS = 4
+SHARERS = 8
 
 
 def dot_nn(left, right):
@@ -110,11 +110,11 @@
         copy.start()
     for copy in loads:
         copy.wait()
-    depth = slab.shape[0]
+    depth = slab.shape[1]
     at = pl.ds(pl.multiple_of(place[3] * depth, depth), depth)
     for t in range(3):
         both[t * width : (t + 1) * width, :] = three_w[t].T
-        slab[:, t * width : (t + 1) * width] = three_w[t, at, :]
+        slab[0, :, t * width : (t + 1) * width] = three_w[t, at, :]
     for r in range(rows):
         in_x[r].wait()
         three = dot_nt(both[...], rows_x[r]).astype(BF16)
@@ -143,6 +143,27 @@
     outs[-1][...] = slab[...]
 
 
+def join_kernel(place, *refs):
+    *parts, out = refs
+    at = 0
+    for part in parts:
+        out[at : at + part.shape[0]] = part[...]
+        at += part.shape[0]
+
+
+def pack_kernel(place, *refs):
+    *slabs, out = refs
+    at = 0
+    for slab in slabs:
+        count, depth, wide = slab.shape
+        folds = out.shape[1] // wide
+        rows = depth // folds
+        for z in range(count):
+            for i in range(folds):
+                out[at : at + rows, i * wide : (i + 1) * wide] = slab[z, i * rows : (i + 1) * rows]
+            at += rows
+
+
 def added(parts, cols=slice(None)):
     total = parts[0][:, cols].astype(F32)
     for part in parts[1:]:
@@ -167,19 +188,19 @@
         base = 2 * jnp.bitwise_xor(place[0], k)
         for side, part in ((place[1], mine[k]), (1 - place[1], other[k])):
             at = pl.ds(pl.multiple_of((base + side) * piece_rows, piece_rows), piece_rows)
-            full[at, :] = part[...].astype(full.dtype)
-
-
-def grads_kernel(pieces, zeds, place, *refs):
+            full[at, :] = part[0:piece_rows].astype(full.dtype)
+
+
+def grads_kernel(pieces, place, *refs):
     mine, other = refs[0:pieces], refs[pieces : 2 * pieces]
     qt, kt, vt, gt = refs[2 * pieces : 2 * pieces + 4]
-    slabs = refs[2 * pieces + 4 : 2 * pieces + 3 + zeds]
-    send_far, four_far, packed, full, send, four, sems = refs[2 * pieces + 3 + zeds :]
+    send_far, four_far, full, send, four, sems = refs[2 * pieces + 4 :]
+    zeds = send.shape[0]
     heads, _, cols = qt.shape
-    rows, stacked, _ = four.shape
-    width = stacked // 4
-    block = cols // zeds
+    stacked, tokens = four.shape
+    rows, width, block = tokens // cols, stacked // 4, cols // zeds
     assemble(place, mine, other, full)
+    copies = []
     for h in range(heads):
         span = slice(h * cols, (h + 1) * cols)
         values = (
@@ -192,47 +213,68 @@
             value = value.astype(BF16)
             at = slice(t * width + h * HEAD_DIM, t * width + (h + 1) * HEAD_DIM)
             for r in range(rows):
-                four[r, at, :] = value[r * HEAD_DIM : (r + 1) * HEAD_DIM]
-    copies = []
-    for z in range(zeds):
-        for r in range(rows):
-            part = four[r, 0 : 3 * width, z * block : (z + 1) * block]
-            send[z, :, r * block : (r + 1) * block] = part
-        copies += fetch([(send.at[z], send_far.at[z])], sems.at[pl.ds(z, 1)])
-    copies += fetch([(four, four_far)], sems.at[pl.ds(zeds, 1)])
-    for k, slab in enumerate(slabs):
-        packed[k] = slab[...]
+                part = value[r * HEAD_DIM : (r + 1) * HEAD_DIM]
+                four[at, r * cols : (r + 1) * cols] = part
+                if t < 3:
+                    for z in range(zeds):
+                        cut = part[:, z * block : (z + 1) * block]
+                        send[z, at, r * block : (r + 1) * block] = cut
+            pairs = [(send.at[:, at], send_far.at[:, at])] if t < 3 else []
+            copies += fetch(pairs + [(four.at[at], four_far.at[at])], sems.at[h * 4 + t])
     for copy in copies:
         copy.wait()
 
 
 def weights_kernel(place, x_far, og_far, four_far, keep, give, x, og, four, total, sems):
-    rows, stacked, _ = four.shape
+    stacked, tokens = four.shape
     three = 3 * stacked // 4
     piece_rows = keep.shape[1]
-    copies = [
-        fetch([(four_far.at[r], four.at[r]), (x_far.at[r], x.at[r]), (og_far.at[r], og.at[r])], sems.at[r])
-        for r in range(rows)
-    ]
-    for r in range(rows):
-        for copy in copies[r]:
+    steps = sems.shape[0]
+    spans = [slice(i * tokens // steps, (i + 1) * tokens // steps) for i in range(steps)]
+    copies = []
+    for i, span in enumerate(spans):
+        pairs = [(four_far.at[:, span], four.at[:, span]), (x_far.at[span], x.at[span])]
+        copies.append(fetch(pairs + [(og_far.at[span], og.at[span])], sems.at[i]))
+    for i, span in enumerate(spans):
+        for copy in copies[i]:
             copy.wait()
-        upper = dot_nn(four[r, 0:three, :], x[r])
-        lower = dot_nn(four[r, three:, :], og[r])
-        if r == 0:
-            total[0:three, :] = upper
-            total[three:, :] = lower
-        else:
-            total[0:three, :] += upper
-            total[three:, :] += lower
-    for i in range(0, stacked, piece_rows):
-        value = total[i : i + piece_rows, :].astype(BF16)
-        deal(place[0], place[1], i // piece_rows, keep, give, value)
-
-
-def sum_kernel(scale, place, *refs):
-    *parts, out = refs
-    out[...] = (added(parts) * scale).astype(out.dtype)
+        for first, last, other in ((0, three, x), (three, stacked, og)):
+            part = dot_nn(four[first:last, span], other[span, :])
+            if i > 0:
+                part = part + total[first:last, :]
+            if i < steps - 1:
+                total[first:last, :] = part
+            else:
+                value = part.astype(BF16)
+                for j in range(first, last, piece_rows):
+                    piece = value[j - first : j - first + piece_rows]
+                    deal(place[0], place[1], j // piece_rows, keep, give, piece)
+
+
+def pair_append_kernel(place, keep, got, packed, *outs):
+    pieces, piece_rows, _ = keep.shape
+    for k in range(pieces):
+        outs[k][0:piece_rows] = (keep[k].astype(F32) + got[k].astype(F32)).astype(BF16)
+        if outs[k].shape[0] > piece_rows:
+            outs[k][piece_rows:] = packed[...]
+
+
+def sum_relay_kernel(scale, place, packed, *refs):
+    *parts, out, first, second, third, slabs = refs
+    rows, extra = out.shape[0], packed.shape[0]
+    total = parts[0][0:rows].astype(F32)
+    for part in parts[1:]:
+        total = total + part[0:rows].astype(F32)
+    total = (total * scale).astype(out.dtype)
+    out[...] = total
+    cut = first.shape[0] - rows
+    for target in (first, second, third):
+        target[0:rows] = total
+    first[rows:] = parts[2][rows : rows + cut]
+    second[rows:] = parts[1][rows + cut : rows + 2 * cut]
+    third[rows:] = packed[2 * cut :]
+    slabs[0] = parts[1][rows:]
+    slabs[1] = parts[2][rows:]
 
 
 def unpack_kernel(pieces, place, *refs):
@@ -245,34 +287,57 @@
     outs[-1][...] = full[(len(outs) - 1) * width :, :]
 
 
-def gather_weights_kernel(slabs, place, wq, wk, wv, *refs):
-    mine, other, full = refs[0:slabs], refs[slabs : 2 * slabs], refs[-1]
-    zeds, _, _ = full.shape
-    width = wq.shape[1]
-    depth = mine[0].shape[1]
+def gather_weights_kernel(zeds, place, wq, wk, wv, own, own_other, near, near_other, *refs):
+    *far, full = refs
+    model, width = wq.shape
+    wide = 3 * width
+    extra = own.shape[0]
+    folds = model // wide
+    rows = extra // (zeds - 1)
+    depth = rows * folds
     zed = place[2]
-    for t, own in enumerate((wq, wk, wv)):
-        full[zed, :, t * width : (t + 1) * width] = own[...]
-    for k in range(slabs):
+    for t, w in enumerate((wq, wk, wv)):
+        full[:, pl.ds(pl.multiple_of((3 * zed + t) * width, width), width)] = w[...]
+    cut = extra // 3 // 16 * 16
+    skip = far[0].shape[0] - cut
+
+    def part(side, k, first, count):
+        if k == 0:
+            return (own, own_other)[side][first : first + count]
+        if k < 3:
+            return (near, near_other)[side][k - 1, first : first + count]
+        way = min(first // cut, 2)
+        at = skip + first - way * cut
+        return far[3 * side + way][at : at + count]
+
+    unit = math.gcd(rows, cut)
+    for k in range(4):
         base = 2 * jnp.bitwise_xor(place[3] // 2, k)
-        for side, part in ((place[1], mine[k]), (1 - place[1], other[k])):
-            at = pl.ds(pl.multiple_of((base + side) * depth, depth), depth)
-            for z in range(1, zeds):
-                full[jnp.bitwise_xor(zed, z), at, :] = part[z - 1]
-
-
-def inputs_kernel(place, sent_far, full, out, sent, sems):
+        for side, core in ((0, place[1]), (1, 1 - place[1])):
+            for first in range(0, extra, unit):
+                z, offset = 1 + first // rows, first % rows
+                cols = pl.ds(pl.multiple_of(jnp.bitwise_xor(zed, z) * wide, width), wide)
+                value = part(side, k, first, unit)
+                for i in range(folds):
+                    row = pl.multiple_of((base + core) * depth + i * rows + offset, unit)
+                    full[pl.ds(row, unit), cols] = value[:, i * wide : (i + 1) * wide]
+
+
+def inputs_kernel(place, sent_far, full, out, sent, total, sems):
     rows, block, _ = out.shape
-    zeds = sent.shape[0]
-    copies = fetch([(sent_far.at[z], sent.at[z]) for z in range(zeds)], sems)
+    deep = sent.shape[0] // 2
+    halves = (slice(0, deep), slice(deep, 2 * deep))
+    copies = fetch([(sent_far.at[half], sent.at[half]) for half in halves], sems)
     copies[0].wait()
-    value = dot_nt(sent[0].T, full[0])
-    for z in range(1, zeds):
-        copies[z].wait()
-        value = value + dot_nt(sent[z].T, full[z])
-    value = value.astype(BF16)
-    for r in range(rows):
-        out[r] = value[r * block : (r + 1) * block]
+    total[...] = dot_nn(full[:, halves[0]], sent[halves[0], :])
+    copies[1].wait()
+    step = min(2, rows)
+    for r in range(0, rows, step):
+        span = slice(r * block, (r + step) * block)
+        value = total[:, span] + dot_nn(full[:, halves[1]], sent[halves[1], span])
+        value = value.astype(BF16).T
+        for i in range(step):
+            out[r + i] = value[i * block : (i + 1) * block]
 
 
 def body(inputs, out_grad, w_query, w_key, w_value, w_output):
@@ -290,6 +355,7 @@
     block = cols // zeds
     sharers = min(seqs, SHARERS)
     depth = model // sharers
+    folds = model // (3 * width)
     me = lax.axis_index("seq")
     zed = lax.axis_index("head")
     place = jnp.stack([me // 2, me % 2, zed, me % sharers]).astype(jnp.int32)
@@ -321,7 +387,7 @@
 
     qt, kt, vt, gt, keep, give, slab = call(
         front_kernel,
-        (blocks,) * 4 + (dealt,) * 2 + (shape(depth, 3 * width),),
+        (blocks,) * 4 + (dealt,) * 2 + (shape(1, depth, 3 * width),),
         (place, inputs, out_grad, w_query, w_key, w_value, w_output),
         hbm=6,
         scratch=[
@@ -343,45 +409,53 @@
         name="pair_scores",
     )
     parts = spread(paired)
-    slabs = [along(slab, k) for k in range(1, zeds)]
+    groups, span = [slab], 1
+    while span < zeds:
+        if span > 1:
+            slab = call(join_kernel, shape(span, depth, 3 * width), (place, *groups), name="join")
+        groups.append(along(slab, span))
+        span *= 2
     scored = call(
         partial(score_kernel, logit_scale),
         shape(shard, 2 * cols),
         (place, *parts),
-        held=slabs,
+        held=(slab,),
         name="score",
     )
+    packed = call(
+        pack_kernel, shape((zeds - 1) * depth // folds, model), (place, *groups[1:]), name="pack"
+    )
+    packed_other = swap(packed)
     mine, other = gathered(scored, pieces)
-    send, four, packed = call(
-        partial(grads_kernel, pieces, zeds),
+    send, four = call(
+        partial(grads_kernel, pieces),
         (
-            shape(zeds, 3 * width, rows * block),
-            shape(rows, 4 * width, cols),
-            shape(zeds - 1, depth, 3 * width),
+            pltpu.HBM((zeds, 3 * width, rows * block), BF16),
+            pltpu.HBM((4 * width, rows * cols), BF16),
         ),
-        (place, *mine, *other, qt, kt, vt, gt, *slabs),
-        out_specs=(hbm_spec(), hbm_spec(), vmem_spec()),
+        (place, *mine, *other, qt, kt, vt, gt),
+        held=(packed_other,),
+        out_specs=(hbm_spec(), hbm_spec()),
         scratch=[
             pltpu.VMEM((heads * cols, 2 * cols), BF16),
             pltpu.VMEM((zeds, 3 * width, rows * block), BF16),
-            pltpu.VMEM((rows, 4 * width, cols), BF16),
-            pltpu.SemaphoreType.DMA((zeds + 1,)),
+            pltpu.VMEM((4 * width, rows * cols), BF16),
+            pltpu.SemaphoreType.DMA((heads * 4, 2)),
         ],
         flops=4 * score_flops,
         name="grads",
     )
     sent = lax.all_to_all(send, "head", 0, 0, tiled=True)
-    mine_w, other_w = gathered(packed, sharers // 2)
 
     keep, give = call(
         weights_kernel,
         [shape(pieces, wide, model)] * 2,
-        (place, inputs, out_grad, four),
+        (place, inputs.reshape(-1, model), out_grad.reshape(-1, model), four),
         hbm=3,
         scratch=[
-            rows_in,
-            rows_in,
-            pltpu.VMEM((rows, 4 * width, cols), BF16),
+            pltpu.VMEM((rows * cols, model), BF16),
+            pltpu.VMEM((rows * cols, model), BF16),
+            pltpu.VMEM((4 * width, rows * cols), BF16),
             pltpu.VMEM((4 * width, model), F32),
             pltpu.SemaphoreType.DMA((rows, 3)),
         ],
@@ -389,24 +463,38 @@
         moved=inputs.size * 4,
         name="weights",
     )
+    extra = packed.shape[0]
+    cut = extra // 48 * 16
+    near = (1, 2)
     paired = call(
-        pair_kernel, [shape(wide, model)] * pieces, (place, keep, swap(give)), name="pair_weights"
+        pair_append_kernel,
+        [shape(wide + (extra if k in near else 0), model) for k in range(pieces)],
+        (place, keep, swap(give), packed),
+        name="pair_weights",
     )
     parts = spread(paired)
+    total_w, first, second, third, slabs = call(
+        partial(sum_relay_kernel, inv_root),
+        (
+            shape(wide, model),
+            shape(wide + cut, model),
+            shape(wide + cut, model),
+            shape(wide + extra - 2 * cut, model),
+            shape(2, extra, model),
+        ),
+        (place, packed, *parts),
+        name="sum_weights",
+    )
+    sums = [total_w, first, second, third] + [total_w] * (pieces - 4)
+    mine = [total_w] + [across(sums[k], k) for k in range(1, pieces)]
+    other = [swap(part) for part in mine]
     full = call(
-        partial(gather_weights_kernel, sharers // 2),
-        shape(zeds, model, 3 * width),
-        (place, w_query, w_key, w_value, *mine_w, *other_w),
+        partial(gather_weights_kernel, zeds),
+        shape(model, zeds * 3 * width),
+        (place, w_query, w_key, w_value, packed, packed_other, slabs, swap(slabs))
+        + (*mine[1:4], *other[1:4]),
         name="gather_weights",
     )
-    total_w = call(
-        partial(sum_kernel, inv_root),
-        shape(wide, model),
-        (place, *parts),
-        held=(full,),
-        name="sum_weights",
-    )
-    mine, other = gathered(total_w, pieces)
     grad_q, grad_k, grad_v, grad_o = call(
         partial(unpack_kernel, pieces),
         [shape(model, width, dtype=F32)] * 3 + [shape(width, model, dtype=F32)],
@@ -417,9 +505,13 @@
     grad_inputs = call(
         inputs_kernel,
         shape(rows, block, model),
-        (place, sent, full),
+        (place, sent.reshape(-1, rows * block), full),
         hbm=1,
-        scratch=[pltpu.VMEM((zeds, 3 * width, rows * block), BF16), pltpu.SemaphoreType.DMA((zeds,))],
+        scratch=[
+            pltpu.VMEM((zeds * 3 * width, rows * block), BF16),
+            pltpu.VMEM((model, rows * block), F32),
+            pltpu.SemaphoreType.DMA((2,)),
+        ],
         flops=3 * dot_flops,
         name="inputs",
     )

time: 102 us -> 95 us (0.931)
  starting transfers between devices: 33.8 us -> 26.4 us
  waiting for transfers between devices: 39.5 us -> 41.4 us
  local copies, waits for them, and re-layouts: 1.37 us -> 0.02 us
    ppermute x13 -> x12, waiting for transfers between devices: 24.1 us -> 31.6 us  [across(): return lax.ppermute(value, 'seq', [(i, i ^ 2 * k) for i in range(seqs)])]
    ppermute x3 -> x2, starting transfers between devices: 11.8 us -> 4.58 us  [along(): return lax.ppermute(value, 'head', [(i, i ^ k) for i in range(zeds)])]
    all_to_all x1, waiting for transfers between devices: 5.01 us -> 0.75 us  [body(): sent = lax.all_to_all(send, 'head', 0, 0, tiled=True)]
    ppermute x3 -> x2, waiting for transfers between devices: 5.69 us -> 2.33 us  [along(): return lax.ppermute(value, 'head', [(i, i ^ k) for i in range(zeds)])]
    ppermute x12, waiting for transfers between devices: 4.72 us -> 6.78 us  [swap(): return lax.ppermute(value, 'seq', [(i, i ^ 1) for i in range(seqs)])]
    unnamed x8 -> x6, local copies, waits for them, and re-layouts: 1.37 us -> 0.02 us
    ppermute x13 -> x12, starting transfers between devices: 15.7 us -> 15.1 us  [across(): return lax.ppermute(value, 'seq', [(i, i ^ 2 * k) for i in range(seqs)])]
    pallas_call x10 -> x12, Pallas kernels: 25.9 us -> 26 us  [call(): pl.pallas_call(run, out_shape=outs, in_specs=[smem_spec()] + [hbm_spec()]...]
  transfers between devices with their start and end apart: 29 -> 27, of which waited for: 18 -> 14; matrix products, arithmetic and copies ran while one was open for 0% -> 0% of each run, Pallas kernels for 9% -> 11%
where the time goes in v3:
time: 95 us; the launch traced here: 94.8 us
  waiting for transfers between devices  41.4 us (44%)
  starting transfers between devices  26.4 us (28%)
  Pallas kernels  26 us (27%)
    ppermute x12, waiting for transfers between devices, across(): return lax.ppermute(value, 'seq', [(i, i ^ 2 * k) for i in range(seqs)])  31.6 us
    pallas_call x12, Pallas kernels, call(): pl.pallas_call(run, out_shape=outs, in_specs=[smem_spec()] + [hbm_spec()]...  26 us
    ppermute x12, starting transfers between devices, across(): return lax.ppermute(value, 'seq', [(i, i ^ 2 * k) for i in range(seqs)])  15.1 us
    ppermute x12, waiting for transfers between devices, swap(): return lax.ppermute(value, 'seq', [(i, i ^ 1) for i in range(seqs)])  6.78 us
    all_to_all x1, starting transfers between devices, body(): sent = lax.all_to_all(send, 'head', 0, 0, tiled=True)  4.89 us
    ppermute x2, starting transfers between devices, along(): return lax.ppermute(value, 'head', [(i, i ^ k) for i in range(zeds)])  4.58 us
    ppermute x2, waiting for transfers between devices, along(): return lax.ppermute(value, 'head', [(i, i ^ k) for i in range(zeds)])  2.33 us
  transfers between devices with their start and end apart: 27, of which 14 were waited for; matrix products, arithmetic and copies ran while one was open for 0% of the time, Pallas kernels for 11%

profile of v3, /device:TPU:0, one launch (start us, length us, event | category | flops | bytes accessed | tf_op | source)
XLA Modules:
  0.0 94.8 jit_solution(9653388851499813414)
XLA Ops:
  0.7 7.2 %front.1 = (bf16[2,256,512]{2,1,0:T(8,128)(2,1)S(1)}, bf16[2,256,512]{2,1,0:T(8,128)(2,1)S(1)}, bf16[2,256,512]{2,1,0:T(8,128)(2,1)S(1)}, bf16[2,256,512]{2,1,0:...) custom-call(s32[4]{0:T(128)S(1)} %pad_add_fusion.refs_0_, ...), custom_call_target="tpu_custom_call" | custom-call | flops 2147483648 | tf_op jit(solution)/shard_map/front/pallas_call | solution.py:49
  8.4 2.3 %collective-permute-done.refs_2_ = bf16[4,128,1024]{2,1,0:T(8,128)(2,1)S(1)} collective-permute-done((bf16[4,128,1024]{2,1,0:T(8,128)(2,1)S(1)}, bf16[4,128,1024]{2,1,0:T(8,128)(2,1)S(1)}, u32[]{:S(2)}, u32[]{:S(2)}) %collective-permute-start) | collective-permute-done | bytes 1048608 | tf_op jit(solution)/shard_map/ppermute | solution.py:364
  10.7 0.8 pair_scores.1
  11.5 2.9 %collective-permute-start.1 = (bf16[128,1024]{1,0:T(8,128)(2,1)S(1)}, bf16[128,1024]{1,0:T(8,128)(2,1)S(1)}, u32[]{:S(2)}, u32[]{:S(2)}) collective-permute-start(bf16[128,1024]{1,0:T(8,128)(2,1)S(1)} %get-tuple-element.38), channel_id=1, source_target_pairs={{0,8},{4,12},{8,0},{12,4},{16,24},{20,28},{24,16},{28,20},{1,9},{5... | collective-permute-start | bytes 786440 | tf_op jit(solution)/shard_map/ppermute | solution.py:367
  14.4 1.5 %collective-permute-start.2 = (bf16[128,1024]{1,0:T(8,128)(2,1)S(1)}, bf16[128,1024]{1,0:T(8,128)(2,1)S(1)}, u32[]{:S(2)}, u32[]{:S(2)}) collective-permute-start(bf16[128,1024]{1,0:T(8,128)(2,1)S(1)} %get-tuple-element.39), channel_id=1, source_target_pairs={{0,16},{4,20},{8,24},{12,28},{16,0},{20,4},{24,8},{28,12},{1,17},{... | collective-permute-start | bytes 786440 | tf_op jit(solution)/shard_map/ppermute | solution.py:367
  16.0 2.0 %collective-permute-start.4 = (bf16[1,96,384]{2,1,0:T(8,128)(2,1)S(1)}, bf16[1,96,384]{2,1,0:T(8,128)(2,1)S(1)}, u32[]{:S(2)}, u32[]{:S(2)}) collective-permute-start(bf16[1,96,384]{2,1,0:T(8,128)(2,1)S(1)} %get-tuple-element.41.refs_1_), channel_id=1, source_target_pairs={{0,1},{1,0},{2,3},{3,2},{4,5},{5,4},{6,7},{7,6},{8,9},{9,8},{10,11... | collective-permute-start | bytes 221192 | tf_op jit(solution)/shard_map/ppermute | solution.py:370
  18.0 2.3 %collective-permute-done.4.refs_2_.refs_1_ = bf16[1,96,384]{2,1,0:T(8,128)(2,1)S(1)} collective-permute-done((bf16[1,96,384]{2,1,0:T(8,128)(2,1)S(1)}, bf16[1,96,384]{2,1,0:T(8,128)(2,1)S(1)}, u32[]{:S(2)}, u32[]{:S(2)}) %collective-permute-start.4) | collective-permute-done | bytes 73760 | tf_op jit(solution)/shard_map/ppermute | solution.py:370
  21.5 6.6 %collective-permute-done.2.refs_3_ = bf16[128,1024]{1,0:T(8,128)(2,1)S(1)} collective-permute-done((bf16[128,1024]{1,0:T(8,128)(2,1)S(1)}, bf16[128,1024]{1,0:T(8,128)(2,1)S(1)}, u32[]{:S(2)}, u32[]{:S(2)}) %collective-permute-start.2) | collective-permute-done | bytes 262176 | tf_op jit(solution)/shard_map/ppermute | solution.py:367
  28.1 0.8 score.1.refs_1_
  28.9 1.5 %collective-permute-start.7 = (bf16[128,1024]{1,0:T(8,128)(2,1)S(1)}, bf16[128,1024]{1,0:T(8,128)(2,1)S(1)}, u32[]{:S(2)}, u32[]{:S(2)}) collective-permute-start(bf16[128,1024]{1,0:T(8,128)(2,1)S(1)} %score.1.refs_1_), channel_id=1, source_target_pairs={{0,24},{4,28},{8,16},{12,20},{16,8},{20,12},{24,0},{28,4},{1,25},{... | collective-permute-start | bytes 786440 | tf_op jit(solution)/shard_map/ppermute | solution.py:367
  30.5 1.2 %collective-permute-start.6 = (bf16[128,1024]{1,0:T(8,128)(2,1)S(1)}, bf16[128,1024]{1,0:T(8,128)(2,1)S(1)}, u32[]{:S(2)}, u32[]{:S(2)}) collective-permute-start(bf16[128,1024]{1,0:T(8,128)(2,1)S(1)} %score.1.refs_1_), channel_id=1, source_target_pairs={{0,16},{4,20},{8,24},{12,28},{16,0},{20,4},{24,8},{28,12},{1,17},{... | collective-permute-start | bytes 786440 | tf_op jit(solution)/shard_map/ppermute | solution.py:367
  31.7 0.8 collective-permute-start.5
  32.5 2.6 %collective-permute-start.12 = (bf16[2,96,384]{2,1,0:T(8,128)(2,1)S(1)}, bf16[2,96,384]{2,1,0:T(8,128)(2,1)S(1)}, u32[]{:S(2)}, u32[]{:S(2)}) collective-permute-start(bf16[2,96,384]{2,1,0:T(8,128)(2,1)S(1)} %join.1.refs_5_), channel_id=1, source_target_pairs={{0,2},{1,3},{2,0},{3,1},{4,6},{5,7},{6,4},{7,5},{8,10},{9,11},{10,... | collective-permute-start | bytes 442376 | tf_op jit(solution)/shard_map/ppermute | solution.py:370
  35.0 4.1 %collective-permute-done.7.refs_4_ = bf16[128,1024]{1,0:T(8,128)(2,1)S(1)} collective-permute-done((bf16[128,1024]{1,0:T(8,128)(2,1)S(1)}, bf16[128,1024]{1,0:T(8,128)(2,1)S(1)}, u32[]{:S(2)}, u32[]{:S(2)}) %collective-permute-start.7) | collective-permute-done | bytes 262176 | tf_op jit(solution)/shard_map/ppermute | solution.py:367
  39.2 3.6 %collective-permute-done.6.refs_3_ = bf16[128,1024]{1,0:T(8,128)(2,1)S(1)} collective-permute-done((bf16[128,1024]{1,0:T(8,128)(2,1)S(1)}, bf16[128,1024]{1,0:T(8,128)(2,1)S(1)}, u32[]{:S(2)}, u32[]{:S(2)}) %collective-permute-start.6) | collective-permute-done | bytes 262176 | tf_op jit(solution)/shard_map/ppermute | solution.py:367
  44.0 1.5 %collective-permute-done.13.refs_13_.refs_5_ = bf16[144,768]{1,0:T(8,128)(2,1)S(1)} collective-permute-done((bf16[144,768]{1,0:T(8,128)(2,1)S(1)}, bf16[144,768]{1,0:T(8,128)(2,1)S(1)}, u32[]{:S(2)}, u32[]{:S(2)}) %collective-permute-start.13) | collective-permute-done | bytes 221216 | tf_op jit(solution)/shard_map/ppermute | solution.py:364
  45.4 3.0 %grads.1 = (bf16[4,384,512]{2,1,0:T(8,128)(2,1)}, bf16[512,2048]{1,0:T(8,128)(2,1)}) custom-call(s32[4]{0:T(128)S(1)} %pad_add_fusion.refs_0_, bf16[128,1024]{1,0:T(8,128)(2,1)S(1)} %score.1.refs_1_, bf16[128,1024]{1,0:T(8,128)(2,1)S(1)} %collective-permute-done.5.refs_2_, bf16[128,1024]{1,0:T(8,128)(2,1)S(1)} %collective-permute-done.6.refs_3_, ...), custom_call_target="tpu_custom_call" | custom-call | flops 1073741824 | tf_op jit(solution)/shard_map/grads/pallas_call | solution.py:49
  48.4 4.9 %all-to-all-start = ((bf16[4,384,512]{2,1,0:T(8,128)(2,1)}), bf16[4,384,512]{2,1,0:T(8,128)(2,1)}, u32[]{:S(2)}, u32[]{:S(2)}) async-start(bf16[4,384,512]{2,1,0:T(8,128)(2,1)} %get-tuple-element.46), calls=%async_computation | async-start | bytes 3145728 | tf_op jit(solution)/shard_map/all_to_all | solution.py:448
  53.3 5.1 %weights.1 = (bf16[4,64,768]{2,1,0:T(8,128)(2,1)S(1)}, bf16[4,64,768]{2,1,0:T(8,128)(2,1)S(1)}) custom-call(s32[4]{0:T(128)S(1)} %pad_add_fusion.refs_0_, bf16[2048,768]{1,0:T(8,128)(2,1)} %bitcast.7, bf16[2048,768]{1,0:T(8,128)(2,1)} %bitcast.8, bf16[512,2048]{1,0:T(8,128)(2,1)} %get-tuple-element.47.refs_3_), custom_call_target="tpu_custom_call" | custom-call | flops 1610612736 | bytes 6291456 | tf_op jit(solution)/shard_map/weights/pallas_call | solution.py:49
  58.6 1.7 %collective-permute-done.14.refs_2_ = bf16[4,64,768]{2,1,0:T(8,128)(2,1)S(1)} collective-permute-done((bf16[4,64,768]{2,1,0:T(8,128)(2,1)S(1)}, bf16[4,64,768]{2,1,0:T(8,128)(2,1)S(1)}, u32[]{:S(2)}, u32[]{:S(2)}) %collective-permute-start.14) | collective-permute-done | bytes 393248 | tf_op jit(solution)/shard_map/ppermute | solution.py:364
  60.9 1.5 %collective-permute-start.15 = (bf16[208,768]{1,0:T(8,128)(2,1)S(1)}, bf16[208,768]{1,0:T(8,128)(2,1)S(1)}, u32[]{:S(2)}, u32[]{:S(2)}) collective-permute-start(bf16[208,768]{1,0:T(8,128)(2,1)S(1)} %get-tuple-element.51), channel_id=1, source_target_pairs={{0,8},{4,12},{8,0},{12,4},{16,24},{20,28},{24,16},{28,20},{1,9},{5... | collective-permute-start | bytes 958472 | tf_op jit(solution)/shard_map/ppermute | solution.py:367
  63.0 1.5 %collective-permute-start.17 = (bf16[64,768]{1,0:T(8,128)(2,1)S(1)}, bf16[64,768]{1,0:T(8,128)(2,1)S(1)}, u32[]{:S(2)}, u32[]{:S(2)}) collective-permute-start(bf16[64,768]{1,0:T(8,128)(2,1)S(1)} %get-tuple-element.53), channel_id=1, source_target_pairs={{0,24},{4,28},{8,16},{12,20},{16,8},{20,12},{24,0},{28,4},{1,25},{... | collective-permute-start | bytes 294920 | tf_op jit(solution)/shard_map/ppermute | solution.py:367
  64.5 9.1 %collective-permute-done.17.refs_5_ = bf16[64,768]{1,0:T(8,128)(2,1)S(1)} collective-permute-done((bf16[64,768]{1,0:T(8,128)(2,1)S(1)}, bf16[64,768]{1,0:T(8,128)(2,1)S(1)}, u32[]{:S(2)}, u32[]{:S(2)}) %collective-permute-start.17) | collective-permute-done | bytes 98336 | tf_op jit(solution)/shard_map/ppermute | solution.py:367
  75.2 1.4 %collective-permute-start.20 = (bf16[112,768]{1,0:T(8,128)(2,1)S(1)}, bf16[112,768]{1,0:T(8,128)(2,1)S(1)}, u32[]{:S(2)}, u32[]{:S(2)}) collective-permute-start(bf16[112,768]{1,0:T(8,128)(2,1)S(1)} %get-tuple-element.56), channel_id=1, source_target_pairs={{0,16},{4,20},{8,24},{12,28},{16,0},{20,4},{24,8},{28,12},{1,17},{... | collective-permute-start | bytes 516104 | tf_op jit(solution)/shard_map/ppermute | solution.py:367
  76.6 1.5 %collective-permute-start.21 = (bf16[112,768]{1,0:T(8,128)(2,1)S(1)}, bf16[112,768]{1,0:T(8,128)(2,1)S(1)}, u32[]{:S(2)}, u32[]{:S(2)}) collective-permute-start(bf16[112,768]{1,0:T(8,128)(2,1)S(1)} %get-tuple-element.57), channel_id=1, source_target_pairs={{0,24},{4,28},{8,16},{12,20},{16,8},{20,12},{24,0},{28,4},{1,25},{... | collective-permute-start | bytes 516104 | tf_op jit(solution)/shard_map/ppermute | solution.py:367
  78.1 3.7 %collective-permute-done.19.refs_8_.refs_2_ = bf16[112,768]{1,0:T(8,128)(2,1)S(1)} collective-permute-done((bf16[112,768]{1,0:T(8,128)(2,1)S(1)}, bf16[112,768]{1,0:T(8,128)(2,1)S(1)}, u32[]{:S(2)}, u32[]{:S(2)}) %collective-permute-start.19) | collective-permute-done | bytes 172064 | tf_op jit(solution)/shard_map/ppermute | solution.py:367
  81.7 3.6 %collective-permute-done.20.refs_9_.refs_3_ = bf16[112,768]{1,0:T(8,128)(2,1)S(1)} collective-permute-done((bf16[112,768]{1,0:T(8,128)(2,1)S(1)}, bf16[112,768]{1,0:T(8,128)(2,1)S(1)}, u32[]{:S(2)}, u32[]{:S(2)}) %collective-permute-start.20) | collective-permute-done | bytes 172064 | tf_op jit(solution)/shard_map/ppermute | solution.py:367
  85.8 1.3 %collective-permute-done.25.refs_5_ = bf16[64,768]{1,0:T(8,128)(2,1)S(1)} collective-permute-done((bf16[64,768]{1,0:T(8,128)(2,1)S(1)}, bf16[64,768]{1,0:T(8,128)(2,1)S(1)}, u32[]{:S(2)}, u32[]{:S(2)}) %collective-permute-start.25) | collective-permute-done | bytes 98336 | tf_op jit(solution)/shard_map/ppermute | solution.py:364
  87.1 2.0 %unpack.1 = (f32[768,128]{1,0:T(8,128)}, f32[768,128]{1,0:T(8,128)}, f32[768,128]{1,0:T(8,128)}, f32[128,768]{1,0:T(8,128)}) custom-call(s32[4]{0:T(128)S(1)} %pad_add_fusion.refs_0_, bf16[64,768]{1,0:T(8,128)(2,1)S(1)} %get-tuple-element.58.refs_1_, bf16[112,768]{1,0:T(8,128)(2,1)S(1)} %collective-permute-done.19.refs_8_.refs_2_, ...), custom_call_target="tpu_custom_call" | custom-call | tf_op jit(solution)/shard_map/unpack/pallas_call | solution.py:49
  89.1 0.8 gather_weights.1.refs_2_
  89.9 0.7 all-to-all-done
  90.7 4.1 %inputs.1 = bf16[4,128,768]{2,1,0:T(8,128)(2,1)} custom-call(s32[4]{0:T(128)S(1)} %pad_add_fusion.refs_0_, bf16[1536,512]{1,0:T(8,128)(2,1)} %bitcast.4.refs_1_, bf16[768,1536]{1,0:T(8,128)(2,1)S(1)} %gather_weights.1.refs_2_), custom_call_target="tpu_custom_call" | custom-call | flops 1207959552 | tf_op jit(solution)/shard_map/inputs/pallas_call | solution.py:49
  (41 shorter events, 6.4 us)
Async XLA Ops:
  7.9 2.8 %collective-permute-start = (bf16[4,128,1024]{2,1,0:T(8,128)(2,1)S(1)}, bf16[4,128,1024]{2,1,0:T(8,128)(2,1)S(1)}, u32[]{:S(2)}, u32[]{:S(2)}) collective-permute-start(bf16[4,128,1024]{2,1,0:T(8,128)(2,1)S(1)} %get-tuple-element.35), channel_id=1, source_target_pairs={{0,4},{4,0},{8,12},{12,8},{16,20},{20,16},{24,28},{28,24},{1,5},{5... | collective-permute-start | bytes 3145736 | tf_op jit(solution)/shard_map/ppermute | solution.py:364
  11.5 10.0 %collective-permute-start.1 = (bf16[128,1024]{1,0:T(8,128)(2,1)S(1)}, bf16[128,1024]{1,0:T(8,128)(2,1)S(1)}, u32[]{:S(2)}, u32[]{:S(2)}) collective-permute-start(bf16[128,1024]{1,0:T(8,128)(2,1)S(1)} %get-tuple-element.38), channel_id=1, source_target_pairs={{0,8},{4,12},{8,0},{12,4},{16,24},{20,28},{24,16},{28,20},{1,9},{5... | collective-permute-start | bytes 786440 | tf_op jit(solution)/shard_map/ppermute | solution.py:367
  14.4 13.7 %collective-permute-start.2 = (bf16[128,1024]{1,0:T(8,128)(2,1)S(1)}, bf16[128,1024]{1,0:T(8,128)(2,1)S(1)}, u32[]{:S(2)}, u32[]{:S(2)}) collective-permute-start(bf16[128,1024]{1,0:T(8,128)(2,1)S(1)} %get-tuple-element.39), channel_id=1, source_target_pairs={{0,16},{4,20},{8,24},{12,28},{16,0},{20,4},{24,8},{28,12},{1,17},{... | collective-permute-start | bytes 786440 | tf_op jit(solution)/shard_map/ppermute | solution.py:367
  15.9 12.2 %collective-permute-start.3 = (bf16[128,1024]{1,0:T(8,128)(2,1)S(1)}, bf16[128,1024]{1,0:T(8,128)(2,1)S(1)}, u32[]{:S(2)}, u32[]{:S(2)}) collective-permute-start(bf16[128,1024]{1,0:T(8,128)(2,1)S(1)} %get-tuple-element.40), channel_id=1, source_target_pairs={{0,24},{4,28},{8,16},{12,20},{16,8},{20,12},{24,0},{28,4},{1,25},{... | collective-permute-start | bytes 786440 | tf_op jit(solution)/shard_map/ppermute | solution.py:367
  16.0 4.4 %collective-permute-start.4 = (bf16[1,96,384]{2,1,0:T(8,128)(2,1)S(1)}, bf16[1,96,384]{2,1,0:T(8,128)(2,1)S(1)}, u32[]{:S(2)}, u32[]{:S(2)}) collective-permute-start(bf16[1,96,384]{2,1,0:T(8,128)(2,1)S(1)} %get-tuple-element.41.refs_1_), channel_id=1, source_target_pairs={{0,1},{1,0},{2,3},{3,2},{4,5},{5,4},{6,7},{7,6},{8,9},{9,8},{10,11... | collective-permute-start | bytes 221192 | tf_op jit(solution)/shard_map/ppermute | solution.py:370
  28.9 10.2 %collective-permute-start.7 = (bf16[128,1024]{1,0:T(8,128)(2,1)S(1)}, bf16[128,1024]{1,0:T(8,128)(2,1)S(1)}, u32[]{:S(2)}, u32[]{:S(2)}) collective-permute-start(bf16[128,1024]{1,0:T(8,128)(2,1)S(1)} %score.1.refs_1_), channel_id=1, source_target_pairs={{0,24},{4,28},{8,16},{12,20},{16,8},{20,12},{24,0},{28,4},{1,25},{... | collective-permute-start | bytes 786440 | tf_op jit(solution)/shard_map/ppermute | solution.py:367
  30.5 12.3 %collective-permute-start.6 = (bf16[128,1024]{1,0:T(8,128)(2,1)S(1)}, bf16[128,1024]{1,0:T(8,128)(2,1)S(1)}, u32[]{:S(2)}, u32[]{:S(2)}) collective-permute-start(bf16[128,1024]{1,0:T(8,128)(2,1)S(1)} %score.1.refs_1_), channel_id=1, source_target_pairs={{0,16},{4,20},{8,24},{12,28},{16,0},{20,4},{24,8},{28,12},{1,17},{... | collective-permute-start | bytes 786440 | tf_op jit(solution)/shard_map/ppermute | solution.py:367
  31.7 11.1 %collective-permute-start.5 = (bf16[128,1024]{1,0:T(8,128)(2,1)S(1)}, bf16[128,1024]{1,0:T(8,128)(2,1)S(1)}, u32[]{:S(2)}, u32[]{:S(2)}) collective-permute-start(bf16[128,1024]{1,0:T(8,128)(2,1)S(1)} %score.1.refs_1_), channel_id=1, source_target_pairs={{0,8},{4,12},{8,0},{12,4},{16,24},{20,28},{24,16},{28,20},{1,9},{5... | collective-permute-start | bytes 786440 | tf_op jit(solution)/shard_map/ppermute | solution.py:367
  32.5 10.8 %collective-permute-start.12 = (bf16[2,96,384]{2,1,0:T(8,128)(2,1)S(1)}, bf16[2,96,384]{2,1,0:T(8,128)(2,1)S(1)}, u32[]{:S(2)}, u32[]{:S(2)}) collective-permute-start(bf16[2,96,384]{2,1,0:T(8,128)(2,1)S(1)} %join.1.refs_5_), channel_id=1, source_target_pairs={{0,2},{1,3},{2,0},{3,1},{4,6},{5,7},{6,4},{7,5},{8,10},{9,11},{10,... | collective-permute-start | bytes 442376 | tf_op jit(solution)/shard_map/ppermute | solution.py:370
  35.0 10.4 %collective-permute-start.8 = (bf16[128,1024]{1,0:T(8,128)(2,1)S(1)}, bf16[128,1024]{1,0:T(8,128)(2,1)S(1)}, u32[]{:S(2)}, u32[]{:S(2)}) collective-permute-start(bf16[128,1024]{1,0:T(8,128)(2,1)S(1)} %score.1.refs_1_), channel_id=1, source_target_pairs={{0,4},{4,0},{8,12},{12,8},{16,20},{20,16},{24,28},{28,24},{1,5},{5... | collective-permute-start | bytes 786440 | tf_op jit(solution)/shard_map/ppermute | solution.py:364
  39.2 6.3 %collective-permute-start.11 = (bf16[128,1024]{1,0:T(8,128)(2,1)S(1)}, bf16[128,1024]{1,0:T(8,128)(2,1)S(1)}, u32[]{:S(2)}, u32[]{:S(2)}) collective-permute-start(bf16[128,1024]{1,0:T(8,128)(2,1)S(1)} %collective-permute-done.7.refs_4_), channel_id=1, source_target_pairs={{0,4},{4,0},{8,12},{12,8},{16,20},{20,16},{24,28},{28,24},{1,5},{5... | collective-permute-start | bytes 786440 | tf_op jit(solution)/shard_map/ppermute | solution.py:364
  42.8 2.6 %collective-permute-start.10 = (bf16[128,1024]{1,0:T(8,128)(2,1)S(1)}, bf16[128,1024]{1,0:T(8,128)(2,1)S(1)}, u32[]{:S(2)}, u32[]{:S(2)}) collective-permute-start(bf16[128,1024]{1,0:T(8,128)(2,1)S(1)} %collective-permute-done.6.refs_3_), channel_id=1, source_target_pairs={{0,4},{4,0},{8,12},{12,8},{16,20},{20,16},{24,28},{28,24},{1,5},{5... | collective-permute-start | bytes 786440 | tf_op jit(solution)/shard_map/ppermute | solution.py:364
  42.8 2.6 %collective-permute-start.9 = (bf16[128,1024]{1,0:T(8,128)(2,1)S(1)}, bf16[128,1024]{1,0:T(8,128)(2,1)S(1)}, u32[]{:S(2)}, u32[]{:S(2)}) collective-permute-start(bf16[128,1024]{1,0:T(8,128)(2,1)S(1)} %collective-permute-done.5.refs_2_), channel_id=1, source_target_pairs={{0,4},{4,0},{8,12},{12,8},{16,20},{20,16},{24,28},{28,24},{1,5},{5... | collective-permute-start | bytes 786440 | tf_op jit(solution)/shard_map/ppermute | solution.py:364
  43.9 1.5 %collective-permute-start.13 = (bf16[144,768]{1,0:T(8,128)(2,1)S(1)}, bf16[144,768]{1,0:T(8,128)(2,1)S(1)}, u32[]{:S(2)}, u32[]{:S(2)}) collective-permute-start(bf16[144,768]{1,0:T(8,128)(2,1)S(1)} %pack.1.refs_3_.refs_1_.refs_4_), channel_id=1, source_target_pairs={{0,4},{4,0},{8,12},{12,8},{16,20},{20,16},{24,28},{28,24},{1,5},{5... | collective-permute-start | bytes 663560 | tf_op jit(solution)/shard_map/ppermute | solution.py:364
  48.4 42.3 %all-to-all-start = ((bf16[4,384,512]{2,1,0:T(8,128)(2,1)}), bf16[4,384,512]{2,1,0:T(8,128)(2,1)}, u32[]{:S(2)}, u32[]{:S(2)}) async-start(bf16[4,384,512]{2,1,0:T(8,128)(2,1)} %get-tuple-element.46), calls=%async_computation | async-start | bytes 3145728 | tf_op jit(solution)/shard_map/all_to_all | solution.py:448
  58.4 30.7 %copy-start = (bf16[768,128]{1,0:T(8,128)(2,1)S(1)}, bf16[768,128]{1,0:T(8,128)(2,1)}, u32[]{:S(2)}) copy-start(bf16[768,128]{1,0:T(8,128)(2,1)} %refs_1_.3) | copy-start | bytes 589828
  58.5 30.7 %copy-start.1 = (bf16[768,128]{1,0:T(8,128)(2,1)S(1)}, bf16[768,128]{1,0:T(8,128)(2,1)}, u32[]{:S(2)}) copy-start(bf16[768,128]{1,0:T(8,128)(2,1)} %refs_2_.3) | copy-start | bytes 589828
  58.5 30.7 %copy-start.2 = (bf16[768,128]{1,0:T(8,128)(2,1)S(1)}, bf16[768,128]{1,0:T(8,128)(2,1)}, u32[]{:S(2)}) copy-start(bf16[768,128]{1,0:T(8,128)(2,1)} %refs_3_.3) | copy-start | bytes 589828
  58.5 1.8 %collective-permute-start.14 = (bf16[4,64,768]{2,1,0:T(8,128)(2,1)S(1)}, bf16[4,64,768]{2,1,0:T(8,128)(2,1)S(1)}, u32[]{:S(2)}, u32[]{:S(2)}) collective-permute-start(bf16[4,64,768]{2,1,0:T(8,128)(2,1)S(1)} %get-tuple-element.49), channel_id=1, source_target_pairs={{0,4},{4,0},{8,12},{12,8},{16,20},{20,16},{24,28},{28,24},{1,5},{5... | collective-permute-start | bytes 1179656 | tf_op jit(solution)/shard_map/ppermute | solution.py:364
  60.9 12.7 %collective-permute-start.15 = (bf16[208,768]{1,0:T(8,128)(2,1)S(1)}, bf16[208,768]{1,0:T(8,128)(2,1)S(1)}, u32[]{:S(2)}, u32[]{:S(2)}) collective-permute-start(bf16[208,768]{1,0:T(8,128)(2,1)S(1)} %get-tuple-element.51), channel_id=1, source_target_pairs={{0,8},{4,12},{8,0},{12,4},{16,24},{20,28},{24,16},{28,20},{1,9},{5... | collective-permute-start | bytes 958472 | tf_op jit(solution)/shard_map/ppermute | solution.py:367
  62.4 11.4 %collective-permute-start.16 = (bf16[208,768]{1,0:T(8,128)(2,1)S(1)}, bf16[208,768]{1,0:T(8,128)(2,1)S(1)}, u32[]{:S(2)}, u32[]{:S(2)}) collective-permute-start(bf16[208,768]{1,0:T(8,128)(2,1)S(1)} %get-tuple-element.52), channel_id=1, source_target_pairs={{0,16},{4,20},{8,24},{12,28},{16,0},{20,4},{24,8},{28,12},{1,17},{... | collective-permute-start | bytes 958472 | tf_op jit(solution)/shard_map/ppermute | solution.py:367
  63.0 10.6 %collective-permute-start.17 = (bf16[64,768]{1,0:T(8,128)(2,1)S(1)}, bf16[64,768]{1,0:T(8,128)(2,1)S(1)}, u32[]{:S(2)}, u32[]{:S(2)}) collective-permute-start(bf16[64,768]{1,0:T(8,128)(2,1)S(1)} %get-tuple-element.53), channel_id=1, source_target_pairs={{0,24},{4,28},{8,16},{12,20},{16,8},{20,12},{24,0},{28,4},{1,25},{... | collective-permute-start | bytes 294920 | tf_op jit(solution)/shard_map/ppermute | solution.py:367
  74.4 14.7 %collective-permute-start.18 = (bf16[2,144,768]{2,1,0:T(8,128)(2,1)S(1)}, bf16[2,144,768]{2,1,0:T(8,128)(2,1)S(1)}, u32[]{:S(2)}, u32[]{:S(2)}) collective-permute-start(bf16[2,144,768]{2,1,0:T(8,128)(2,1)S(1)} %get-tuple-element.54.refs_6_), channel_id=1, source_target_pairs={{0,4},{4,0},{8,12},{12,8},{16,20},{20,16},{24,28},{28,24},{1,5},{5... | collective-permute-start | bytes 1327112 | tf_op jit(solution)/shard_map/ppermute | solution.py:364
  74.5 7.2 %collective-permute-start.19 = (bf16[112,768]{1,0:T(8,128)(2,1)S(1)}, bf16[112,768]{1,0:T(8,128)(2,1)S(1)}, u32[]{:S(2)}, u32[]{:S(2)}) collective-permute-start(bf16[112,768]{1,0:T(8,128)(2,1)S(1)} %get-tuple-element.55), channel_id=1, source_target_pairs={{0,8},{4,12},{8,0},{12,4},{16,24},{20,28},{24,16},{28,20},{1,9},{5... | collective-permute-start | bytes 516104 | tf_op jit(solution)/shard_map/ppermute | solution.py:367
  75.2 10.1 %collective-permute-start.20 = (bf16[112,768]{1,0:T(8,128)(2,1)S(1)}, bf16[112,768]{1,0:T(8,128)(2,1)S(1)}, u32[]{:S(2)}, u32[]{:S(2)}) collective-permute-start(bf16[112,768]{1,0:T(8,128)(2,1)S(1)} %get-tuple-element.56), channel_id=1, source_target_pairs={{0,16},{4,20},{8,24},{12,28},{16,0},{20,4},{24,8},{28,12},{1,17},{... | collective-permute-start | bytes 516104 | tf_op jit(solution)/shard_map/ppermute | solution.py:367
  76.6 8.8 %collective-permute-start.21 = (bf16[112,768]{1,0:T(8,128)(2,1)S(1)}, bf16[112,768]{1,0:T(8,128)(2,1)S(1)}, u32[]{:S(2)}, u32[]{:S(2)}) collective-permute-start(bf16[112,768]{1,0:T(8,128)(2,1)S(1)} %get-tuple-element.57), channel_id=1, source_target_pairs={{0,24},{4,28},{8,16},{12,20},{16,8},{20,12},{24,0},{28,4},{1,25},{... | collective-permute-start | bytes 516104 | tf_op jit(solution)/shard_map/ppermute | solution.py:367
  81.7 5.4 %collective-permute-start.22 = (bf16[112,768]{1,0:T(8,128)(2,1)S(1)}, bf16[112,768]{1,0:T(8,128)(2,1)S(1)}, u32[]{:S(2)}, u32[]{:S(2)}) collective-permute-start(bf16[112,768]{1,0:T(8,128)(2,1)S(1)} %collective-permute-done.19.refs_8_.refs_2_), channel_id=1, source_target_pairs={{0,4},{4,0},{8,12},{12,8},{16,20},{20,16},{24,28},{28,24},{1,5},{5... | collective-permute-start | bytes 516104 | tf_op jit(solution)/shard_map/ppermute | solution.py:364
  85.3 1.8 %collective-permute-start.23 = (bf16[112,768]{1,0:T(8,128)(2,1)S(1)}, bf16[112,768]{1,0:T(8,128)(2,1)S(1)}, u32[]{:S(2)}, u32[]{:S(2)}) collective-permute-start(bf16[112,768]{1,0:T(8,128)(2,1)S(1)} %collective-permute-done.20.refs_9_.refs_3_), channel_id=1, source_target_pairs={{0,4},{4,0},{8,12},{12,8},{16,20},{20,16},{24,28},{28,24},{1,5},{5... | collective-permute-start | bytes 516104 | tf_op jit(solution)/shard_map/ppermute | solution.py:364
  85.3 1.8 %collective-permute-start.24 = (bf16[112,768]{1,0:T(8,128)(2,1)S(1)}, bf16[112,768]{1,0:T(8,128)(2,1)S(1)}, u32[]{:S(2)}, u32[]{:S(2)}) collective-permute-start(bf16[112,768]{1,0:T(8,128)(2,1)S(1)} %collective-permute-done.21.refs_10_.refs_4_), channel_id=1, source_target_pairs={{0,4},{4,0},{8,12},{12,8},{16,20},{20,16},{24,28},{28,24},{1,5},{5... | collective-permute-start | bytes 516104 | tf_op jit(solution)/shard_map/ppermute | solution.py:364
  85.8 1.3 %collective-permute-start.25 = (bf16[64,768]{1,0:T(8,128)(2,1)S(1)}, bf16[64,768]{1,0:T(8,128)(2,1)S(1)}, u32[]{:S(2)}, u32[]{:S(2)}) collective-permute-start(bf16[64,768]{1,0:T(8,128)(2,1)S(1)} %get-tuple-element.58.refs_1_), channel_id=1, source_target_pairs={{0,4},{4,0},{8,12},{12,8},{16,20},{20,16},{24,28},{28,24},{1,5},{5... | collective-permute-start | bytes 294920 | tf_op jit(solution)/shard_map/ppermute | solution.py:364

commit v4 on v3

--- a/solution.py
+++ b/solution.py
@@ -73,17 +73,14 @@
 
 
 def deal(chip, core, shard, keep, give, value, first=0):
-    slot = jnp.bitwise_xor(chip, shard // 2)
-
-    cols = pl.ds(first, value.shape[1])
-
-    @pl.when(core == shard % 2)
-    def _():
-        keep[slot, :, cols] = value
-
-    @pl.when(core != shard % 2)
-    def _():
-        give[slot, :, cols] = value
+    rows = keep.shape[1]
+    cols = slice(first, first + value.shape[1])
+    mine = core == 0
+    for i in range(0, value.shape[0], 2 * rows):
+        even, odd = value[i : i + rows], value[i + rows : i + 2 * rows]
+        slot = jnp.bitwise_xor(chip, (shard + i // rows) // 2)
+        keep[slot, :, cols] = jnp.where(mine, even, odd)
+        give[slot, :, cols] = jnp.where(mine, odd, even)
 
 
 def scores(chip, core, left, right, turned, keep, give, first):
@@ -92,8 +89,7 @@
     for h in range(heads):
         turned[...] = left[h].T
         total = dot_nn(turned[...], right[h]).astype(BF16)
-        for i in range(0, cols, piece_rows):
-            deal(chip, core, (h * cols + i) // piece_rows, keep, give, total[i : i + piece_rows], first)
+        deal(chip, core, h * cols // piece_rows, keep, give, total, first)
 
 
 def front_kernel(
@@ -104,8 +100,10 @@
     width = wq.shape[1]
     loads = [pltpu.make_async_copy(w, three_w.at[t], sems.at[2, t]) for t, w in enumerate((wq, wk, wv))]
     loads.append(pltpu.make_async_copy(wo, held_wo, sems.at[2, 3]))
-    in_x = [pltpu.make_async_copy(x.at[r], rows_x.at[r], sems.at[0, r]) for r in range(rows)]
-    in_og = [pltpu.make_async_copy(og.at[r], rows_og.at[r], sems.at[1, r]) for r in range(rows)]
+    span = max(1, rows // 2)
+    spans = [pl.ds(r, span) for r in range(0, rows, span)]
+    in_x = [pltpu.make_async_copy(x.at[at], rows_x.at[at], sems.at[0, i]) for i, at in enumerate(spans)]
+    in_og = [pltpu.make_async_copy(og, rows_og, sems.at[1, 0])]
     for copy in loads + in_x + in_og:
         copy.start()
     for copy in loads:
@@ -116,7 +114,8 @@
         both[t * width : (t + 1) * width, :] = three_w[t].T
         slab[0, :, t * width : (t + 1) * width] = three_w[t, at, :]
     for r in range(rows):
-        in_x[r].wait()
+        if r % span == 0:
+            in_x[r // span].wait()
         three = dot_nt(both[...], rows_x[r]).astype(BF16)
         at = slice(r * HEAD_DIM, (r + 1) * HEAD_DIM)
         for t, out in enumerate((qt, kt, vt)):
@@ -124,8 +123,8 @@
                 first = t * width + h * HEAD_DIM
                 out[h, at, :] = three[first : first + HEAD_DIM]
     scores(place[0], place[1], qt, kt, turned, keep, give, 0)
+    in_og[0].wait()
     for r in range(rows):
-        in_og[r].wait()
         grad = dot_nt(held_wo[...], rows_og[r]).astype(BF16)
         at = slice(r * HEAD_DIM, (r + 1) * HEAD_DIM)
         for h in range(width // HEAD_DIM):
@@ -245,10 +244,7 @@
             if i < steps - 1:
                 total[first:last, :] = part
             else:
-                value = part.astype(BF16)
-                for j in range(first, last, piece_rows):
-                    piece = value[j - first : j - first + piece_rows]
-                    deal(place[0], place[1], j // piece_rows, keep, give, piece)
+                deal(place[0], place[1], first // piece_rows, keep, give, part.astype(BF16))
 
 
 def pair_append_kernel(place, keep, got, packed, *outs):
@@ -287,17 +283,14 @@
     outs[-1][...] = full[(len(outs) - 1) * width :, :]
 
 
-def gather_weights_kernel(zeds, place, wq, wk, wv, own, own_other, near, near_other, *refs):
+def gather_weights_kernel(zeds, place, own, own_other, near, near_other, *refs):
     *far, full = refs
-    model, width = wq.shape
-    wide = 3 * width
+    model = full.shape[0]
+    wide = full.shape[1] // (zeds - 1)
     extra = own.shape[0]
     folds = model // wide
     rows = extra // (zeds - 1)
     depth = rows * folds
-    zed = place[2]
-    for t, w in enumerate((wq, wk, wv)):
-        full[:, pl.ds(pl.multiple_of((3 * zed + t) * width, width), width)] = w[...]
     cut = extra // 3 // 16 * 16
     skip = far[0].shape[0] - cut
 
@@ -316,25 +309,34 @@
         for side, core in ((0, place[1]), (1, 1 - place[1])):
             for first in range(0, extra, unit):
                 z, offset = 1 + first // rows, first % rows
-                cols = pl.ds(pl.multiple_of(jnp.bitwise_xor(zed, z) * wide, width), wide)
+                cols = slice((z - 1) * wide, z * wide)
                 value = part(side, k, first, unit)
                 for i in range(folds):
                     row = pl.multiple_of((base + core) * depth + i * rows + offset, unit)
                     full[pl.ds(row, unit), cols] = value[:, i * wide : (i + 1) * wide]
 
 
-def inputs_kernel(place, sent_far, full, out, sent, total, sems):
+def own_inputs_kernel(place, send_far, wq, wk, wv, total, send, full, sems):
+    width = wq.shape[1]
+    pairs = [(w, full.at[:, t * width : (t + 1) * width]) for t, w in enumerate((wq, wk, wv))]
+    for copy in fetch([(send_far.at[place[2]], send)] + pairs, sems):
+        copy.wait()
+    total[...] = dot_nn(full[...], send[...])
+
+
+def inputs_kernel(place, sent_far, own_part, full, out, sent, sems):
     rows, block, _ = out.shape
-    deep = sent.shape[0] // 2
-    halves = (slice(0, deep), slice(deep, 2 * deep))
-    copies = fetch([(sent_far.at[half], sent.at[half]) for half in halves], sems)
-    copies[0].wait()
-    total[...] = dot_nn(full[:, halves[0]], sent[halves[0], :])
-    copies[1].wait()
+    zeds, depth, _ = sent_far.shape
+    pairs = []
+    for k in range(1, zeds):
+        far = sent_far.at[jnp.bitwise_xor(place[2], k)]
+        pairs.append((far, sent.at[(k - 1) * depth : k * depth]))
+    for copy in fetch(pairs, sems):
+        copy.wait()
     step = min(2, rows)
     for r in range(0, rows, step):
         span = slice(r * block, (r + step) * block)
-        value = total[:, span] + dot_nn(full[:, halves[1]], sent[halves[1], span])
+        value = own_part[:, span] + dot_nn(full[...], sent[:, span])
         value = value.astype(BF16).T
         for i in range(step):
             out[r + i] = value[i * block : (i + 1) * block]
@@ -422,10 +424,7 @@
         held=(slab,),
         name="score",
     )
-    packed = call(
-        pack_kernel, shape((zeds - 1) * depth // folds, model), (place, *groups[1:]), name="pack"
-    )
-    packed_other = swap(packed)
+    swapped = [swap(group) for group in groups[1:]]
     mine, other = gathered(scored, pieces)
     send, four = call(
         partial(grads_kernel, pieces),
@@ -434,7 +433,7 @@
             pltpu.HBM((4 * width, rows * cols), BF16),
         ),
         (place, *mine, *other, qt, kt, vt, gt),
-        held=(packed_other,),
+        held=swapped[1:] or swapped,
         out_specs=(hbm_spec(), hbm_spec()),
         scratch=[
             pltpu.VMEM((heads * cols, 2 * cols), BF16),
@@ -444,6 +443,19 @@
         ],
         flops=4 * score_flops,
         name="grads",
+    )
+    own_part = call(
+        own_inputs_kernel,
+        shape(model, rows * block, dtype=F32),
+        (place, send, w_query, w_key, w_value),
+        hbm=4,
+        scratch=[
+            pltpu.VMEM((3 * width, rows * block), BF16),
+            pltpu.VMEM((model, 3 * width), BF16),
+            pltpu.SemaphoreType.DMA((4,)),
+        ],
+        flops=3 * dot_flops // zeds,
+        name="own_inputs",
     )
     sent = lax.all_to_all(send, "head", 0, 0, tiled=True)
 
@@ -463,6 +475,10 @@
         moved=inputs.size * 4,
         name="weights",
     )
+    packed, packed_other = [
+        call(pack_kernel, shape((zeds - 1) * depth // folds, model), (place, *parts), name="pack")
+        for parts in (groups[1:], swapped)
+    ]
     extra = packed.shape[0]
     cut = extra // 48 * 16
     near = (1, 2)
@@ -483,6 +499,7 @@
             shape(2, extra, model),
         ),
         (place, packed, *parts),
+        held=(own_part,),
         name="sum_weights",
     )
     sums = [total_w, first, second, third] + [total_w] * (pieces - 4)
@@ -490,8 +507,8 @@
     other = [swap(part) for part in mine]
     full = call(
         partial(gather_weights_kernel, zeds),
-        shape(model, zeds * 3 * width),
-        (place, w_query, w_key, w_value, packed, packed_other, slabs, swap(slabs))
+        shape(model, (zeds - 1) * 3 * width),
+        (place, packed, packed_other, slabs, swap(slabs))
         + (*mine[1:4], *other[1:4]),
         name="gather_weights",
     )
@@ -505,14 +522,13 @@
     grad_inputs = call(
         inputs_kernel,
         shape(rows, block, model),
-        (place, sent.reshape(-1, rows * block), full),
+        (place, sent, own_part, full),
         hbm=1,
         scratch=[
-            pltpu.VMEM((zeds * 3 * width, rows * block), BF16),
-            pltpu.VMEM((model, rows * block), F32),
-            pltpu.SemaphoreType.DMA((2,)),
+            pltpu.VMEM(((zeds - 1) * 3 * width, rows * block), BF16),
+            pltpu.SemaphoreType.DMA((zeds - 1,)),
         ],
-        flops=3 * dot_flops,
+        flops=3 * dot_flops * (zeds - 1) // zeds,
         name="inputs",
     )
     return (grad_inputs, grad_q, grad_k, grad_v, grad_o)

time: 95 us -> 93.5 us (0.984)
  waiting for transfers between devices: 41.4 us -> 38.8 us
  Pallas kernels: 26 us -> 27.1 us
    ppermute x12, waiting for transfers between devices: 31.6 us -> 29.5 us  [across(): return lax.ppermute(value, 'seq', [(i, i ^ 2 * k) for i in range(seqs)])]
    ppermute x12 -> x13, waiting for transfers between devices: 6.78 us -> 5.65 us  [swap(): return lax.ppermute(value, 'seq', [(i, i ^ 1) for i in range(seqs)])]
    pallas_call x12 -> x14, Pallas kernels: 26 us -> 27.1 us  [call(): pl.pallas_call(run, out_shape=outs, in_specs=[smem_spec()] + [hbm_spec()]...]
  transfers between devices with their start and end apart: 27 -> 28, of which waited for: 14 -> 14; matrix products, arithmetic and copies ran while one was open for 0% -> 0% of each run, Pallas kernels for 11% -> 14%
where the time goes in v4:
time: 93.5 us; the launch traced here: 93.2 us
  waiting for transfers between devices  38.8 us (41%)
  Pallas kernels  27.1 us (29%)
  starting transfers between devices  26.5 us (28%)
    ppermute x12, waiting for transfers between devices, across(): return lax.ppermute(value, 'seq', [(i, i ^ 2 * k) for i in range(seqs)])  29.5 us
    pallas_call x14, Pallas kernels, call(): pl.pallas_call(run, out_shape=outs, in_specs=[smem_spec()] + [hbm_spec()]...  27.1 us
    ppermute x12, starting transfers between devices, across(): return lax.ppermute(value, 'seq', [(i, i ^ 2 * k) for i in range(seqs)])  15.1 us
    ppermute x13, waiting for transfers between devices, swap(): return lax.ppermute(value, 'seq', [(i, i ^ 1) for i in range(seqs)])  5.65 us
    all_to_all x1, starting transfers between devices, body(): sent = lax.all_to_all(send, 'head', 0, 0, tiled=True)  4.88 us
    ppermute x2, starting transfers between devices, along(): return lax.ppermute(value, 'head', [(i, i ^ k) for i in range(zeds)])  4.63 us
    ppermute x2, waiting for transfers between devices, along(): return lax.ppermute(value, 'head', [(i, i ^ k) for i in range(zeds)])  2.33 us
  transfers between devices with their start and end apart: 28, of which 14 were waited for; matrix products, arithmetic and copies ran while one was open for 0% of the time, Pallas kernels for 14%

profile of v4, /device:TPU:0, one launch (start us, length us, event | category | flops | bytes accessed | tf_op | source)
XLA Modules:
  0.0 93.2 jit_solution(15584331053449847548)
XLA Ops:
  0.7 6.0 %front.1 = (bf16[2,256,512]{2,1,0:T(8,128)(2,1)S(1)}, bf16[2,256,512]{2,1,0:T(8,128)(2,1)S(1)}, bf16[2,256,512]{2,1,0:T(8,128)(2,1)S(1)}, bf16[2,256,512]{2,1,0:...) custom-call(s32[4]{0:T(128)S(1)} %pad_add_fusion.refs_0_, ...), custom_call_target="tpu_custom_call" | custom-call | flops 2147483648 | tf_op jit(solution)/shard_map/front/pallas_call | solution.py:49
  7.2 2.3 %collective-permute-done.refs_2_ = bf16[4,128,1024]{2,1,0:T(8,128)(2,1)S(1)} collective-permute-done((bf16[4,128,1024]{2,1,0:T(8,128)(2,1)S(1)}, bf16[4,128,1024]{2,1,0:T(8,128)(2,1)S(1)}, u32[]{:S(2)}, u32[]{:S(2)}) %collective-permute-start) | collective-permute-done | bytes 1048608 | tf_op jit(solution)/shard_map/ppermute | solution.py:366
  9.5 0.8 pair_scores.1
  10.3 2.9 %collective-permute-start.1 = (bf16[128,1024]{1,0:T(8,128)(2,1)S(1)}, bf16[128,1024]{1,0:T(8,128)(2,1)S(1)}, u32[]{:S(2)}, u32[]{:S(2)}) collective-permute-start(bf16[128,1024]{1,0:T(8,128)(2,1)S(1)} %get-tuple-element.38), channel_id=1, source_target_pairs={{0,8},{4,12},{8,0},{12,4},{16,24},{20,28},{24,16},{28,20},{1,9},{5... | collective-permute-start | bytes 786440 | tf_op jit(solution)/shard_map/ppermute | solution.py:369
  13.2 1.5 %collective-permute-start.2 = (bf16[128,1024]{1,0:T(8,128)(2,1)S(1)}, bf16[128,1024]{1,0:T(8,128)(2,1)S(1)}, u32[]{:S(2)}, u32[]{:S(2)}) collective-permute-start(bf16[128,1024]{1,0:T(8,128)(2,1)S(1)} %get-tuple-element.39), channel_id=1, source_target_pairs={{0,16},{4,20},{8,24},{12,28},{16,0},{20,4},{24,8},{28,12},{1,17},{... | collective-permute-start | bytes 786440 | tf_op jit(solution)/shard_map/ppermute | solution.py:369
  14.8 2.0 %collective-permute-start.4 = (bf16[1,96,384]{2,1,0:T(8,128)(2,1)S(1)}, bf16[1,96,384]{2,1,0:T(8,128)(2,1)S(1)}, u32[]{:S(2)}, u32[]{:S(2)}) collective-permute-start(bf16[1,96,384]{2,1,0:T(8,128)(2,1)S(1)} %get-tuple-element.41.refs_1_), channel_id=1, source_target_pairs={{0,1},{1,0},{2,3},{3,2},{4,5},{5,4},{6,7},{7,6},{8,9},{9,8},{10,11... | collective-permute-start | bytes 221192 | tf_op jit(solution)/shard_map/ppermute | solution.py:372
  16.8 2.3 %collective-permute-done.4.refs_2_.refs_1_ = bf16[1,96,384]{2,1,0:T(8,128)(2,1)S(1)} collective-permute-done((bf16[1,96,384]{2,1,0:T(8,128)(2,1)S(1)}, bf16[1,96,384]{2,1,0:T(8,128)(2,1)S(1)}, u32[]{:S(2)}, u32[]{:S(2)}) %collective-permute-start.4) | collective-permute-done | bytes 73760 | tf_op jit(solution)/shard_map/ppermute | solution.py:372
  20.3 6.6 %collective-permute-done.2.refs_3_ = bf16[128,1024]{1,0:T(8,128)(2,1)S(1)} collective-permute-done((bf16[128,1024]{1,0:T(8,128)(2,1)S(1)}, bf16[128,1024]{1,0:T(8,128)(2,1)S(1)}, u32[]{:S(2)}, u32[]{:S(2)}) %collective-permute-start.2) | collective-permute-done | bytes 262176 | tf_op jit(solution)/shard_map/ppermute | solution.py:369
  26.9 0.8 score.1.refs_1_
  27.7 1.3 %collective-permute-start.5 = (bf16[128,1024]{1,0:T(8,128)(2,1)S(1)}, bf16[128,1024]{1,0:T(8,128)(2,1)S(1)}, u32[]{:S(2)}, u32[]{:S(2)}) collective-permute-start(bf16[128,1024]{1,0:T(8,128)(2,1)S(1)} %score.1.refs_1_), channel_id=1, source_target_pairs={{0,8},{4,12},{8,0},{12,4},{16,24},{20,28},{24,16},{28,20},{1,9},{5... | collective-permute-start | bytes 786440 | tf_op jit(solution)/shard_map/ppermute | solution.py:369
  29.0 0.8 collective-permute-start.6
  29.9 1.4 %collective-permute-start.7 = (bf16[128,1024]{1,0:T(8,128)(2,1)S(1)}, bf16[128,1024]{1,0:T(8,128)(2,1)S(1)}, u32[]{:S(2)}, u32[]{:S(2)}) collective-permute-start(bf16[128,1024]{1,0:T(8,128)(2,1)S(1)} %score.1.refs_1_), channel_id=1, source_target_pairs={{0,24},{4,28},{8,16},{12,20},{16,8},{20,12},{24,0},{28,4},{1,25},{... | collective-permute-start | bytes 786440 | tf_op jit(solution)/shard_map/ppermute | solution.py:369
  31.3 2.6 %collective-permute-start.12 = (bf16[2,96,384]{2,1,0:T(8,128)(2,1)S(1)}, bf16[2,96,384]{2,1,0:T(8,128)(2,1)S(1)}, u32[]{:S(2)}, u32[]{:S(2)}) collective-permute-start(bf16[2,96,384]{2,1,0:T(8,128)(2,1)S(1)} %join.1.refs_5_), channel_id=1, source_target_pairs={{0,2},{1,3},{2,0},{3,1},{4,6},{5,7},{6,4},{7,5},{8,10},{9,11},{10,... | collective-permute-start | bytes 442376 | tf_op jit(solution)/shard_map/ppermute | solution.py:372
  33.9 3.2 %collective-permute-done.5.refs_2_ = bf16[128,1024]{1,0:T(8,128)(2,1)S(1)} collective-permute-done((bf16[128,1024]{1,0:T(8,128)(2,1)S(1)}, bf16[128,1024]{1,0:T(8,128)(2,1)S(1)}, u32[]{:S(2)}, u32[]{:S(2)}) %collective-permute-start.5) | collective-permute-done | bytes 262176 | tf_op jit(solution)/shard_map/ppermute | solution.py:369
  37.1 4.8 %collective-permute-done.6.refs_3_ = bf16[128,1024]{1,0:T(8,128)(2,1)S(1)} collective-permute-done((bf16[128,1024]{1,0:T(8,128)(2,1)S(1)}, bf16[128,1024]{1,0:T(8,128)(2,1)S(1)}, u32[]{:S(2)}, u32[]{:S(2)}) %collective-permute-start.6) | collective-permute-done | bytes 262176 | tf_op jit(solution)/shard_map/ppermute | solution.py:369
  42.5 1.5 %collective-permute-done.13.refs_13_.refs_2_ = bf16[2,96,384]{2,1,0:T(8,128)(2,1)S(1)} collective-permute-done((bf16[2,96,384]{2,1,0:T(8,128)(2,1)S(1)}, bf16[2,96,384]{2,1,0:T(8,128)(2,1)S(1)}, u32[]{:S(2)}, u32[]{:S(2)}) %collective-permute-start.13) | collective-permute-done | bytes 147488 | tf_op jit(solution)/shard_map/ppermute | solution.py:366
  44.0 3.0 %grads.1 = (bf16[4,384,512]{2,1,0:T(8,128)(2,1)}, bf16[512,2048]{1,0:T(8,128)(2,1)}) custom-call(s32[4]{0:T(128)S(1)} %pad_add_fusion.refs_0_, bf16[128,1024]{1,0:T(8,128)(2,1)S(1)} %score.1.refs_1_, bf16[128,1024]{1,0:T(8,128)(2,1)S(1)} %collective-permute-done.5.refs_2_, bf16[128,1024]{1,0:T(8,128)(2,1)S(1)} %collective-permute-done.6.refs_3_, ...), custom_call_target="tpu_custom_call" | custom-call | flops 1073741824 | tf_op jit(solution)/shard_map/grads/pallas_call | solution.py:49
  47.0 4.9 %all-to-all-start = ((bf16[4,384,512]{2,1,0:T(8,128)(2,1)}), bf16[4,384,512]{2,1,0:T(8,128)(2,1)}, u32[]{:S(2)}, u32[]{:S(2)}) async-start(bf16[4,384,512]{2,1,0:T(8,128)(2,1)} %get-tuple-element.46.refs_1_), calls=%async_computation | async-start | bytes 3145728 | tf_op jit(solution)/shard_map/all_to_all | solution.py:460
  51.9 4.6 %weights.1 = (bf16[4,64,768]{2,1,0:T(8,128)(2,1)S(1)}, bf16[4,64,768]{2,1,0:T(8,128)(2,1)S(1)}) custom-call(s32[4]{0:T(128)S(1)} %pad_add_fusion.refs_0_, bf16[2048,768]{1,0:T(8,128)(2,1)} %bitcast.6, bf16[2048,768]{1,0:T(8,128)(2,1)} %bitcast.7, bf16[512,2048]{1,0:T(8,128)(2,1)} %get-tuple-element.47.refs_3_), custom_call_target="tpu_custom_call" | custom-call | flops 1610612736 | bytes 6291456 | tf_op jit(solution)/shard_map/weights/pallas_call | solution.py:49
  57.2 1.1 %collective-permute-done.15.refs_2_ = bf16[4,64,768]{2,1,0:T(8,128)(2,1)S(1)} collective-permute-done((bf16[4,64,768]{2,1,0:T(8,128)(2,1)S(1)}, bf16[4,64,768]{2,1,0:T(8,128)(2,1)S(1)}, u32[]{:S(2)}, u32[]{:S(2)}) %collective-permute-start.15) | collective-permute-done | bytes 393248 | tf_op jit(solution)/shard_map/ppermute | solution.py:366
  59.7 1.4 %collective-permute-start.17 = (bf16[208,768]{1,0:T(8,128)(2,1)S(1)}, bf16[208,768]{1,0:T(8,128)(2,1)S(1)}, u32[]{:S(2)}, u32[]{:S(2)}) collective-permute-start(bf16[208,768]{1,0:T(8,128)(2,1)S(1)} %get-tuple-element.52), channel_id=1, source_target_pairs={{0,16},{4,20},{8,24},{12,28},{16,0},{20,4},{24,8},{28,12},{1,17},{... | collective-permute-start | bytes 958472 | tf_op jit(solution)/shard_map/ppermute | solution.py:369
  61.1 1.5 %collective-permute-start.18 = (bf16[64,768]{1,0:T(8,128)(2,1)S(1)}, bf16[64,768]{1,0:T(8,128)(2,1)S(1)}, u32[]{:S(2)}, u32[]{:S(2)}) collective-permute-start(bf16[64,768]{1,0:T(8,128)(2,1)S(1)} %get-tuple-element.53), channel_id=1, source_target_pairs={{0,24},{4,28},{8,16},{12,20},{16,8},{20,12},{24,0},{28,4},{1,25},{... | collective-permute-start | bytes 294920 | tf_op jit(solution)/shard_map/ppermute | solution.py:369
  62.6 2.3 %own_inputs.1.refs_6_.refs_2_ = f32[768,512]{1,0:T(8,128)S(1)} custom-call(s32[4]{0:T(128)S(1)} %pad_add_fusion.refs_0_, bf16[4,384,512]{2,1,0:T(8,128)(2,1)} %get-tuple-element.46.refs_1_, bf16[768,128]{1,0:T(8,128)(2,1)} %refs_2_.3, bf16[768,128]{1,0:T(8,128)(2,1)} %refs_3_.3, bf16[768,128]{1,0:T(8,128)(2,1)} %refs_4_.3), custom_call_target="tpu_custom_call" | custom-call | flops 301989888 | tf_op jit(solution)/shard_map/own_inputs/pallas_call | solution.py:49
  64.9 5.9 %collective-permute-done.18.refs_5_ = bf16[64,768]{1,0:T(8,128)(2,1)S(1)} collective-permute-done((bf16[64,768]{1,0:T(8,128)(2,1)S(1)}, bf16[64,768]{1,0:T(8,128)(2,1)S(1)}, u32[]{:S(2)}, u32[]{:S(2)}) %collective-permute-start.18) | collective-permute-done | bytes 98336 | tf_op jit(solution)/shard_map/ppermute | solution.py:369
  71.8 1.5 %collective-permute-start.20 = (bf16[112,768]{1,0:T(8,128)(2,1)S(1)}, bf16[112,768]{1,0:T(8,128)(2,1)S(1)}, u32[]{:S(2)}, u32[]{:S(2)}) collective-permute-start(bf16[112,768]{1,0:T(8,128)(2,1)S(1)} %get-tuple-element.55), channel_id=1, source_target_pairs={{0,8},{4,12},{8,0},{12,4},{16,24},{20,28},{24,16},{28,20},{1,9},{5... | collective-permute-start | bytes 516104 | tf_op jit(solution)/shard_map/ppermute | solution.py:369
  73.8 1.5 %collective-permute-start.22 = (bf16[112,768]{1,0:T(8,128)(2,1)S(1)}, bf16[112,768]{1,0:T(8,128)(2,1)S(1)}, u32[]{:S(2)}, u32[]{:S(2)}) collective-permute-start(bf16[112,768]{1,0:T(8,128)(2,1)S(1)} %get-tuple-element.57), channel_id=1, source_target_pairs={{0,24},{4,28},{8,16},{12,20},{16,8},{20,12},{24,0},{28,4},{1,25},{... | collective-permute-start | bytes 516104 | tf_op jit(solution)/shard_map/ppermute | solution.py:369
  75.3 3.7 %collective-permute-done.20.refs_5_.refs_2_ = bf16[112,768]{1,0:T(8,128)(2,1)S(1)} collective-permute-done((bf16[112,768]{1,0:T(8,128)(2,1)S(1)}, bf16[112,768]{1,0:T(8,128)(2,1)S(1)}, u32[]{:S(2)}, u32[]{:S(2)}) %collective-permute-start.20) | collective-permute-done | bytes 172064 | tf_op jit(solution)/shard_map/ppermute | solution.py:369
  79.0 4.4 %collective-permute-done.21.refs_6_.refs_3_ = bf16[112,768]{1,0:T(8,128)(2,1)S(1)} collective-permute-done((bf16[112,768]{1,0:T(8,128)(2,1)S(1)}, bf16[112,768]{1,0:T(8,128)(2,1)S(1)}, u32[]{:S(2)}, u32[]{:S(2)}) %collective-permute-start.21) | collective-permute-done | bytes 172064 | tf_op jit(solution)/shard_map/ppermute | solution.py:369
  85.2 2.0 %unpack.1 = (f32[768,128]{1,0:T(8,128)}, f32[768,128]{1,0:T(8,128)}, f32[768,128]{1,0:T(8,128)}, f32[128,768]{1,0:T(8,128)}) custom-call(s32[4]{0:T(128)S(1)} %pad_add_fusion.refs_0_, bf16[64,768]{1,0:T(8,128)(2,1)S(1)} %get-tuple-element.58.refs_1_, bf16[112,768]{1,0:T(8,128)(2,1)S(1)} %collective-permute-done.20.refs_5_.refs_2_, ...), custom_call_target="tpu_custom_call" | custom-call | tf_op jit(solution)/shard_map/unpack/pallas_call | solution.py:49
  87.2 0.7 gather_weights.1.refs_3_
  87.9 1.4 %all-to-all-done.refs_1_ = bf16[4,384,512]{2,1,0:T(8,128)(2,1)} async-done(((bf16[4,384,512]{2,1,0:T(8,128)(2,1)}), bf16[4,384,512]{2,1,0:T(8,128)(2,1)}, u32[]{:S(2)}, u32[]{:S(2)}) %all-to-all-start) | async-done | bytes 1572896 | tf_op jit(solution)/shard_map/all_to_all | solution.py:460
  89.3 3.9 %inputs.1 = bf16[4,128,768]{2,1,0:T(8,128)(2,1)} custom-call(s32[4]{0:T(128)S(1)} %pad_add_fusion.refs_0_, bf16[4,384,512]{2,1,0:T(8,128)(2,1)} %all-to-all-done.refs_1_, f32[768,512]{1,0:T(8,128)S(1)} %own_inputs.1.refs_6_.refs_2_, bf16[768,1152]{1,0:T(8,128)(2,1)S(1)} %gather_weights.1.refs_3_), custom_call_target="tpu_custom_call" | custom-call | flops 905969664 | tf_op jit(solution)/shard_map/inputs/pallas_call | solution.py:49
  (39 shorter events, 7.6 us)
Async XLA Ops:
  6.7 2.8 %collective-permute-start = (bf16[4,128,1024]{2,1,0:T(8,128)(2,1)S(1)}, bf16[4,128,1024]{2,1,0:T(8,128)(2,1)S(1)}, u32[]{:S(2)}, u32[]{:S(2)}) collective-permute-start(bf16[4,128,1024]{2,1,0:T(8,128)(2,1)S(1)} %get-tuple-element.35), channel_id=1, source_target_pairs={{0,4},{4,0},{8,12},{12,8},{16,20},{20,16},{24,28},{28,24},{1,5},{5... | collective-permute-start | bytes 3145736 | tf_op jit(solution)/shard_map/ppermute | solution.py:366
  10.3 10.0 %collective-permute-start.1 = (bf16[128,1024]{1,0:T(8,128)(2,1)S(1)}, bf16[128,1024]{1,0:T(8,128)(2,1)S(1)}, u32[]{:S(2)}, u32[]{:S(2)}) collective-permute-start(bf16[128,1024]{1,0:T(8,128)(2,1)S(1)} %get-tuple-element.38), channel_id=1, source_target_pairs={{0,8},{4,12},{8,0},{12,4},{16,24},{20,28},{24,16},{28,20},{1,9},{5... | collective-permute-start | bytes 786440 | tf_op jit(solution)/shard_map/ppermute | solution.py:369
  13.2 13.7 %collective-permute-start.2 = (bf16[128,1024]{1,0:T(8,128)(2,1)S(1)}, bf16[128,1024]{1,0:T(8,128)(2,1)S(1)}, u32[]{:S(2)}, u32[]{:S(2)}) collective-permute-start(bf16[128,1024]{1,0:T(8,128)(2,1)S(1)} %get-tuple-element.39), channel_id=1, source_target_pairs={{0,16},{4,20},{8,24},{12,28},{16,0},{20,4},{24,8},{28,12},{1,17},{... | collective-permute-start | bytes 786440 | tf_op jit(solution)/shard_map/ppermute | solution.py:369
  14.8 12.2 %collective-permute-start.3 = (bf16[128,1024]{1,0:T(8,128)(2,1)S(1)}, bf16[128,1024]{1,0:T(8,128)(2,1)S(1)}, u32[]{:S(2)}, u32[]{:S(2)}) collective-permute-start(bf16[128,1024]{1,0:T(8,128)(2,1)S(1)} %get-tuple-element.40), channel_id=1, source_target_pairs={{0,24},{4,28},{8,16},{12,20},{16,8},{20,12},{24,0},{28,4},{1,25},{... | collective-permute-start | bytes 786440 | tf_op jit(solution)/shard_map/ppermute | solution.py:369
  14.8 4.4 %collective-permute-start.4 = (bf16[1,96,384]{2,1,0:T(8,128)(2,1)S(1)}, bf16[1,96,384]{2,1,0:T(8,128)(2,1)S(1)}, u32[]{:S(2)}, u32[]{:S(2)}) collective-permute-start(bf16[1,96,384]{2,1,0:T(8,128)(2,1)S(1)} %get-tuple-element.41.refs_1_), channel_id=1, source_target_pairs={{0,1},{1,0},{2,3},{3,2},{4,5},{5,4},{6,7},{7,6},{8,9},{9,8},{10,11... | collective-permute-start | bytes 221192 | tf_op jit(solution)/shard_map/ppermute | solution.py:372
  27.7 9.3 %collective-permute-start.5 = (bf16[128,1024]{1,0:T(8,128)(2,1)S(1)}, bf16[128,1024]{1,0:T(8,128)(2,1)S(1)}, u32[]{:S(2)}, u32[]{:S(2)}) collective-permute-start(bf16[128,1024]{1,0:T(8,128)(2,1)S(1)} %score.1.refs_1_), channel_id=1, source_target_pairs={{0,8},{4,12},{8,0},{12,4},{16,24},{20,28},{24,16},{28,20},{1,9},{5... | collective-permute-start | bytes 786440 | tf_op jit(solution)/shard_map/ppermute | solution.py:369
  29.0 12.9 %collective-permute-start.6 = (bf16[128,1024]{1,0:T(8,128)(2,1)S(1)}, bf16[128,1024]{1,0:T(8,128)(2,1)S(1)}, u32[]{:S(2)}, u32[]{:S(2)}) collective-permute-start(bf16[128,1024]{1,0:T(8,128)(2,1)S(1)} %score.1.refs_1_), channel_id=1, source_target_pairs={{0,16},{4,20},{8,24},{12,28},{16,0},{20,4},{24,8},{28,12},{1,17},{... | collective-permute-start | bytes 786440 | tf_op jit(solution)/shard_map/ppermute | solution.py:369
  29.9 12.0 %collective-permute-start.7 = (bf16[128,1024]{1,0:T(8,128)(2,1)S(1)}, bf16[128,1024]{1,0:T(8,128)(2,1)S(1)}, u32[]{:S(2)}, u32[]{:S(2)}) collective-permute-start(bf16[128,1024]{1,0:T(8,128)(2,1)S(1)} %score.1.refs_1_), channel_id=1, source_target_pairs={{0,24},{4,28},{8,16},{12,20},{16,8},{20,12},{24,0},{28,4},{1,25},{... | collective-permute-start | bytes 786440 | tf_op jit(solution)/shard_map/ppermute | solution.py:369
  31.3 11.1 %collective-permute-start.12 = (bf16[2,96,384]{2,1,0:T(8,128)(2,1)S(1)}, bf16[2,96,384]{2,1,0:T(8,128)(2,1)S(1)}, u32[]{:S(2)}, u32[]{:S(2)}) collective-permute-start(bf16[2,96,384]{2,1,0:T(8,128)(2,1)S(1)} %join.1.refs_5_), channel_id=1, source_target_pairs={{0,2},{1,3},{2,0},{3,1},{4,6},{5,7},{6,4},{7,5},{8,10},{9,11},{10,... | collective-permute-start | bytes 442376 | tf_op jit(solution)/shard_map/ppermute | solution.py:372
  33.9 10.1 %collective-permute-start.8 = (bf16[128,1024]{1,0:T(8,128)(2,1)S(1)}, bf16[128,1024]{1,0:T(8,128)(2,1)S(1)}, u32[]{:S(2)}, u32[]{:S(2)}) collective-permute-start(bf16[128,1024]{1,0:T(8,128)(2,1)S(1)} %score.1.refs_1_), channel_id=1, source_target_pairs={{0,4},{4,0},{8,12},{12,8},{16,20},{20,16},{24,28},{28,24},{1,5},{5... | collective-permute-start | bytes 786440 | tf_op jit(solution)/shard_map/ppermute | solution.py:366
  37.0 7.0 %collective-permute-start.9 = (bf16[128,1024]{1,0:T(8,128)(2,1)S(1)}, bf16[128,1024]{1,0:T(8,128)(2,1)S(1)}, u32[]{:S(2)}, u32[]{:S(2)}) collective-permute-start(bf16[128,1024]{1,0:T(8,128)(2,1)S(1)} %collective-permute-done.5.refs_2_), channel_id=1, source_target_pairs={{0,4},{4,0},{8,12},{12,8},{16,20},{20,16},{24,28},{28,24},{1,5},{5... | collective-permute-start | bytes 786440 | tf_op jit(solution)/shard_map/ppermute | solution.py:366
  41.9 2.1 %collective-permute-start.10 = (bf16[128,1024]{1,0:T(8,128)(2,1)S(1)}, bf16[128,1024]{1,0:T(8,128)(2,1)S(1)}, u32[]{:S(2)}, u32[]{:S(2)}) collective-permute-start(bf16[128,1024]{1,0:T(8,128)(2,1)S(1)} %collective-permute-done.6.refs_3_), channel_id=1, source_target_pairs={{0,4},{4,0},{8,12},{12,8},{16,20},{20,16},{24,28},{28,24},{1,5},{5... | collective-permute-start | bytes 786440 | tf_op jit(solution)/shard_map/ppermute | solution.py:366
  41.9 2.1 %collective-permute-start.11 = (bf16[128,1024]{1,0:T(8,128)(2,1)S(1)}, bf16[128,1024]{1,0:T(8,128)(2,1)S(1)}, u32[]{:S(2)}, u32[]{:S(2)}) collective-permute-start(bf16[128,1024]{1,0:T(8,128)(2,1)S(1)} %collective-permute-done.7.refs_4_), channel_id=1, source_target_pairs={{0,4},{4,0},{8,12},{12,8},{16,20},{20,16},{24,28},{28,24},{1,5},{5... | collective-permute-start | bytes 786440 | tf_op jit(solution)/shard_map/ppermute | solution.py:366
  42.4 1.6 %collective-permute-start.13 = (bf16[2,96,384]{2,1,0:T(8,128)(2,1)S(1)}, bf16[2,96,384]{2,1,0:T(8,128)(2,1)S(1)}, u32[]{:S(2)}, u32[]{:S(2)}) collective-permute-start(bf16[2,96,384]{2,1,0:T(8,128)(2,1)S(1)} %collective-permute-done.12.refs_2_), channel_id=1, source_target_pairs={{0,4},{4,0},{8,12},{12,8},{16,20},{20,16},{24,28},{28,24},{1,5},{5... | collective-permute-start | bytes 442376 | tf_op jit(solution)/shard_map/ppermute | solution.py:366
  47.0 42.2 %all-to-all-start = ((bf16[4,384,512]{2,1,0:T(8,128)(2,1)}), bf16[4,384,512]{2,1,0:T(8,128)(2,1)}, u32[]{:S(2)}, u32[]{:S(2)}) async-start(bf16[4,384,512]{2,1,0:T(8,128)(2,1)} %get-tuple-element.46.refs_1_), calls=%async_computation | async-start | bytes 3145728 | tf_op jit(solution)/shard_map/all_to_all | solution.py:460
  56.6 1.8 %collective-permute-start.15 = (bf16[4,64,768]{2,1,0:T(8,128)(2,1)S(1)}, bf16[4,64,768]{2,1,0:T(8,128)(2,1)S(1)}, u32[]{:S(2)}, u32[]{:S(2)}) collective-permute-start(bf16[4,64,768]{2,1,0:T(8,128)(2,1)S(1)} %get-tuple-element.49), channel_id=1, source_target_pairs={{0,4},{4,0},{8,12},{12,8},{16,20},{20,16},{24,28},{28,24},{1,5},{5... | collective-permute-start | bytes 1179656 | tf_op jit(solution)/shard_map/ppermute | solution.py:366
  59.0 11.8 %collective-permute-start.16 = (bf16[208,768]{1,0:T(8,128)(2,1)S(1)}, bf16[208,768]{1,0:T(8,128)(2,1)S(1)}, u32[]{:S(2)}, u32[]{:S(2)}) collective-permute-start(bf16[208,768]{1,0:T(8,128)(2,1)S(1)} %get-tuple-element.51), channel_id=1, source_target_pairs={{0,8},{4,12},{8,0},{12,4},{16,24},{20,28},{24,16},{28,20},{1,9},{5... | collective-permute-start | bytes 958472 | tf_op jit(solution)/shard_map/ppermute | solution.py:369
  59.7 11.4 %collective-permute-start.17 = (bf16[208,768]{1,0:T(8,128)(2,1)S(1)}, bf16[208,768]{1,0:T(8,128)(2,1)S(1)}, u32[]{:S(2)}, u32[]{:S(2)}) collective-permute-start(bf16[208,768]{1,0:T(8,128)(2,1)S(1)} %get-tuple-element.52), channel_id=1, source_target_pairs={{0,16},{4,20},{8,24},{12,28},{16,0},{20,4},{24,8},{28,12},{1,17},{... | collective-permute-start | bytes 958472 | tf_op jit(solution)/shard_map/ppermute | solution.py:369
  61.1 9.8 %collective-permute-start.18 = (bf16[64,768]{1,0:T(8,128)(2,1)S(1)}, bf16[64,768]{1,0:T(8,128)(2,1)S(1)}, u32[]{:S(2)}, u32[]{:S(2)}) collective-permute-start(bf16[64,768]{1,0:T(8,128)(2,1)S(1)} %get-tuple-element.53), channel_id=1, source_target_pairs={{0,24},{4,28},{8,16},{12,20},{16,8},{20,12},{24,0},{28,4},{1,25},{... | collective-permute-start | bytes 294920 | tf_op jit(solution)/shard_map/ppermute | solution.py:369
  71.7 15.5 %collective-permute-start.19 = (bf16[2,144,768]{2,1,0:T(8,128)(2,1)S(1)}, bf16[2,144,768]{2,1,0:T(8,128)(2,1)S(1)}, u32[]{:S(2)}, u32[]{:S(2)}) collective-permute-start(bf16[2,144,768]{2,1,0:T(8,128)(2,1)S(1)} %get-tuple-element.54.refs_3_), channel_id=1, source_target_pairs={{0,4},{4,0},{8,12},{12,8},{16,20},{20,16},{24,28},{28,24},{1,5},{5... | collective-permute-start | bytes 1327112 | tf_op jit(solution)/shard_map/ppermute | solution.py:366
  71.8 7.2 %collective-permute-start.20 = (bf16[112,768]{1,0:T(8,128)(2,1)S(1)}, bf16[112,768]{1,0:T(8,128)(2,1)S(1)}, u32[]{:S(2)}, u32[]{:S(2)}) collective-permute-start(bf16[112,768]{1,0:T(8,128)(2,1)S(1)} %get-tuple-element.55), channel_id=1, source_target_pairs={{0,8},{4,12},{8,0},{12,4},{16,24},{20,28},{24,16},{28,20},{1,9},{5... | collective-permute-start | bytes 516104 | tf_op jit(solution)/shard_map/ppermute | solution.py:369
  73.3 10.1 %collective-permute-start.21 = (bf16[112,768]{1,0:T(8,128)(2,1)S(1)}, bf16[112,768]{1,0:T(8,128)(2,1)S(1)}, u32[]{:S(2)}, u32[]{:S(2)}) collective-permute-start(bf16[112,768]{1,0:T(8,128)(2,1)S(1)} %get-tuple-element.56), channel_id=1, source_target_pairs={{0,16},{4,20},{8,24},{12,28},{16,0},{20,4},{24,8},{28,12},{1,17},{... | collective-permute-start | bytes 516104 | tf_op jit(solution)/shard_map/ppermute | solution.py:369
  73.8 9.6 %collective-permute-start.22 = (bf16[112,768]{1,0:T(8,128)(2,1)S(1)}, bf16[112,768]{1,0:T(8,128)(2,1)S(1)}, u32[]{:S(2)}, u32[]{:S(2)}) collective-permute-start(bf16[112,768]{1,0:T(8,128)(2,1)S(1)} %get-tuple-element.57), channel_id=1, source_target_pairs={{0,24},{4,28},{8,16},{12,20},{16,8},{20,12},{24,0},{28,4},{1,25},{... | collective-permute-start | bytes 516104 | tf_op jit(solution)/shard_map/ppermute | solution.py:369
  75.3 8.6 %collective-permute-start.14 = (bf16[1,96,384]{2,1,0:T(8,128)(2,1)S(1)}, bf16[1,96,384]{2,1,0:T(8,128)(2,1)S(1)}, u32[]{:S(2)}, u32[]{:S(2)}) collective-permute-start(bf16[1,96,384]{2,1,0:T(8,128)(2,1)S(1)} %collective-permute-done.4.refs_2_.refs_1_), channel_id=1, source_target_pairs={{0,4},{4,0},{8,12},{12,8},{16,20},{20,16},{24,28},{28,24},{1,5},{5... | collective-permute-start | bytes 221192 | tf_op jit(solution)/shard_map/ppermute | solution.py:366
  79.0 6.2 %collective-permute-start.23 = (bf16[112,768]{1,0:T(8,128)(2,1)S(1)}, bf16[112,768]{1,0:T(8,128)(2,1)S(1)}, u32[]{:S(2)}, u32[]{:S(2)}) collective-permute-start(bf16[112,768]{1,0:T(8,128)(2,1)S(1)} %collective-permute-done.20.refs_5_.refs_2_), channel_id=1, source_target_pairs={{0,4},{4,0},{8,12},{12,8},{16,20},{20,16},{24,28},{28,24},{1,5},{5... | collective-permute-start | bytes 516104 | tf_op jit(solution)/shard_map/ppermute | solution.py:366
  83.4 1.8 %collective-permute-start.24 = (bf16[112,768]{1,0:T(8,128)(2,1)S(1)}, bf16[112,768]{1,0:T(8,128)(2,1)S(1)}, u32[]{:S(2)}, u32[]{:S(2)}) collective-permute-start(bf16[112,768]{1,0:T(8,128)(2,1)S(1)} %collective-permute-done.21.refs_6_.refs_3_), channel_id=1, source_target_pairs={{0,4},{4,0},{8,12},{12,8},{16,20},{20,16},{24,28},{28,24},{1,5},{5... | collective-permute-start | bytes 516104 | tf_op jit(solution)/shard_map/ppermute | solution.py:366
  83.4 1.8 %collective-permute-start.25 = (bf16[112,768]{1,0:T(8,128)(2,1)S(1)}, bf16[112,768]{1,0:T(8,128)(2,1)S(1)}, u32[]{:S(2)}, u32[]{:S(2)}) collective-permute-start(bf16[112,768]{1,0:T(8,128)(2,1)S(1)} %collective-permute-done.22.refs_7_.refs_4_), channel_id=1, source_target_pairs={{0,4},{4,0},{8,12},{12,8},{16,20},{20,16},{24,28},{28,24},{1,5},{5... | collective-permute-start | bytes 516104 | tf_op jit(solution)/shard_map/ppermute | solution.py:366
  83.9 1.3 %collective-permute-start.26 = (bf16[64,768]{1,0:T(8,128)(2,1)S(1)}, bf16[64,768]{1,0:T(8,128)(2,1)S(1)}, u32[]{:S(2)}, u32[]{:S(2)}) collective-permute-start(bf16[64,768]{1,0:T(8,128)(2,1)S(1)} %get-tuple-element.58.refs_1_), channel_id=1, source_target_pairs={{0,4},{4,0},{8,12},{12,8},{16,20},{20,16},{24,28},{28,24},{1,5},{5... | collective-permute-start | bytes 294920 | tf_op jit(solution)/shard_map/ppermute | solution.py:366

commit v5 on v4

--- a/solution.py
+++ b/solution.py
@@ -193,11 +193,10 @@
 def grads_kernel(pieces, place, *refs):
     mine, other = refs[0:pieces], refs[pieces : 2 * pieces]
     qt, kt, vt, gt = refs[2 * pieces : 2 * pieces + 4]
-    send_far, four_far, full, send, four, sems = refs[2 * pieces + 4 :]
-    zeds = send.shape[0]
+    send_far, att_far, full, send, att, sems = refs[2 * pieces + 4 :]
     heads, _, cols = qt.shape
-    stacked, tokens = four.shape
-    rows, width, block = tokens // cols, stacked // 4, cols // zeds
+    zeds, width, tokens = att.shape
+    block = cols // zeds
     assemble(place, mine, other, full)
     copies = []
     for h in range(heads):
@@ -210,38 +209,36 @@
         )
         for t, value in enumerate(values):
             value = value.astype(BF16)
-            at = slice(t * width + h * HEAD_DIM, t * width + (h + 1) * HEAD_DIM)
-            for r in range(rows):
+            near, far, at = (send, send_far, t * width) if t < 3 else (att, att_far, 0)
+            at = slice(at + h * HEAD_DIM, at + (h + 1) * HEAD_DIM)
+            for r in range(tokens // block):
                 part = value[r * HEAD_DIM : (r + 1) * HEAD_DIM]
-                four[at, r * cols : (r + 1) * cols] = part
-                if t < 3:
-                    for z in range(zeds):
-                        cut = part[:, z * block : (z + 1) * block]
-                        send[z, at, r * block : (r + 1) * block] = cut
-            pairs = [(send.at[:, at], send_far.at[:, at])] if t < 3 else []
-            copies += fetch(pairs + [(four.at[at], four_far.at[at])], sems.at[h * 4 + t])
+                for z in range(zeds):
+                    near[z, at, r * block : (r + 1) * block] = part[:, z * block : (z + 1) * block]
+            copies += fetch([(near.at[:, at], far.at[:, at])], sems.at[pl.ds(h * 4 + t, 1)])
     for copy in copies:
         copy.wait()
 
 
-def weights_kernel(place, x_far, og_far, four_far, keep, give, x, og, four, total, sems):
-    stacked, tokens = four.shape
-    three = 3 * stacked // 4
+def weights_kernel(place, x_far, og_far, send_far, att_far, keep, give, x, og, send, att, total, sems):
+    zeds, three, tokens = send.shape
+    rows, cols, model = x_far.shape
+    block = cols // zeds
+    stacked = total.shape[0]
     piece_rows = keep.shape[1]
-    steps = sems.shape[0]
-    spans = [slice(i * tokens // steps, (i + 1) * tokens // steps) for i in range(steps)]
     copies = []
-    for i, span in enumerate(spans):
-        pairs = [(four_far.at[:, span], four.at[:, span]), (x_far.at[span], x.at[span])]
-        copies.append(fetch(pairs + [(og_far.at[span], og.at[span])], sems.at[i]))
-    for i, span in enumerate(spans):
-        for copy in copies[i]:
-            copy.wait()
-        for first, last, other in ((0, three, x), (three, stacked, og)):
-            part = dot_nn(four[first:last, span], other[span, :])
-            if i > 0:
+    for z in range(zeds):
+        at = pl.ds(z * block, block)
+        pairs = [(send_far.at[z], send.at[z]), (x_far.at[:, at], x.at[z])]
+        copies.append(fetch(pairs + [(att_far.at[z], att.at[z]), (og_far.at[:, at], og.at[z])], sems.at[z]))
+    for z in range(zeds):
+        for first, last, left, right, half in ((0, three, send, x, 0), (three, stacked, att, og, 2)):
+            for copy in copies[z][half : half + 2]:
+                copy.wait()
+            part = dot_nn(left[z], right[z].reshape(tokens, model))
+            if z > 0:
                 part = part + total[first:last, :]
-            if i < steps - 1:
+            if z < zeds - 1:
                 total[first:last, :] = part
             else:
                 deal(place[0], place[1], first // piece_rows, keep, give, part.astype(BF16))
@@ -324,22 +321,27 @@
     total[...] = dot_nn(full[...], send[...])
 
 
-def inputs_kernel(place, sent_far, own_part, full, out, sent, sems):
+def inputs_kernel(place, sent_far, own_part, full, out_far, sent, out, sems):
     rows, block, _ = out.shape
     zeds, depth, _ = sent_far.shape
     pairs = []
     for k in range(1, zeds):
         far = sent_far.at[jnp.bitwise_xor(place[2], k)]
         pairs.append((far, sent.at[(k - 1) * depth : k * depth]))
-    for copy in fetch(pairs, sems):
+    for copy in fetch(pairs, sems.at[0]):
         copy.wait()
     step = min(2, rows)
+    copies = []
     for r in range(0, rows, step):
         span = slice(r * block, (r + step) * block)
         value = own_part[:, span] + dot_nn(full[...], sent[:, span])
         value = value.astype(BF16).T
         for i in range(step):
             out[r + i] = value[i * block : (i + 1) * block]
+        here = pl.ds(r, step)
+        copies += fetch([(out.at[here], out_far.at[here])], sems.at[1, pl.ds(r // step, 1)])
+    for copy in copies:
+        copy.wait()
 
 
 def body(inputs, out_grad, w_query, w_key, w_value, w_output):
@@ -426,11 +428,11 @@
     )
     swapped = [swap(group) for group in groups[1:]]
     mine, other = gathered(scored, pieces)
-    send, four = call(
+    send, att = call(
         partial(grads_kernel, pieces),
         (
             pltpu.HBM((zeds, 3 * width, rows * block), BF16),
-            pltpu.HBM((4 * width, rows * cols), BF16),
+            pltpu.HBM((zeds, width, rows * block), BF16),
         ),
         (place, *mine, *other, qt, kt, vt, gt),
         held=swapped[1:] or swapped,
@@ -438,8 +440,8 @@
         scratch=[
             pltpu.VMEM((heads * cols, 2 * cols), BF16),
             pltpu.VMEM((zeds, 3 * width, rows * block), BF16),
-            pltpu.VMEM((4 * width, rows * cols), BF16),
-            pltpu.SemaphoreType.DMA((heads * 4, 2)),
+            pltpu.VMEM((zeds, width, rows * block), BF16),
+            pltpu.SemaphoreType.DMA((heads * 4,)),
         ],
         flops=4 * score_flops,
         name="grads",
@@ -462,14 +464,15 @@
     keep, give = call(
         weights_kernel,
         [shape(pieces, wide, model)] * 2,
-        (place, inputs.reshape(-1, model), out_grad.reshape(-1, model), four),
-        hbm=3,
+        (place, inputs, out_grad, send, att),
+        hbm=4,
         scratch=[
-            pltpu.VMEM((rows * cols, model), BF16),
-            pltpu.VMEM((rows * cols, model), BF16),
-            pltpu.VMEM((4 * width, rows * cols), BF16),
+            pltpu.VMEM((zeds, rows, block, model), BF16),
+            pltpu.VMEM((zeds, rows, block, model), BF16),
+            pltpu.VMEM((zeds, 3 * width, rows * block), BF16),
+            pltpu.VMEM((zeds, width, rows * block), BF16),
             pltpu.VMEM((4 * width, model), F32),
-            pltpu.SemaphoreType.DMA((rows, 3)),
+            pltpu.SemaphoreType.DMA((zeds, 4)),
         ],
         flops=4 * dot_flops,
         moved=inputs.size * 4,
@@ -521,13 +524,15 @@
     )
     grad_inputs = call(
         inputs_kernel,
-        shape(rows, block, model),
+        pltpu.HBM((rows, block, model), BF16),
         (place, sent, own_part, full),
         hbm=1,
         scratch=[
             pltpu.VMEM(((zeds - 1) * 3 * width, rows * block), BF16),
-            pltpu.SemaphoreType.DMA((zeds - 1,)),
+            pltpu.VMEM((rows, block, model), BF16),
+            pltpu.SemaphoreType.DMA((2, max(zeds, rows))),
         ],
+        out_specs=hbm_spec(),
         flops=3 * dot_flops * (zeds - 1) // zeds,
         name="inputs",
     )

time: 93.5 us -> 93.3 us (level)
  no operation moved by 1% of the time
where the time goes in v5:
time: 93.3 us; the launch traced here: 93 us
  waiting for transfers between devices  38.5 us (41%)
  Pallas kernels  27.2 us (29%)
  starting transfers between devices  26.5 us (28%)
    ppermute x12, waiting for transfers between devices, across(): return lax.ppermute(value, 'seq', [(i, i ^ 2 * k) for i in range(seqs)])  29.5 us
    pallas_call x14, Pallas kernels, call(): pl.pallas_call(run, out_shape=outs, in_specs=[smem_spec()] + [hbm_spec()]...  27.2 us
    ppermute x12, starting transfers between devices, across(): return lax.ppermute(value, 'seq', [(i, i ^ 2 * k) for i in range(seqs)])  15.1 us
    ppermute x13, waiting for transfers between devices, swap(): return lax.ppermute(value, 'seq', [(i, i ^ 1) for i in range(seqs)])  5.65 us
    all_to_all x1, starting transfers between devices, body(): sent = lax.all_to_all(send, 'head', 0, 0, tiled=True)  4.88 us
    ppermute x2, starting transfers between devices, along(): return lax.ppermute(value, 'head', [(i, i ^ k) for i in range(zeds)])  4.63 us
    ppermute x2, waiting for transfers between devices, along(): return lax.ppermute(value, 'head', [(i, i ^ k) for i in range(zeds)])  2.33 us
  transfers between devices with their start and end apart: 28, of which 14 were waited for; matrix products, arithmetic and copies ran while one was open for 0% of the time, Pallas kernels for 14%

profile of v5, /device:TPU:0, one launch (start us, length us, event | category | flops | bytes accessed | tf_op | source)
XLA Modules:
  0.0 93.0 jit_solution(3383114345253599602)
XLA Ops:
  0.7 6.0 %front.1 = (bf16[2,256,512]{2,1,0:T(8,128)(2,1)S(1)}, bf16[2,256,512]{2,1,0:T(8,128)(2,1)S(1)}, bf16[2,256,512]{2,1,0:T(8,128)(2,1)S(1)}, bf16[2,256,512]{2,1,0:...) custom-call(s32[4]{0:T(128)S(1)} %pad_add_fusion.refs_0_, ...), custom_call_target="tpu_custom_call" | custom-call | flops 2147483648 | tf_op jit(solution)/shard_map/front/pallas_call | solution.py:49
  7.2 2.3 %collective-permute-done.refs_2_ = bf16[4,128,1024]{2,1,0:T(8,128)(2,1)S(1)} collective-permute-done((bf16[4,128,1024]{2,1,0:T(8,128)(2,1)S(1)}, bf16[4,128,1024]{2,1,0:T(8,128)(2,1)S(1)}, u32[]{:S(2)}, u32[]{:S(2)}) %collective-permute-start) | collective-permute-done | bytes 1048608 | tf_op jit(solution)/shard_map/ppermute | solution.py:368
  9.5 0.8 pair_scores.1
  10.3 2.9 %collective-permute-start.1 = (bf16[128,1024]{1,0:T(8,128)(2,1)S(1)}, bf16[128,1024]{1,0:T(8,128)(2,1)S(1)}, u32[]{:S(2)}, u32[]{:S(2)}) collective-permute-start(bf16[128,1024]{1,0:T(8,128)(2,1)S(1)} %get-tuple-element.38), channel_id=1, source_target_pairs={{0,8},{4,12},{8,0},{12,4},{16,24},{20,28},{24,16},{28,20},{1,9},{5... | collective-permute-start | bytes 786440 | tf_op jit(solution)/shard_map/ppermute | solution.py:371
  13.2 1.5 %collective-permute-start.2 = (bf16[128,1024]{1,0:T(8,128)(2,1)S(1)}, bf16[128,1024]{1,0:T(8,128)(2,1)S(1)}, u32[]{:S(2)}, u32[]{:S(2)}) collective-permute-start(bf16[128,1024]{1,0:T(8,128)(2,1)S(1)} %get-tuple-element.39), channel_id=1, source_target_pairs={{0,16},{4,20},{8,24},{12,28},{16,0},{20,4},{24,8},{28,12},{1,17},{... | collective-permute-start | bytes 786440 | tf_op jit(solution)/shard_map/ppermute | solution.py:371
  14.8 2.0 %collective-permute-start.4 = (bf16[1,96,384]{2,1,0:T(8,128)(2,1)S(1)}, bf16[1,96,384]{2,1,0:T(8,128)(2,1)S(1)}, u32[]{:S(2)}, u32[]{:S(2)}) collective-permute-start(bf16[1,96,384]{2,1,0:T(8,128)(2,1)S(1)} %get-tuple-element.41.refs_1_), channel_id=1, source_target_pairs={{0,1},{1,0},{2,3},{3,2},{4,5},{5,4},{6,7},{7,6},{8,9},{9,8},{10,11... | collective-permute-start | bytes 221192 | tf_op jit(solution)/shard_map/ppermute | solution.py:374
  16.8 2.3 %collective-permute-done.4.refs_2_.refs_1_ = bf16[1,96,384]{2,1,0:T(8,128)(2,1)S(1)} collective-permute-done((bf16[1,96,384]{2,1,0:T(8,128)(2,1)S(1)}, bf16[1,96,384]{2,1,0:T(8,128)(2,1)S(1)}, u32[]{:S(2)}, u32[]{:S(2)}) %collective-permute-start.4) | collective-permute-done | bytes 73760 | tf_op jit(solution)/shard_map/ppermute | solution.py:374
  20.3 6.6 %collective-permute-done.2.refs_3_ = bf16[128,1024]{1,0:T(8,128)(2,1)S(1)} collective-permute-done((bf16[128,1024]{1,0:T(8,128)(2,1)S(1)}, bf16[128,1024]{1,0:T(8,128)(2,1)S(1)}, u32[]{:S(2)}, u32[]{:S(2)}) %collective-permute-start.2) | collective-permute-done | bytes 262176 | tf_op jit(solution)/shard_map/ppermute | solution.py:371
  26.9 0.8 score.1.refs_1_
  27.7 1.3 %collective-permute-start.5 = (bf16[128,1024]{1,0:T(8,128)(2,1)S(1)}, bf16[128,1024]{1,0:T(8,128)(2,1)S(1)}, u32[]{:S(2)}, u32[]{:S(2)}) collective-permute-start(bf16[128,1024]{1,0:T(8,128)(2,1)S(1)} %score.1.refs_1_), channel_id=1, source_target_pairs={{0,8},{4,12},{8,0},{12,4},{16,24},{20,28},{24,16},{28,20},{1,9},{5... | collective-permute-start | bytes 786440 | tf_op jit(solution)/shard_map/ppermute | solution.py:371
  29.0 0.8 collective-permute-start.6
  29.9 1.4 %collective-permute-start.7 = (bf16[128,1024]{1,0:T(8,128)(2,1)S(1)}, bf16[128,1024]{1,0:T(8,128)(2,1)S(1)}, u32[]{:S(2)}, u32[]{:S(2)}) collective-permute-start(bf16[128,1024]{1,0:T(8,128)(2,1)S(1)} %score.1.refs_1_), channel_id=1, source_target_pairs={{0,24},{4,28},{8,16},{12,20},{16,8},{20,12},{24,0},{28,4},{1,25},{... | collective-permute-start | bytes 786440 | tf_op jit(solution)/shard_map/ppermute | solution.py:371
  31.3 2.6 %collective-permute-start.12 = (bf16[2,96,384]{2,1,0:T(8,128)(2,1)S(1)}, bf16[2,96,384]{2,1,0:T(8,128)(2,1)S(1)}, u32[]{:S(2)}, u32[]{:S(2)}) collective-permute-start(bf16[2,96,384]{2,1,0:T(8,128)(2,1)S(1)} %join.1.refs_5_), channel_id=1, source_target_pairs={{0,2},{1,3},{2,0},{3,1},{4,6},{5,7},{6,4},{7,5},{8,10},{9,11},{10,... | collective-permute-start | bytes 442376 | tf_op jit(solution)/shard_map/ppermute | solution.py:374
  33.9 3.2 %collective-permute-done.5.refs_2_ = bf16[128,1024]{1,0:T(8,128)(2,1)S(1)} collective-permute-done((bf16[128,1024]{1,0:T(8,128)(2,1)S(1)}, bf16[128,1024]{1,0:T(8,128)(2,1)S(1)}, u32[]{:S(2)}, u32[]{:S(2)}) %collective-permute-start.5) | collective-permute-done | bytes 262176 | tf_op jit(solution)/shard_map/ppermute | solution.py:371
  37.1 4.8 %collective-permute-done.6.refs_3_ = bf16[128,1024]{1,0:T(8,128)(2,1)S(1)} collective-permute-done((bf16[128,1024]{1,0:T(8,128)(2,1)S(1)}, bf16[128,1024]{1,0:T(8,128)(2,1)S(1)}, u32[]{:S(2)}, u32[]{:S(2)}) %collective-permute-start.6) | collective-permute-done | bytes 262176 | tf_op jit(solution)/shard_map/ppermute | solution.py:371
  42.5 1.5 %collective-permute-done.13.refs_13_.refs_2_ = bf16[2,96,384]{2,1,0:T(8,128)(2,1)S(1)} collective-permute-done((bf16[2,96,384]{2,1,0:T(8,128)(2,1)S(1)}, bf16[2,96,384]{2,1,0:T(8,128)(2,1)S(1)}, u32[]{:S(2)}, u32[]{:S(2)}) %collective-permute-start.13) | collective-permute-done | bytes 147488 | tf_op jit(solution)/shard_map/ppermute | solution.py:368
  44.0 2.8 %grads.1 = (bf16[4,384,512]{2,1,0:T(8,128)(2,1)}, bf16[4,128,512]{2,1,0:T(8,128)(2,1)}) custom-call(s32[4]{0:T(128)S(1)} %pad_add_fusion.refs_0_, bf16[128,1024]{1,0:T(8,128)(2,1)S(1)} %score.1.refs_1_, bf16[128,1024]{1,0:T(8,128)(2,1)S(1)} %collective-permute-done.5.refs_2_, bf16[128,1024]{1,0:T(8,128)(2,1)S(1)} %collective-permute-done.6.refs_3_, ...), custom_call_target="tpu_custom_call" | custom-call | flops 1073741824 | tf_op jit(solution)/shard_map/grads/pallas_call | solution.py:49
  46.8 4.9 %all-to-all-start = ((bf16[4,384,512]{2,1,0:T(8,128)(2,1)}), bf16[4,384,512]{2,1,0:T(8,128)(2,1)}, u32[]{:S(2)}, u32[]{:S(2)}) async-start(bf16[4,384,512]{2,1,0:T(8,128)(2,1)} %get-tuple-element.46.refs_1_.refs_3_), calls=%async_computation | async-start | bytes 3145728 | tf_op jit(solution)/shard_map/all_to_all | solution.py:462
  51.7 4.9 %weights.1 = (bf16[4,64,768]{2,1,0:T(8,128)(2,1)S(1)}, bf16[4,64,768]{2,1,0:T(8,128)(2,1)S(1)}) custom-call(s32[4]{0:T(128)S(1)} %pad_add_fusion.refs_0_, bf16[4,512,768]{2,1,0:T(8,128)(2,1)} %refs_1_.3, bf16[4,512,768]{2,1,0:T(8,128)(2,1)} %refs_2_.5, bf16[4,384,512]{2,1,0:T(8,128)(2,1)} %get-tuple-element.46.refs_1_.refs_3_, ...), custom_call_target="tpu_custom_call" | custom-call | flops 1610612736 | bytes 6291456 | tf_op jit(solution)/shard_map/weights/pallas_call | solution.py:49
  57.3 1.1 %collective-permute-done.15.refs_2_ = bf16[4,64,768]{2,1,0:T(8,128)(2,1)S(1)} collective-permute-done((bf16[4,64,768]{2,1,0:T(8,128)(2,1)S(1)}, bf16[4,64,768]{2,1,0:T(8,128)(2,1)S(1)}, u32[]{:S(2)}, u32[]{:S(2)}) %collective-permute-start.15) | collective-permute-done | bytes 393248 | tf_op jit(solution)/shard_map/ppermute | solution.py:368
  59.7 1.4 %collective-permute-start.17 = (bf16[208,768]{1,0:T(8,128)(2,1)S(1)}, bf16[208,768]{1,0:T(8,128)(2,1)S(1)}, u32[]{:S(2)}, u32[]{:S(2)}) collective-permute-start(bf16[208,768]{1,0:T(8,128)(2,1)S(1)} %get-tuple-element.52), channel_id=1, source_target_pairs={{0,16},{4,20},{8,24},{12,28},{16,0},{20,4},{24,8},{28,12},{1,17},{... | collective-permute-start | bytes 958472 | tf_op jit(solution)/shard_map/ppermute | solution.py:371
  61.1 1.5 %collective-permute-start.18 = (bf16[64,768]{1,0:T(8,128)(2,1)S(1)}, bf16[64,768]{1,0:T(8,128)(2,1)S(1)}, u32[]{:S(2)}, u32[]{:S(2)}) collective-permute-start(bf16[64,768]{1,0:T(8,128)(2,1)S(1)} %get-tuple-element.53), channel_id=1, source_target_pairs={{0,24},{4,28},{8,16},{12,20},{16,8},{20,12},{24,0},{28,4},{1,25},{... | collective-permute-start | bytes 294920 | tf_op jit(solution)/shard_map/ppermute | solution.py:371
  62.6 2.3 %own_inputs.1.refs_6_.refs_2_ = f32[768,512]{1,0:T(8,128)S(1)} custom-call(s32[4]{0:T(128)S(1)} %pad_add_fusion.refs_0_, bf16[4,384,512]{2,1,0:T(8,128)(2,1)} %get-tuple-element.46.refs_1_.refs_3_, bf16[768,128]{1,0:T(8,128)(2,1)} %refs_2_.4, bf16[768,128]{1,0:T(8,128)(2,1)} %refs_3_.3, bf16[768,128]{1,0:T(8,128)(2,1)} %refs_4_.3), custom_call_target="tpu_custom_call" | custom-call | flops 301989888 | tf_op jit(solution)/shard_map/own_inputs/pallas_call | solution.py:49
  65.0 5.9 %collective-permute-done.18.refs_5_ = bf16[64,768]{1,0:T(8,128)(2,1)S(1)} collective-permute-done((bf16[64,768]{1,0:T(8,128)(2,1)S(1)}, bf16[64,768]{1,0:T(8,128)(2,1)S(1)}, u32[]{:S(2)}, u32[]{:S(2)}) %collective-permute-start.18) | collective-permute-done | bytes 98336 | tf_op jit(solution)/shard_map/ppermute | solution.py:371
  71.8 1.5 %collective-permute-start.20 = (bf16[112,768]{1,0:T(8,128)(2,1)S(1)}, bf16[112,768]{1,0:T(8,128)(2,1)S(1)}, u32[]{:S(2)}, u32[]{:S(2)}) collective-permute-start(bf16[112,768]{1,0:T(8,128)(2,1)S(1)} %get-tuple-element.55), channel_id=1, source_target_pairs={{0,8},{4,12},{8,0},{12,4},{16,24},{20,28},{24,16},{28,20},{1,9},{5... | collective-permute-start | bytes 516104 | tf_op jit(solution)/shard_map/ppermute | solution.py:371
  73.9 1.5 %collective-permute-start.22 = (bf16[112,768]{1,0:T(8,128)(2,1)S(1)}, bf16[112,768]{1,0:T(8,128)(2,1)S(1)}, u32[]{:S(2)}, u32[]{:S(2)}) collective-permute-start(bf16[112,768]{1,0:T(8,128)(2,1)S(1)} %get-tuple-element.57), channel_id=1, source_target_pairs={{0,24},{4,28},{8,16},{12,20},{16,8},{20,12},{24,0},{28,4},{1,25},{... | collective-permute-start | bytes 516104 | tf_op jit(solution)/shard_map/ppermute | solution.py:371
  75.4 3.7 %collective-permute-done.20.refs_5_.refs_2_ = bf16[112,768]{1,0:T(8,128)(2,1)S(1)} collective-permute-done((bf16[112,768]{1,0:T(8,128)(2,1)S(1)}, bf16[112,768]{1,0:T(8,128)(2,1)S(1)}, u32[]{:S(2)}, u32[]{:S(2)}) %collective-permute-start.20) | collective-permute-done | bytes 172064 | tf_op jit(solution)/shard_map/ppermute | solution.py:371
  79.1 4.4 %collective-permute-done.21.refs_6_.refs_3_ = bf16[112,768]{1,0:T(8,128)(2,1)S(1)} collective-permute-done((bf16[112,768]{1,0:T(8,128)(2,1)S(1)}, bf16[112,768]{1,0:T(8,128)(2,1)S(1)}, u32[]{:S(2)}, u32[]{:S(2)}) %collective-permute-start.21) | collective-permute-done | bytes 172064 | tf_op jit(solution)/shard_map/ppermute | solution.py:371
  85.3 2.0 %unpack.1 = (f32[768,128]{1,0:T(8,128)}, f32[768,128]{1,0:T(8,128)}, f32[768,128]{1,0:T(8,128)}, f32[128,768]{1,0:T(8,128)}) custom-call(s32[4]{0:T(128)S(1)} %pad_add_fusion.refs_0_, bf16[64,768]{1,0:T(8,128)(2,1)S(1)} %get-tuple-element.58.refs_1_, bf16[112,768]{1,0:T(8,128)(2,1)S(1)} %collective-permute-done.20.refs_5_.refs_2_, ...), custom_call_target="tpu_custom_call" | custom-call | tf_op jit(solution)/shard_map/unpack/pallas_call | solution.py:49
  87.3 0.7 gather_weights.1.refs_3_
  88.0 1.1 %all-to-all-done.refs_1_ = bf16[4,384,512]{2,1,0:T(8,128)(2,1)} async-done(((bf16[4,384,512]{2,1,0:T(8,128)(2,1)}), bf16[4,384,512]{2,1,0:T(8,128)(2,1)}, u32[]{:S(2)}, u32[]{:S(2)}) %all-to-all-start) | async-done | bytes 1572896 | tf_op jit(solution)/shard_map/all_to_all | solution.py:462
  89.1 4.0 %inputs.1 = bf16[4,128,768]{2,1,0:T(8,128)(2,1)} custom-call(s32[4]{0:T(128)S(1)} %pad_add_fusion.refs_0_, bf16[4,384,512]{2,1,0:T(8,128)(2,1)} %all-to-all-done.refs_1_, f32[768,512]{1,0:T(8,128)S(1)} %own_inputs.1.refs_6_.refs_2_, bf16[768,1152]{1,0:T(8,128)(2,1)S(1)} %gather_weights.1.refs_3_), custom_call_target="tpu_custom_call" | custom-call | flops 905969664 | tf_op jit(solution)/shard_map/inputs/pallas_call | solution.py:49
  (39 shorter events, 7.6 us)
Async XLA Ops:
  6.7 2.8 %collective-permute-start = (bf16[4,128,1024]{2,1,0:T(8,128)(2,1)S(1)}, bf16[4,128,1024]{2,1,0:T(8,128)(2,1)S(1)}, u32[]{:S(2)}, u32[]{:S(2)}) collective-permute-start(bf16[4,128,1024]{2,1,0:T(8,128)(2,1)S(1)} %get-tuple-element.35), channel_id=1, source_target_pairs={{0,4},{4,0},{8,12},{12,8},{16,20},{20,16},{24,28},{28,24},{1,5},{5... | collective-permute-start | bytes 3145736 | tf_op jit(solution)/shard_map/ppermute | solution.py:368
  10.3 10.0 %collective-permute-start.1 = (bf16[128,1024]{1,0:T(8,128)(2,1)S(1)}, bf16[128,1024]{1,0:T(8,128)(2,1)S(1)}, u32[]{:S(2)}, u32[]{:S(2)}) collective-permute-start(bf16[128,1024]{1,0:T(8,128)(2,1)S(1)} %get-tuple-element.38), channel_id=1, source_target_pairs={{0,8},{4,12},{8,0},{12,4},{16,24},{20,28},{24,16},{28,20},{1,9},{5... | collective-permute-start | bytes 786440 | tf_op jit(solution)/shard_map/ppermute | solution.py:371
  13.2 13.7 %collective-permute-start.2 = (bf16[128,1024]{1,0:T(8,128)(2,1)S(1)}, bf16[128,1024]{1,0:T(8,128)(2,1)S(1)}, u32[]{:S(2)}, u32[]{:S(2)}) collective-permute-start(bf16[128,1024]{1,0:T(8,128)(2,1)S(1)} %get-tuple-element.39), channel_id=1, source_target_pairs={{0,16},{4,20},{8,24},{12,28},{16,0},{20,4},{24,8},{28,12},{1,17},{... | collective-permute-start | bytes 786440 | tf_op jit(solution)/shard_map/ppermute | solution.py:371
  14.8 12.2 %collective-permute-start.3 = (bf16[128,1024]{1,0:T(8,128)(2,1)S(1)}, bf16[128,1024]{1,0:T(8,128)(2,1)S(1)}, u32[]{:S(2)}, u32[]{:S(2)}) collective-permute-start(bf16[128,1024]{1,0:T(8,128)(2,1)S(1)} %get-tuple-element.40), channel_id=1, source_target_pairs={{0,24},{4,28},{8,16},{12,20},{16,8},{20,12},{24,0},{28,4},{1,25},{... | collective-permute-start | bytes 786440 | tf_op jit(solution)/shard_map/ppermute | solution.py:371
  14.8 4.4 %collective-permute-start.4 = (bf16[1,96,384]{2,1,0:T(8,128)(2,1)S(1)}, bf16[1,96,384]{2,1,0:T(8,128)(2,1)S(1)}, u32[]{:S(2)}, u32[]{:S(2)}) collective-permute-start(bf16[1,96,384]{2,1,0:T(8,128)(2,1)S(1)} %get-tuple-element.41.refs_1_), channel_id=1, source_target_pairs={{0,1},{1,0},{2,3},{3,2},{4,5},{5,4},{6,7},{7,6},{8,9},{9,8},{10,11... | collective-permute-start | bytes 221192 | tf_op jit(solution)/shard_map/ppermute | solution.py:374
  27.7 9.3 %collective-permute-start.5 = (bf16[128,1024]{1,0:T(8,128)(2,1)S(1)}, bf16[128,1024]{1,0:T(8,128)(2,1)S(1)}, u32[]{:S(2)}, u32[]{:S(2)}) collective-permute-start(bf16[128,1024]{1,0:T(8,128)(2,1)S(1)} %score.1.refs_1_), channel_id=1, source_target_pairs={{0,8},{4,12},{8,0},{12,4},{16,24},{20,28},{24,16},{28,20},{1,9},{5... | collective-permute-start | bytes 786440 | tf_op jit(solution)/shard_map/ppermute | solution.py:371
  29.0 12.9 %collective-permute-start.6 = (bf16[128,1024]{1,0:T(8,128)(2,1)S(1)}, bf16[128,1024]{1,0:T(8,128)(2,1)S(1)}, u32[]{:S(2)}, u32[]{:S(2)}) collective-permute-start(bf16[128,1024]{1,0:T(8,128)(2,1)S(1)} %score.1.refs_1_), channel_id=1, source_target_pairs={{0,16},{4,20},{8,24},{12,28},{16,0},{20,4},{24,8},{28,12},{1,17},{... | collective-permute-start | bytes 786440 | tf_op jit(solution)/shard_map/ppermute | solution.py:371
  29.9 12.0 %collective-permute-start.7 = (bf16[128,1024]{1,0:T(8,128)(2,1)S(1)}, bf16[128,1024]{1,0:T(8,128)(2,1)S(1)}, u32[]{:S(2)}, u32[]{:S(2)}) collective-permute-start(bf16[128,1024]{1,0:T(8,128)(2,1)S(1)} %score.1.refs_1_), channel_id=1, source_target_pairs={{0,24},{4,28},{8,16},{12,20},{16,8},{20,12},{24,0},{28,4},{1,25},{... | collective-permute-start | bytes 786440 | tf_op jit(solution)/shard_map/ppermute | solution.py:371
  31.3 11.1 %collective-permute-start.12 = (bf16[2,96,384]{2,1,0:T(8,128)(2,1)S(1)}, bf16[2,96,384]{2,1,0:T(8,128)(2,1)S(1)}, u32[]{:S(2)}, u32[]{:S(2)}) collective-permute-start(bf16[2,96,384]{2,1,0:T(8,128)(2,1)S(1)} %join.1.refs_5_), channel_id=1, source_target_pairs={{0,2},{1,3},{2,0},{3,1},{4,6},{5,7},{6,4},{7,5},{8,10},{9,11},{10,... | collective-permute-start | bytes 442376 | tf_op jit(solution)/shard_map/ppermute | solution.py:374
  33.9 10.1 %collective-permute-start.8 = (bf16[128,1024]{1,0:T(8,128)(2,1)S(1)}, bf16[128,1024]{1,0:T(8,128)(2,1)S(1)}, u32[]{:S(2)}, u32[]{:S(2)}) collective-permute-start(bf16[128,1024]{1,0:T(8,128)(2,1)S(1)} %score.1.refs_1_), channel_id=1, source_target_pairs={{0,4},{4,0},{8,12},{12,8},{16,20},{20,16},{24,28},{28,24},{1,5},{5... | collective-permute-start | bytes 786440 | tf_op jit(solution)/shard_map/ppermute | solution.py:368
  37.0 7.0 %collective-permute-start.9 = (bf16[128,1024]{1,0:T(8,128)(2,1)S(1)}, bf16[128,1024]{1,0:T(8,128)(2,1)S(1)}, u32[]{:S(2)}, u32[]{:S(2)}) collective-permute-start(bf16[128,1024]{1,0:T(8,128)(2,1)S(1)} %collective-permute-done.5.refs_2_), channel_id=1, source_target_pairs={{0,4},{4,0},{8,12},{12,8},{16,20},{20,16},{24,28},{28,24},{1,5},{5... | collective-permute-start | bytes 786440 | tf_op jit(solution)/shard_map/ppermute | solution.py:368
  41.9 2.1 %collective-permute-start.10 = (bf16[128,1024]{1,0:T(8,128)(2,1)S(1)}, bf16[128,1024]{1,0:T(8,128)(2,1)S(1)}, u32[]{:S(2)}, u32[]{:S(2)}) collective-permute-start(bf16[128,1024]{1,0:T(8,128)(2,1)S(1)} %collective-permute-done.6.refs_3_), channel_id=1, source_target_pairs={{0,4},{4,0},{8,12},{12,8},{16,20},{20,16},{24,28},{28,24},{1,5},{5... | collective-permute-start | bytes 786440 | tf_op jit(solution)/shard_map/ppermute | solution.py:368
  41.9 2.1 %collective-permute-start.11 = (bf16[128,1024]{1,0:T(8,128)(2,1)S(1)}, bf16[128,1024]{1,0:T(8,128)(2,1)S(1)}, u32[]{:S(2)}, u32[]{:S(2)}) collective-permute-start(bf16[128,1024]{1,0:T(8,128)(2,1)S(1)} %collective-permute-done.7.refs_4_), channel_id=1, source_target_pairs={{0,4},{4,0},{8,12},{12,8},{16,20},{20,16},{24,28},{28,24},{1,5},{5... | collective-permute-start | bytes 786440 | tf_op jit(solution)/shard_map/ppermute | solution.py:368
  42.4 1.6 %collective-permute-start.13 = (bf16[2,96,384]{2,1,0:T(8,128)(2,1)S(1)}, bf16[2,96,384]{2,1,0:T(8,128)(2,1)S(1)}, u32[]{:S(2)}, u32[]{:S(2)}) collective-permute-start(bf16[2,96,384]{2,1,0:T(8,128)(2,1)S(1)} %collective-permute-done.12.refs_2_), channel_id=1, source_target_pairs={{0,4},{4,0},{8,12},{12,8},{16,20},{20,16},{24,28},{28,24},{1,5},{5... | collective-permute-start | bytes 442376 | tf_op jit(solution)/shard_map/ppermute | solution.py:368
  46.8 42.2 %all-to-all-start = ((bf16[4,384,512]{2,1,0:T(8,128)(2,1)}), bf16[4,384,512]{2,1,0:T(8,128)(2,1)}, u32[]{:S(2)}, u32[]{:S(2)}) async-start(bf16[4,384,512]{2,1,0:T(8,128)(2,1)} %get-tuple-element.46.refs_1_.refs_3_), calls=%async_computation | async-start | bytes 3145728 | tf_op jit(solution)/shard_map/all_to_all | solution.py:462
  56.6 1.8 %collective-permute-start.15 = (bf16[4,64,768]{2,1,0:T(8,128)(2,1)S(1)}, bf16[4,64,768]{2,1,0:T(8,128)(2,1)S(1)}, u32[]{:S(2)}, u32[]{:S(2)}) collective-permute-start(bf16[4,64,768]{2,1,0:T(8,128)(2,1)S(1)} %get-tuple-element.49), channel_id=1, source_target_pairs={{0,4},{4,0},{8,12},{12,8},{16,20},{20,16},{24,28},{28,24},{1,5},{5... | collective-permute-start | bytes 1179656 | tf_op jit(solution)/shard_map/ppermute | solution.py:368
  59.1 11.8 %collective-permute-start.16 = (bf16[208,768]{1,0:T(8,128)(2,1)S(1)}, bf16[208,768]{1,0:T(8,128)(2,1)S(1)}, u32[]{:S(2)}, u32[]{:S(2)}) collective-permute-start(bf16[208,768]{1,0:T(8,128)(2,1)S(1)} %get-tuple-element.51), channel_id=1, source_target_pairs={{0,8},{4,12},{8,0},{12,4},{16,24},{20,28},{24,16},{28,20},{1,9},{5... | collective-permute-start | bytes 958472 | tf_op jit(solution)/shard_map/ppermute | solution.py:371
  59.7 11.4 %collective-permute-start.17 = (bf16[208,768]{1,0:T(8,128)(2,1)S(1)}, bf16[208,768]{1,0:T(8,128)(2,1)S(1)}, u32[]{:S(2)}, u32[]{:S(2)}) collective-permute-start(bf16[208,768]{1,0:T(8,128)(2,1)S(1)} %get-tuple-element.52), channel_id=1, source_target_pairs={{0,16},{4,20},{8,24},{12,28},{16,0},{20,4},{24,8},{28,12},{1,17},{... | collective-permute-start | bytes 958472 | tf_op jit(solution)/shard_map/ppermute | solution.py:371
  61.1 9.8 %collective-permute-start.18 = (bf16[64,768]{1,0:T(8,128)(2,1)S(1)}, bf16[64,768]{1,0:T(8,128)(2,1)S(1)}, u32[]{:S(2)}, u32[]{:S(2)}) collective-permute-start(bf16[64,768]{1,0:T(8,128)(2,1)S(1)} %get-tuple-element.53), channel_id=1, source_target_pairs={{0,24},{4,28},{8,16},{12,20},{16,8},{20,12},{24,0},{28,4},{1,25},{... | collective-permute-start | bytes 294920 | tf_op jit(solution)/shard_map/ppermute | solution.py:371
  71.8 15.5 %collective-permute-start.19 = (bf16[2,144,768]{2,1,0:T(8,128)(2,1)S(1)}, bf16[2,144,768]{2,1,0:T(8,128)(2,1)S(1)}, u32[]{:S(2)}, u32[]{:S(2)}) collective-permute-start(bf16[2,144,768]{2,1,0:T(8,128)(2,1)S(1)} %get-tuple-element.54.refs_3_), channel_id=1, source_target_pairs={{0,4},{4,0},{8,12},{12,8},{16,20},{20,16},{24,28},{28,24},{1,5},{5... | collective-permute-start | bytes 1327112 | tf_op jit(solution)/shard_map/ppermute | solution.py:368
  71.8 7.2 %collective-permute-start.20 = (bf16[112,768]{1,0:T(8,128)(2,1)S(1)}, bf16[112,768]{1,0:T(8,128)(2,1)S(1)}, u32[]{:S(2)}, u32[]{:S(2)}) collective-permute-start(bf16[112,768]{1,0:T(8,128)(2,1)S(1)} %get-tuple-element.55), channel_id=1, source_target_pairs={{0,8},{4,12},{8,0},{12,4},{16,24},{20,28},{24,16},{28,20},{1,9},{5... | collective-permute-start | bytes 516104 | tf_op jit(solution)/shard_map/ppermute | solution.py:371
  73.3 10.1 %collective-permute-start.21 = (bf16[112,768]{1,0:T(8,128)(2,1)S(1)}, bf16[112,768]{1,0:T(8,128)(2,1)S(1)}, u32[]{:S(2)}, u32[]{:S(2)}) collective-permute-start(bf16[112,768]{1,0:T(8,128)(2,1)S(1)} %get-tuple-element.56), channel_id=1, source_target_pairs={{0,16},{4,20},{8,24},{12,28},{16,0},{20,4},{24,8},{28,12},{1,17},{... | collective-permute-start | bytes 516104 | tf_op jit(solution)/shard_map/ppermute | solution.py:371
  73.9 9.6 %collective-permute-start.22 = (bf16[112,768]{1,0:T(8,128)(2,1)S(1)}, bf16[112,768]{1,0:T(8,128)(2,1)S(1)}, u32[]{:S(2)}, u32[]{:S(2)}) collective-permute-start(bf16[112,768]{1,0:T(8,128)(2,1)S(1)} %get-tuple-element.57), channel_id=1, source_target_pairs={{0,24},{4,28},{8,16},{12,20},{16,8},{20,12},{24,0},{28,4},{1,25},{... | collective-permute-start | bytes 516104 | tf_op jit(solution)/shard_map/ppermute | solution.py:371
  75.4 8.6 %collective-permute-start.14 = (bf16[1,96,384]{2,1,0:T(8,128)(2,1)S(1)}, bf16[1,96,384]{2,1,0:T(8,128)(2,1)S(1)}, u32[]{:S(2)}, u32[]{:S(2)}) collective-permute-start(bf16[1,96,384]{2,1,0:T(8,128)(2,1)S(1)} %collective-permute-done.4.refs_2_.refs_1_), channel_id=1, source_target_pairs={{0,4},{4,0},{8,12},{12,8},{16,20},{20,16},{24,28},{28,24},{1,5},{5... | collective-permute-start | bytes 221192 | tf_op jit(solution)/shard_map/ppermute | solution.py:368
  79.1 6.2 %collective-permute-start.23 = (bf16[112,768]{1,0:T(8,128)(2,1)S(1)}, bf16[112,768]{1,0:T(8,128)(2,1)S(1)}, u32[]{:S(2)}, u32[]{:S(2)}) collective-permute-start(bf16[112,768]{1,0:T(8,128)(2,1)S(1)} %collective-permute-done.20.refs_5_.refs_2_), channel_id=1, source_target_pairs={{0,4},{4,0},{8,12},{12,8},{16,20},{20,16},{24,28},{28,24},{1,5},{5... | collective-permute-start | bytes 516104 | tf_op jit(solution)/shard_map/ppermute | solution.py:368
  83.5 1.8 %collective-permute-start.24 = (bf16[112,768]{1,0:T(8,128)(2,1)S(1)}, bf16[112,768]{1,0:T(8,128)(2,1)S(1)}, u32[]{:S(2)}, u32[]{:S(2)}) collective-permute-start(bf16[112,768]{1,0:T(8,128)(2,1)S(1)} %collective-permute-done.21.refs_6_.refs_3_), channel_id=1, source_target_pairs={{0,4},{4,0},{8,12},{12,8},{16,20},{20,16},{24,28},{28,24},{1,5},{5... | collective-permute-start | bytes 516104 | tf_op jit(solution)/shard_map/ppermute | solution.py:368
  83.5 1.8 %collective-permute-start.25 = (bf16[112,768]{1,0:T(8,128)(2,1)S(1)}, bf16[112,768]{1,0:T(8,128)(2,1)S(1)}, u32[]{:S(2)}, u32[]{:S(2)}) collective-permute-start(bf16[112,768]{1,0:T(8,128)(2,1)S(1)} %collective-permute-done.22.refs_7_.refs_4_), channel_id=1, source_target_pairs={{0,4},{4,0},{8,12},{12,8},{16,20},{20,16},{24,28},{28,24},{1,5},{5... | collective-permute-start | bytes 516104 | tf_op jit(solution)/shard_map/ppermute | solution.py:368
  84.0 1.3 %collective-permute-start.26 = (bf16[64,768]{1,0:T(8,128)(2,1)S(1)}, bf16[64,768]{1,0:T(8,128)(2,1)S(1)}, u32[]{:S(2)}, u32[]{:S(2)}) collective-permute-start(bf16[64,768]{1,0:T(8,128)(2,1)S(1)} %get-tuple-element.58.refs_1_), channel_id=1, source_target_pairs={{0,4},{4,0},{8,12},{12,8},{16,20},{20,16},{24,28},{28,24},{1,5},{5... | collective-permute-start | bytes 294920 | tf_op jit(solution)/shard_map/ppermute | solution.py:368

commit v6 on v5

--- a/solution.py
+++ b/solution.py
@@ -83,18 +83,19 @@
         give[slot, :, cols] = jnp.where(mine, odd, even)
 
 
-def scores(chip, core, left, right, turned, keep, give, first):
+def scores(chip, core, left, right, keep, give, first):
     heads, _, cols = left.shape
     piece_rows = keep.shape[1]
     for h in range(heads):
-        turned[...] = left[h].T
-        total = dot_nn(turned[...], right[h]).astype(BF16)
-        deal(chip, core, h * cols // piece_rows, keep, give, total, first)
+        total = lax.dot_general(
+            left[h], right[h], (((0,), (0,)), ((), ())), preferred_element_type=F32
+        )
+        deal(chip, core, h * cols // piece_rows, keep, give, total.astype(BF16), first)
 
 
 def front_kernel(
     place, x, og, wq, wk, wv, wo, qt, kt, vt, gt, keep, give, slab,
-    rows_x, rows_og, three_w, held_wo, both, turned, sems,
+    rows_x, rows_og, three_w, held_wo, both, sems,
 ):
     rows = x.shape[0]
     width = wq.shape[1]
@@ -122,24 +123,19 @@
             for h in range(width // HEAD_DIM):
                 first = t * width + h * HEAD_DIM
                 out[h, at, :] = three[first : first + HEAD_DIM]
-    scores(place[0], place[1], qt, kt, turned, keep, give, 0)
     in_og[0].wait()
     for r in range(rows):
         grad = dot_nt(held_wo[...], rows_og[r]).astype(BF16)
         at = slice(r * HEAD_DIM, (r + 1) * HEAD_DIM)
         for h in range(width // HEAD_DIM):
             gt[h, at, :] = grad[h * HEAD_DIM : (h + 1) * HEAD_DIM]
-    scores(place[0], place[1], gt, vt, turned, keep, give, kt.shape[2])
+    scores(place[0], place[1], qt, kt, keep, give, 0)
+    scores(place[0], place[1], gt, vt, keep, give, kt.shape[2])
 
 
 def pair_kernel(place, keep, got, *outs):
     for k in range(keep.shape[0]):
         outs[k][...] = (keep[k].astype(F32) + got[k].astype(F32)).astype(outs[k].dtype)
-
-
-def pair_pass_kernel(place, keep, got, slab, *outs):
-    pair_kernel(place, keep, got, *outs[:-1])
-    outs[-1][...] = slab[...]
 
 
 def join_kernel(place, *refs):
@@ -148,6 +144,17 @@
     for part in parts:
         out[at : at + part.shape[0]] = part[...]
         at += part.shape[0]
+
+
+def pair_pass_kernel(place, keep, got, slab, *refs):
+    *outs, passed = refs
+    halves = len(outs) // keep.shape[0]
+    rows = outs[0].shape[0]
+    for k in range(keep.shape[0]):
+        for j in range(halves):
+            at = slice(j * rows, (j + 1) * rows)
+            outs[k * halves + j][...] = (keep[k, at].astype(F32) + got[k, at].astype(F32)).astype(BF16)
+    passed[...] = slab[...]
 
 
 def pack_kernel(place, *refs):
@@ -181,23 +188,27 @@
     out[:, cols:] = (logit_scale * probs * (grad - inner)).astype(BF16)
 
 
-def assemble(place, mine, other, full):
+def assemble(place, mine, other, full, halves=1, half=0):
     piece_rows = mine[0].shape[0]
     for k in range(len(mine)):
         base = 2 * jnp.bitwise_xor(place[0], k)
         for side, part in ((place[1], mine[k]), (1 - place[1], other[k])):
-            at = pl.ds(pl.multiple_of((base + side) * piece_rows, piece_rows), piece_rows)
+            first = ((base + side) * halves + half) * piece_rows
+            at = pl.ds(pl.multiple_of(first, piece_rows), piece_rows)
             full[at, :] = part[0:piece_rows].astype(full.dtype)
 
 
-def grads_kernel(pieces, place, *refs):
-    mine, other = refs[0:pieces], refs[pieces : 2 * pieces]
-    qt, kt, vt, gt = refs[2 * pieces : 2 * pieces + 4]
-    send_far, att_far, full, send, att, sems = refs[2 * pieces + 4 :]
+def grads_kernel(pieces, halves, place, *refs):
+    count = pieces * halves
+    mine, other = refs[0:count], refs[count : 2 * count]
+    qt, kt, vt, gt = refs[2 * count : 2 * count + 4]
+    send_far, att_far, full, send, att, sems = refs[2 * count + 4 :]
     heads, _, cols = qt.shape
     zeds, width, tokens = att.shape
     block = cols // zeds
-    assemble(place, mine, other, full)
+    for j in range(halves):
+        each = slice(j * pieces, (j + 1) * pieces)
+        assemble(place, mine[each], other[each], full, halves, j)
     copies = []
     for h in range(heads):
         span = slice(h * cols, (h + 1) * cols)
@@ -400,42 +411,46 @@
             pltpu.VMEM((3, model, width), BF16),
             pltpu.VMEM((width, model), BF16),
             pltpu.VMEM((3 * width, model), BF16),
-            pltpu.VMEM((cols, merged), BF16),
             pltpu.SemaphoreType.DMA((3, max(4, rows))),
         ],
         flops=4 * dot_flops + 2 * score_flops,
         name="front",
     )
+    halves = 2 if shard % 32 == 0 else 1
     *paired, slab = call(
         pair_pass_kernel,
-        [shape(shard, 2 * cols)] * pieces + [shape(*slab.shape)],
+        [shape(shard // halves, 2 * cols)] * (pieces * halves) + [shape(*slab.shape)],
         (place, keep, swap(give), slab),
         name="pair_scores",
     )
-    parts = spread(paired)
+    parts = [spread(paired[j::halves]) for j in range(halves)]
     groups, span = [slab], 1
     while span < zeds:
         if span > 1:
             slab = call(join_kernel, shape(span, depth, 3 * width), (place, *groups), name="join")
         groups.append(along(slab, span))
         span *= 2
-    scored = call(
-        partial(score_kernel, logit_scale),
-        shape(shard, 2 * cols),
-        (place, *parts),
-        held=(slab,),
-        name="score",
-    )
+    mine, other = [], []
+    for j in range(halves):
+        scored = call(
+            partial(score_kernel, logit_scale),
+            shape(shard // halves, 2 * cols),
+            (place, *parts[j]),
+            held=(slab,) if j == 9 else (),
+            name="score",
+        )
+        near, far = gathered(scored, pieces)
+        mine += near
+        other += far
     swapped = [swap(group) for group in groups[1:]]
-    mine, other = gathered(scored, pieces)
     send, att = call(
-        partial(grads_kernel, pieces),
+        partial(grads_kernel, pieces, halves),
         (
             pltpu.HBM((zeds, 3 * width, rows * block), BF16),
             pltpu.HBM((zeds, width, rows * block), BF16),
         ),
         (place, *mine, *other, qt, kt, vt, gt),
-        held=swapped[1:] or swapped,
+        held=groups[1:],
         out_specs=(hbm_spec(), hbm_spec()),
         scratch=[
             pltpu.VMEM((heads * cols, 2 * cols), BF16),

time: 93.3 us -> 92 us (0.986)
  waiting for transfers between devices: 38.5 us -> 28 us
  starting transfers between devices: 26.5 us -> 35.2 us
    ppermute x12 -> x18, waiting for transfers between devices: 29.5 us -> 20.6 us  [across(): return lax.ppermute(value, 'seq', [(i, i ^ 2 * k) for i in range(seqs)])]
    ppermute x12 -> x18, starting transfers between devices: 15.1 us -> 23.8 us  [across(): return lax.ppermute(value, 'seq', [(i, i ^ 2 * k) for i in range(seqs)])]
    ppermute x2, waiting for transfers between devices: 2.33 us -> 0.01 us  [along(): return lax.ppermute(value, 'head', [(i, i ^ k) for i in range(zeds)])]
    ppermute x13 -> x17, starting transfers between devices: 1.83 us -> 2.91 us  [swap(): return lax.ppermute(value, 'seq', [(i, i ^ 1) for i in range(seqs)])]
    pallas_call x14 -> x15, Pallas kernels: 27.2 us -> 27.7 us  [call(): pl.pallas_call(run, out_shape=outs, in_specs=[smem_spec()] + [hbm_spec()]...]
    ppermute x13 -> x17, waiting for transfers between devices: 5.65 us -> 6.09 us  [swap(): return lax.ppermute(value, 'seq', [(i, i ^ 1) for i in range(seqs)])]
  transfers between devices with their start and end apart: 28 -> 38, of which waited for: 14 -> 18; matrix products, arithmetic and copies ran while one was open for 0% -> 0% of each run, Pallas kernels for 14% -> 16%
where the time goes in v6:
time: 92 us; the launch traced here: 91.8 us
  starting transfers between devices  35.2 us (38%)
  waiting for transfers between devices  28 us (30%)
  Pallas kernels  27.7 us (30%)
    pallas_call x15, Pallas kernels, call(): pl.pallas_call(run, out_shape=outs, in_specs=[smem_spec()] + [hbm_spec()]...  27.7 us
    ppermute x18, starting transfers between devices, across(): return lax.ppermute(value, 'seq', [(i, i ^ 2 * k) for i in range(seqs)])  23.8 us
    ppermute x18, waiting for transfers between devices, across(): return lax.ppermute(value, 'seq', [(i, i ^ 2 * k) for i in range(seqs)])  20.6 us
    ppermute x17, waiting for transfers between devices, swap(): return lax.ppermute(value, 'seq', [(i, i ^ 1) for i in range(seqs)])  6.09 us
    all_to_all x1, starting transfers between devices, body(): sent = lax.all_to_all(send, 'head', 0, 0, tiled=True)  4.35 us
    ppermute x2, starting transfers between devices, along(): return lax.ppermute(value, 'head', [(i, i ^ k) for i in range(zeds)])  4.17 us
    ppermute x17, starting transfers between devices, swap(): return lax.ppermute(value, 'seq', [(i, i ^ 1) for i in range(seqs)])  2.91 us
  transfers between devices with their start and end apart: 38, of which 18 were waited for; matrix products, arithmetic and copies ran while one was open for 0% of the time, Pallas kernels for 16%

profile of v6, /device:TPU:0, one launch (start us, length us, event | category | flops | bytes accessed | tf_op | source)
XLA Modules:
  0.0 91.8 jit_solution(17556751378519163142)
XLA Ops:
  0.7 5.8 %front.1 = (bf16[2,256,512]{2,1,0:T(8,128)(2,1)S(1)}, bf16[2,256,512]{2,1,0:T(8,128)(2,1)S(1)}, bf16[2,256,512]{2,1,0:T(8,128)(2,1)S(1)}, bf16[2,256,512]{2,1,0:...) custom-call(s32[4]{0:T(128)S(1)} %pad_add_fusion.refs_0_, ...), custom_call_target="tpu_custom_call" | custom-call | flops 2147483648 | tf_op jit(solution)/shard_map/front/pallas_call | solution.py:49
  7.0 2.3 %collective-permute-done.refs_2_ = bf16[4,128,1024]{2,1,0:T(8,128)(2,1)S(1)} collective-permute-done((bf16[4,128,1024]{2,1,0:T(8,128)(2,1)S(1)}, bf16[4,128,1024]{2,1,0:T(8,128)(2,1)S(1)}, u32[]{:S(2)}, u32[]{:S(2)}) %collective-permute-start) | collective-permute-done | bytes 1048608 | tf_op jit(solution)/shard_map/ppermute | solution.py:379
  10.1 2.9 %collective-permute-start.1 = (bf16[64,1024]{1,0:T(8,128)(2,1)S(1)}, bf16[64,1024]{1,0:T(8,128)(2,1)S(1)}, u32[]{:S(2)}, u32[]{:S(2)}) collective-permute-start(bf16[64,1024]{1,0:T(8,128)(2,1)S(1)} %get-tuple-element.42), channel_id=1, source_target_pairs={{0,8},{4,12},{8,0},{12,4},{16,24},{20,28},{24,16},{28,20},{1,9},{5... | collective-permute-start | bytes 393224 | tf_op jit(solution)/shard_map/ppermute | solution.py:382
  13.0 1.6 %collective-permute-start.21 = (bf16[1,96,384]{2,1,0:T(8,128)(2,1)S(1)}, bf16[1,96,384]{2,1,0:T(8,128)(2,1)S(1)}, u32[]{:S(2)}, u32[]{:S(2)}) collective-permute-start(bf16[1,96,384]{2,1,0:T(8,128)(2,1)S(1)} %get-tuple-element.53.refs_1_), channel_id=1, source_target_pairs={{0,1},{1,0},{2,3},{3,2},{4,5},{5,4},{6,7},{7,6},{8,9},{9,8},{10,11... | collective-permute-start | bytes 221192 | tf_op jit(solution)/shard_map/ppermute | solution.py:385
  14.6 1.5 %collective-permute-start.2 = (bf16[64,1024]{1,0:T(8,128)(2,1)S(1)}, bf16[64,1024]{1,0:T(8,128)(2,1)S(1)}, u32[]{:S(2)}, u32[]{:S(2)}) collective-permute-start(bf16[64,1024]{1,0:T(8,128)(2,1)S(1)} %get-tuple-element.43), channel_id=1, source_target_pairs={{0,16},{4,20},{8,24},{12,28},{16,0},{20,4},{24,8},{28,12},{1,17},{... | collective-permute-start | bytes 393224 | tf_op jit(solution)/shard_map/ppermute | solution.py:382
  16.6 1.5 %collective-permute-start.7 = (bf16[64,1024]{1,0:T(8,128)(2,1)S(1)}, bf16[64,1024]{1,0:T(8,128)(2,1)S(1)}, u32[]{:S(2)}, u32[]{:S(2)}) collective-permute-start(bf16[64,1024]{1,0:T(8,128)(2,1)S(1)} %get-tuple-element.46), channel_id=1, source_target_pairs={{0,8},{4,12},{8,0},{12,4},{16,24},{20,28},{24,16},{28,20},{1,9},{5... | collective-permute-start | bytes 393224 | tf_op jit(solution)/shard_map/ppermute | solution.py:382
  18.1 1.5 %collective-permute-start.8 = (bf16[64,1024]{1,0:T(8,128)(2,1)S(1)}, bf16[64,1024]{1,0:T(8,128)(2,1)S(1)}, u32[]{:S(2)}, u32[]{:S(2)}) collective-permute-start(bf16[64,1024]{1,0:T(8,128)(2,1)S(1)} %get-tuple-element.47), channel_id=1, source_target_pairs={{0,16},{4,20},{8,24},{12,28},{16,0},{20,4},{24,8},{28,12},{1,17},{... | collective-permute-start | bytes 393224 | tf_op jit(solution)/shard_map/ppermute | solution.py:382
  20.7 3.3 %collective-permute-done.2.refs_3_ = bf16[64,1024]{1,0:T(8,128)(2,1)S(1)} collective-permute-done((bf16[64,1024]{1,0:T(8,128)(2,1)S(1)}, bf16[64,1024]{1,0:T(8,128)(2,1)S(1)}, u32[]{:S(2)}, u32[]{:S(2)}) %collective-permute-start.2) | collective-permute-done | bytes 131104 | tf_op jit(solution)/shard_map/ppermute | solution.py:382
  24.0 2.6 %collective-permute-start.22 = (bf16[2,96,384]{2,1,0:T(8,128)(2,1)S(1)}, bf16[2,96,384]{2,1,0:T(8,128)(2,1)S(1)}, u32[]{:S(2)}, u32[]{:S(2)}) collective-permute-start(bf16[2,96,384]{2,1,0:T(8,128)(2,1)S(1)} %join.1), channel_id=1, source_target_pairs={{0,2},{1,3},{2,0},{3,1},{4,6},{5,7},{6,4},{7,5},{8,10},{9,11},{10,... | collective-permute-start | bytes 442376 | tf_op jit(solution)/shard_map/ppermute | solution.py:385
  28.0 2.7 %collective-permute-start.5 = (bf16[64,1024]{1,0:T(8,128)(2,1)S(1)}, bf16[64,1024]{1,0:T(8,128)(2,1)S(1)}, u32[]{:S(2)}, u32[]{:S(2)}) collective-permute-start(bf16[64,1024]{1,0:T(8,128)(2,1)S(1)} %score.2.refs_1_), channel_id=1, source_target_pairs={{0,16},{4,20},{8,24},{12,28},{16,0},{20,4},{24,8},{28,12},{1,17},{... | collective-permute-start | bytes 393224 | tf_op jit(solution)/shard_map/ppermute | solution.py:382
  30.6 0.9 %collective-permute-start.6 = (bf16[64,1024]{1,0:T(8,128)(2,1)S(1)}, bf16[64,1024]{1,0:T(8,128)(2,1)S(1)}, u32[]{:S(2)}, u32[]{:S(2)}) collective-permute-start(bf16[64,1024]{1,0:T(8,128)(2,1)S(1)} %score.2.refs_1_), channel_id=1, source_target_pairs={{0,24},{4,28},{8,16},{12,20},{16,8},{20,12},{24,0},{28,4},{1,25},{... | collective-permute-start | bytes 393224 | tf_op jit(solution)/shard_map/ppermute | solution.py:382
  33.0 2.0 %collective-permute-start.11 = (bf16[64,1024]{1,0:T(8,128)(2,1)S(1)}, bf16[64,1024]{1,0:T(8,128)(2,1)S(1)}, u32[]{:S(2)}, u32[]{:S(2)}) collective-permute-start(bf16[64,1024]{1,0:T(8,128)(2,1)S(1)} %score.3.refs_5_), channel_id=1, source_target_pairs={{0,16},{4,20},{8,24},{12,28},{16,0},{20,4},{24,8},{28,12},{1,17},{... | collective-permute-start | bytes 393224 | tf_op jit(solution)/shard_map/ppermute | solution.py:382
  34.9 1.4 %collective-permute-start.12 = (bf16[64,1024]{1,0:T(8,128)(2,1)S(1)}, bf16[64,1024]{1,0:T(8,128)(2,1)S(1)}, u32[]{:S(2)}, u32[]{:S(2)}) collective-permute-start(bf16[64,1024]{1,0:T(8,128)(2,1)S(1)} %score.3.refs_5_), channel_id=1, source_target_pairs={{0,24},{4,28},{8,16},{12,20},{16,8},{20,12},{24,0},{28,4},{1,25},{... | collective-permute-start | bytes 393224 | tf_op jit(solution)/shard_map/ppermute | solution.py:382
  36.4 1.1 %collective-permute-done.6.refs_4_ = bf16[64,1024]{1,0:T(8,128)(2,1)S(1)} collective-permute-done((bf16[64,1024]{1,0:T(8,128)(2,1)S(1)}, bf16[64,1024]{1,0:T(8,128)(2,1)S(1)}, u32[]{:S(2)}, u32[]{:S(2)}) %collective-permute-start.6) | collective-permute-done | bytes 131104 | tf_op jit(solution)/shard_map/ppermute | solution.py:382
  38.0 0.8 collective-permute-done.11.refs_7_
  38.8 2.0 %collective-permute-done.12.refs_8_ = bf16[64,1024]{1,0:T(8,128)(2,1)S(1)} collective-permute-done((bf16[64,1024]{1,0:T(8,128)(2,1)S(1)}, bf16[64,1024]{1,0:T(8,128)(2,1)S(1)}, u32[]{:S(2)}, u32[]{:S(2)}) %collective-permute-start.12) | collective-permute-done | bytes 131104 | tf_op jit(solution)/shard_map/ppermute | solution.py:382
  42.9 2.8 %grads.1 = (bf16[4,384,512]{2,1,0:T(8,128)(2,1)}, bf16[4,128,512]{2,1,0:T(8,128)(2,1)}) custom-call(s32[4]{0:T(128)S(1)} %pad_add_fusion.refs_0_, bf16[64,1024]{1,0:T(8,128)(2,1)S(1)} %score.2.refs_1_, bf16[64,1024]{1,0:T(8,128)(2,1)S(1)} %collective-permute-done.4.refs_2_, bf16[64,1024]{1,0:T(8,128)(2,1)S(1)} %collective-permute-done.5.refs_3_, ...), custom_call_target="tpu_custom_call" | custom-call | flops 1073741824 | tf_op jit(solution)/shard_map/grads/pallas_call | solution.py:49
  45.7 4.4 %all-to-all-start = ((bf16[4,384,512]{2,1,0:T(8,128)(2,1)}), bf16[4,384,512]{2,1,0:T(8,128)(2,1)}, u32[]{:S(2)}, u32[]{:S(2)}) async-start(bf16[4,384,512]{2,1,0:T(8,128)(2,1)} %get-tuple-element.54.refs_1_.refs_3_), calls=%async_computation | async-start | bytes 3145728 | tf_op jit(solution)/shard_map/all_to_all | solution.py:477
  50.0 4.9 %weights.1 = (bf16[4,64,768]{2,1,0:T(8,128)(2,1)S(1)}, bf16[4,64,768]{2,1,0:T(8,128)(2,1)S(1)}) custom-call(s32[4]{0:T(128)S(1)} %pad_add_fusion.refs_0_, bf16[4,512,768]{2,1,0:T(8,128)(2,1)} %refs_1_.3, bf16[4,512,768]{2,1,0:T(8,128)(2,1)} %refs_2_.5, bf16[4,384,512]{2,1,0:T(8,128)(2,1)} %get-tuple-element.54.refs_1_.refs_3_, ...), custom_call_target="tpu_custom_call" | custom-call | flops 1610612736 | bytes 6291456 | tf_op jit(solution)/shard_map/weights/pallas_call | solution.py:49
  55.9 0.8 collective-permute-done.25.refs_2_
  57.4 1.5 %collective-permute-start.26 = (bf16[208,768]{1,0:T(8,128)(2,1)S(1)}, bf16[208,768]{1,0:T(8,128)(2,1)S(1)}, u32[]{:S(2)}, u32[]{:S(2)}) collective-permute-start(bf16[208,768]{1,0:T(8,128)(2,1)S(1)} %get-tuple-element.59), channel_id=1, source_target_pairs={{0,8},{4,12},{8,0},{12,4},{16,24},{20,28},{24,16},{28,20},{1,9},{5... | collective-permute-start | bytes 958472 | tf_op jit(solution)/shard_map/ppermute | solution.py:382
  59.4 1.5 %collective-permute-start.28 = (bf16[64,768]{1,0:T(8,128)(2,1)S(1)}, bf16[64,768]{1,0:T(8,128)(2,1)S(1)}, u32[]{:S(2)}, u32[]{:S(2)}) collective-permute-start(bf16[64,768]{1,0:T(8,128)(2,1)S(1)} %get-tuple-element.61), channel_id=1, source_target_pairs={{0,24},{4,28},{8,16},{12,20},{16,8},{20,12},{24,0},{28,4},{1,25},{... | collective-permute-start | bytes 294920 | tf_op jit(solution)/shard_map/ppermute | solution.py:382
  60.9 2.3 %own_inputs.1.refs_6_.refs_2_ = f32[768,512]{1,0:T(8,128)S(1)} custom-call(s32[4]{0:T(128)S(1)} %pad_add_fusion.refs_0_, bf16[4,384,512]{2,1,0:T(8,128)(2,1)} %get-tuple-element.54.refs_1_.refs_3_, bf16[768,128]{1,0:T(8,128)(2,1)} %refs_2_.4, bf16[768,128]{1,0:T(8,128)(2,1)} %refs_3_.3, bf16[768,128]{1,0:T(8,128)(2,1)} %refs_4_.3), custom_call_target="tpu_custom_call" | custom-call | flops 301989888 | tf_op jit(solution)/shard_map/own_inputs/pallas_call | solution.py:49
  63.3 6.5 %collective-permute-done.28.refs_5_ = bf16[64,768]{1,0:T(8,128)(2,1)S(1)} collective-permute-done((bf16[64,768]{1,0:T(8,128)(2,1)S(1)}, bf16[64,768]{1,0:T(8,128)(2,1)S(1)}, u32[]{:S(2)}, u32[]{:S(2)}) %collective-permute-start.28) | collective-permute-done | bytes 98336 | tf_op jit(solution)/shard_map/ppermute | solution.py:382
  71.8 1.1 %collective-permute-start.31 = (bf16[112,768]{1,0:T(8,128)(2,1)S(1)}, bf16[112,768]{1,0:T(8,128)(2,1)S(1)}, u32[]{:S(2)}, u32[]{:S(2)}) collective-permute-start(bf16[112,768]{1,0:T(8,128)(2,1)S(1)} %get-tuple-element.64), channel_id=1, source_target_pairs={{0,16},{4,20},{8,24},{12,28},{16,0},{20,4},{24,8},{28,12},{1,17},{... | collective-permute-start | bytes 516104 | tf_op jit(solution)/shard_map/ppermute | solution.py:382
  73.0 1.7 %collective-permute-start.32 = (bf16[112,768]{1,0:T(8,128)(2,1)S(1)}, bf16[112,768]{1,0:T(8,128)(2,1)S(1)}, u32[]{:S(2)}, u32[]{:S(2)}) collective-permute-start(bf16[112,768]{1,0:T(8,128)(2,1)S(1)} %get-tuple-element.65), channel_id=1, source_target_pairs={{0,24},{4,28},{8,16},{12,20},{16,8},{20,12},{24,0},{28,4},{1,25},{... | collective-permute-start | bytes 516104 | tf_op jit(solution)/shard_map/ppermute | solution.py:382
  74.7 1.3 %collective-permute-done.23.refs_1_ = bf16[1,96,384]{2,1,0:T(8,128)(2,1)S(1)} collective-permute-done((bf16[1,96,384]{2,1,0:T(8,128)(2,1)S(1)}, bf16[1,96,384]{2,1,0:T(8,128)(2,1)S(1)}, u32[]{:S(2)}, u32[]{:S(2)}) %collective-permute-start.23) | collective-permute-done | bytes 73760 | tf_op jit(solution)/shard_map/ppermute | solution.py:379
  76.1 2.3 %collective-permute-done.30.refs_5_.refs_2_ = bf16[112,768]{1,0:T(8,128)(2,1)S(1)} collective-permute-done((bf16[112,768]{1,0:T(8,128)(2,1)S(1)}, bf16[112,768]{1,0:T(8,128)(2,1)S(1)}, u32[]{:S(2)}, u32[]{:S(2)}) %collective-permute-start.30) | collective-permute-done | bytes 172064 | tf_op jit(solution)/shard_map/ppermute | solution.py:382
  78.4 3.6 %collective-permute-done.31.refs_6_.refs_3_ = bf16[112,768]{1,0:T(8,128)(2,1)S(1)} collective-permute-done((bf16[112,768]{1,0:T(8,128)(2,1)S(1)}, bf16[112,768]{1,0:T(8,128)(2,1)S(1)}, u32[]{:S(2)}, u32[]{:S(2)}) %collective-permute-start.31) | collective-permute-done | bytes 172064 | tf_op jit(solution)/shard_map/ppermute | solution.py:382
  83.8 2.0 %unpack.1 = (f32[768,128]{1,0:T(8,128)}, f32[768,128]{1,0:T(8,128)}, f32[768,128]{1,0:T(8,128)}, f32[128,768]{1,0:T(8,128)}) custom-call(s32[4]{0:T(128)S(1)} %pad_add_fusion.refs_0_, bf16[64,768]{1,0:T(8,128)(2,1)S(1)} %get-tuple-element.66.refs_1_, bf16[112,768]{1,0:T(8,128)(2,1)S(1)} %collective-permute-done.30.refs_5_.refs_2_, ...), custom_call_target="tpu_custom_call" | custom-call | tf_op jit(solution)/shard_map/unpack/pallas_call | solution.py:49
  86.5 1.3 %all-to-all-done.refs_1_ = bf16[4,384,512]{2,1,0:T(8,128)(2,1)} async-done(((bf16[4,384,512]{2,1,0:T(8,128)(2,1)}), bf16[4,384,512]{2,1,0:T(8,128)(2,1)}, u32[]{:S(2)}, u32[]{:S(2)}) %all-to-all-start) | async-done | bytes 1572896 | tf_op jit(solution)/shard_map/all_to_all | solution.py:477
  87.8 4.0 %inputs.1 = bf16[4,128,768]{2,1,0:T(8,128)(2,1)} custom-call(s32[4]{0:T(128)S(1)} %pad_add_fusion.refs_0_, bf16[4,384,512]{2,1,0:T(8,128)(2,1)} %all-to-all-done.refs_1_, f32[768,512]{1,0:T(8,128)S(1)} %own_inputs.1.refs_6_.refs_2_, bf16[768,1152]{1,0:T(8,128)(2,1)S(1)} %gather_weights.1.refs_3_), custom_call_target="tpu_custom_call" | custom-call | flops 905969664 | tf_op jit(solution)/shard_map/inputs/pallas_call | solution.py:49
  (60 shorter events, 15.2 us)
Async XLA Ops:
  6.5 2.8 %collective-permute-start = (bf16[4,128,1024]{2,1,0:T(8,128)(2,1)S(1)}, bf16[4,128,1024]{2,1,0:T(8,128)(2,1)S(1)}, u32[]{:S(2)}, u32[]{:S(2)}) collective-permute-start(bf16[4,128,1024]{2,1,0:T(8,128)(2,1)S(1)} %get-tuple-element.39), channel_id=1, source_target_pairs={{0,4},{4,0},{8,12},{12,8},{16,20},{20,16},{24,28},{28,24},{1,5},{5... | collective-permute-start | bytes 3145736 | tf_op jit(solution)/shard_map/ppermute | solution.py:379
  10.1 9.5 %collective-permute-start.1 = (bf16[64,1024]{1,0:T(8,128)(2,1)S(1)}, bf16[64,1024]{1,0:T(8,128)(2,1)S(1)}, u32[]{:S(2)}, u32[]{:S(2)}) collective-permute-start(bf16[64,1024]{1,0:T(8,128)(2,1)S(1)} %get-tuple-element.42), channel_id=1, source_target_pairs={{0,8},{4,12},{8,0},{12,4},{16,24},{20,28},{24,16},{28,20},{1,9},{5... | collective-permute-start | bytes 393224 | tf_op jit(solution)/shard_map/ppermute | solution.py:382
  13.0 5.1 %collective-permute-start.21 = (bf16[1,96,384]{2,1,0:T(8,128)(2,1)S(1)}, bf16[1,96,384]{2,1,0:T(8,128)(2,1)S(1)}, u32[]{:S(2)}, u32[]{:S(2)}) collective-permute-start(bf16[1,96,384]{2,1,0:T(8,128)(2,1)S(1)} %get-tuple-element.53.refs_1_), channel_id=1, source_target_pairs={{0,1},{1,0},{2,3},{3,2},{4,5},{5,4},{6,7},{7,6},{8,9},{9,8},{10,11... | collective-permute-start | bytes 221192 | tf_op jit(solution)/shard_map/ppermute | solution.py:385
  14.6 9.4 %collective-permute-start.2 = (bf16[64,1024]{1,0:T(8,128)(2,1)S(1)}, bf16[64,1024]{1,0:T(8,128)(2,1)S(1)}, u32[]{:S(2)}, u32[]{:S(2)}) collective-permute-start(bf16[64,1024]{1,0:T(8,128)(2,1)S(1)} %get-tuple-element.43), channel_id=1, source_target_pairs={{0,16},{4,20},{8,24},{12,28},{16,0},{20,4},{24,8},{28,12},{1,17},{... | collective-permute-start | bytes 393224 | tf_op jit(solution)/shard_map/ppermute | solution.py:382
  16.1 10.4 %collective-permute-start.3 = (bf16[64,1024]{1,0:T(8,128)(2,1)S(1)}, bf16[64,1024]{1,0:T(8,128)(2,1)S(1)}, u32[]{:S(2)}, u32[]{:S(2)}) collective-permute-start(bf16[64,1024]{1,0:T(8,128)(2,1)S(1)} %get-tuple-element.44), channel_id=1, source_target_pairs={{0,24},{4,28},{8,16},{12,20},{16,8},{20,12},{24,0},{28,4},{1,25},{... | collective-permute-start | bytes 393224 | tf_op jit(solution)/shard_map/ppermute | solution.py:382
  16.6 11.4 %collective-permute-start.7 = (bf16[64,1024]{1,0:T(8,128)(2,1)S(1)}, bf16[64,1024]{1,0:T(8,128)(2,1)S(1)}, u32[]{:S(2)}, u32[]{:S(2)}) collective-permute-start(bf16[64,1024]{1,0:T(8,128)(2,1)S(1)} %get-tuple-element.46), channel_id=1, source_target_pairs={{0,8},{4,12},{8,0},{12,4},{16,24},{20,28},{24,16},{28,20},{1,9},{5... | collective-permute-start | bytes 393224 | tf_op jit(solution)/shard_map/ppermute | solution.py:382
  18.1 12.5 %collective-permute-start.8 = (bf16[64,1024]{1,0:T(8,128)(2,1)S(1)}, bf16[64,1024]{1,0:T(8,128)(2,1)S(1)}, u32[]{:S(2)}, u32[]{:S(2)}) collective-permute-start(bf16[64,1024]{1,0:T(8,128)(2,1)S(1)} %get-tuple-element.47), channel_id=1, source_target_pairs={{0,16},{4,20},{8,24},{12,28},{16,0},{20,4},{24,8},{28,12},{1,17},{... | collective-permute-start | bytes 393224 | tf_op jit(solution)/shard_map/ppermute | solution.py:382
  19.6 11.9 %collective-permute-start.9 = (bf16[64,1024]{1,0:T(8,128)(2,1)S(1)}, bf16[64,1024]{1,0:T(8,128)(2,1)S(1)}, u32[]{:S(2)}, u32[]{:S(2)}) collective-permute-start(bf16[64,1024]{1,0:T(8,128)(2,1)S(1)} %get-tuple-element.48), channel_id=1, source_target_pairs={{0,24},{4,28},{8,16},{12,20},{16,8},{20,12},{24,0},{28,4},{1,25},{... | collective-permute-start | bytes 393224 | tf_op jit(solution)/shard_map/ppermute | solution.py:382
  24.0 9.0 %collective-permute-start.22 = (bf16[2,96,384]{2,1,0:T(8,128)(2,1)S(1)}, bf16[2,96,384]{2,1,0:T(8,128)(2,1)S(1)}, u32[]{:S(2)}, u32[]{:S(2)}) collective-permute-start(bf16[2,96,384]{2,1,0:T(8,128)(2,1)S(1)} %join.1), channel_id=1, source_target_pairs={{0,2},{1,3},{2,0},{3,1},{4,6},{5,7},{6,4},{7,5},{8,10},{9,11},{10,... | collective-permute-start | bytes 442376 | tf_op jit(solution)/shard_map/ppermute | solution.py:385
  27.3 7.6 %collective-permute-start.4 = (bf16[64,1024]{1,0:T(8,128)(2,1)S(1)}, bf16[64,1024]{1,0:T(8,128)(2,1)S(1)}, u32[]{:S(2)}, u32[]{:S(2)}) collective-permute-start(bf16[64,1024]{1,0:T(8,128)(2,1)S(1)} %score.2.refs_1_), channel_id=1, source_target_pairs={{0,8},{4,12},{8,0},{12,4},{16,24},{20,28},{24,16},{28,20},{1,9},{5... | collective-permute-start | bytes 393224 | tf_op jit(solution)/shard_map/ppermute | solution.py:382
  28.0 8.4 %collective-permute-start.5 = (bf16[64,1024]{1,0:T(8,128)(2,1)S(1)}, bf16[64,1024]{1,0:T(8,128)(2,1)S(1)}, u32[]{:S(2)}, u32[]{:S(2)}) collective-permute-start(bf16[64,1024]{1,0:T(8,128)(2,1)S(1)} %score.2.refs_1_), channel_id=1, source_target_pairs={{0,16},{4,20},{8,24},{12,28},{16,0},{20,4},{24,8},{28,12},{1,17},{... | collective-permute-start | bytes 393224 | tf_op jit(solution)/shard_map/ppermute | solution.py:382
  30.6 6.9 %collective-permute-start.6 = (bf16[64,1024]{1,0:T(8,128)(2,1)S(1)}, bf16[64,1024]{1,0:T(8,128)(2,1)S(1)}, u32[]{:S(2)}, u32[]{:S(2)}) collective-permute-start(bf16[64,1024]{1,0:T(8,128)(2,1)S(1)} %score.2.refs_1_), channel_id=1, source_target_pairs={{0,24},{4,28},{8,16},{12,20},{16,8},{20,12},{24,0},{28,4},{1,25},{... | collective-permute-start | bytes 393224 | tf_op jit(solution)/shard_map/ppermute | solution.py:382
  32.3 5.5 %collective-permute-start.10 = (bf16[64,1024]{1,0:T(8,128)(2,1)S(1)}, bf16[64,1024]{1,0:T(8,128)(2,1)S(1)}, u32[]{:S(2)}, u32[]{:S(2)}) collective-permute-start(bf16[64,1024]{1,0:T(8,128)(2,1)S(1)} %score.3.refs_5_), channel_id=1, source_target_pairs={{0,8},{4,12},{8,0},{12,4},{16,24},{20,28},{24,16},{28,20},{1,9},{5... | collective-permute-start | bytes 393224 | tf_op jit(solution)/shard_map/ppermute | solution.py:382
  33.0 5.8 %collective-permute-start.11 = (bf16[64,1024]{1,0:T(8,128)(2,1)S(1)}, bf16[64,1024]{1,0:T(8,128)(2,1)S(1)}, u32[]{:S(2)}, u32[]{:S(2)}) collective-permute-start(bf16[64,1024]{1,0:T(8,128)(2,1)S(1)} %score.3.refs_5_), channel_id=1, source_target_pairs={{0,16},{4,20},{8,24},{12,28},{16,0},{20,4},{24,8},{28,12},{1,17},{... | collective-permute-start | bytes 393224 | tf_op jit(solution)/shard_map/ppermute | solution.py:382
  34.9 5.9 %collective-permute-start.12 = (bf16[64,1024]{1,0:T(8,128)(2,1)S(1)}, bf16[64,1024]{1,0:T(8,128)(2,1)S(1)}, u32[]{:S(2)}, u32[]{:S(2)}) collective-permute-start(bf16[64,1024]{1,0:T(8,128)(2,1)S(1)} %score.3.refs_5_), channel_id=1, source_target_pairs={{0,24},{4,28},{8,16},{12,20},{16,8},{20,12},{24,0},{28,4},{1,25},{... | collective-permute-start | bytes 393224 | tf_op jit(solution)/shard_map/ppermute | solution.py:382
  36.4 4.4 %collective-permute-start.13 = (bf16[64,1024]{1,0:T(8,128)(2,1)S(1)}, bf16[64,1024]{1,0:T(8,128)(2,1)S(1)}, u32[]{:S(2)}, u32[]{:S(2)}) collective-permute-start(bf16[64,1024]{1,0:T(8,128)(2,1)S(1)} %score.2.refs_1_), channel_id=1, source_target_pairs={{0,4},{4,0},{8,12},{12,8},{16,20},{20,16},{24,28},{28,24},{1,5},{5... | collective-permute-start | bytes 393224 | tf_op jit(solution)/shard_map/ppermute | solution.py:379
  37.5 3.9 %collective-permute-start.17 = (bf16[64,1024]{1,0:T(8,128)(2,1)S(1)}, bf16[64,1024]{1,0:T(8,128)(2,1)S(1)}, u32[]{:S(2)}, u32[]{:S(2)}) collective-permute-start(bf16[64,1024]{1,0:T(8,128)(2,1)S(1)} %score.3.refs_5_), channel_id=1, source_target_pairs={{0,4},{4,0},{8,12},{12,8},{16,20},{20,16},{24,28},{28,24},{1,5},{5... | collective-permute-start | bytes 393224 | tf_op jit(solution)/shard_map/ppermute | solution.py:379
  37.8 3.6 %collective-permute-start.14 = (bf16[64,1024]{1,0:T(8,128)(2,1)S(1)}, bf16[64,1024]{1,0:T(8,128)(2,1)S(1)}, u32[]{:S(2)}, u32[]{:S(2)}) collective-permute-start(bf16[64,1024]{1,0:T(8,128)(2,1)S(1)} %collective-permute-done.4.refs_2_), channel_id=1, source_target_pairs={{0,4},{4,0},{8,12},{12,8},{16,20},{20,16},{24,28},{28,24},{1,5},{5... | collective-permute-start | bytes 393224 | tf_op jit(solution)/shard_map/ppermute | solution.py:379
  38.8 3.0 %collective-permute-start.15 = (bf16[64,1024]{1,0:T(8,128)(2,1)S(1)}, bf16[64,1024]{1,0:T(8,128)(2,1)S(1)}, u32[]{:S(2)}, u32[]{:S(2)}) collective-permute-start(bf16[64,1024]{1,0:T(8,128)(2,1)S(1)} %collective-permute-done.5.refs_3_), channel_id=1, source_target_pairs={{0,4},{4,0},{8,12},{12,8},{16,20},{20,16},{24,28},{28,24},{1,5},{5... | collective-permute-start | bytes 393224 | tf_op jit(solution)/shard_map/ppermute | solution.py:379
  45.7 42.1 %all-to-all-start = ((bf16[4,384,512]{2,1,0:T(8,128)(2,1)}), bf16[4,384,512]{2,1,0:T(8,128)(2,1)}, u32[]{:S(2)}, u32[]{:S(2)}) async-start(bf16[4,384,512]{2,1,0:T(8,128)(2,1)} %get-tuple-element.54.refs_1_.refs_3_), calls=%async_computation | async-start | bytes 3145728 | tf_op jit(solution)/shard_map/all_to_all | solution.py:477
  54.9 1.8 %collective-permute-start.25 = (bf16[4,64,768]{2,1,0:T(8,128)(2,1)S(1)}, bf16[4,64,768]{2,1,0:T(8,128)(2,1)S(1)}, u32[]{:S(2)}, u32[]{:S(2)}) collective-permute-start(bf16[4,64,768]{2,1,0:T(8,128)(2,1)S(1)} %get-tuple-element.57), channel_id=1, source_target_pairs={{0,4},{4,0},{8,12},{12,8},{16,20},{20,16},{24,28},{28,24},{1,5},{5... | collective-permute-start | bytes 1179656 | tf_op jit(solution)/shard_map/ppermute | solution.py:379
  57.4 12.5 %collective-permute-start.26 = (bf16[208,768]{1,0:T(8,128)(2,1)S(1)}, bf16[208,768]{1,0:T(8,128)(2,1)S(1)}, u32[]{:S(2)}, u32[]{:S(2)}) collective-permute-start(bf16[208,768]{1,0:T(8,128)(2,1)S(1)} %get-tuple-element.59), channel_id=1, source_target_pairs={{0,8},{4,12},{8,0},{12,4},{16,24},{20,28},{24,16},{28,20},{1,9},{5... | collective-permute-start | bytes 958472 | tf_op jit(solution)/shard_map/ppermute | solution.py:382
  58.9 11.6 %collective-permute-start.27 = (bf16[208,768]{1,0:T(8,128)(2,1)S(1)}, bf16[208,768]{1,0:T(8,128)(2,1)S(1)}, u32[]{:S(2)}, u32[]{:S(2)}) collective-permute-start(bf16[208,768]{1,0:T(8,128)(2,1)S(1)} %get-tuple-element.60), channel_id=1, source_target_pairs={{0,16},{4,20},{8,24},{12,28},{16,0},{20,4},{24,8},{28,12},{1,17},{... | collective-permute-start | bytes 958472 | tf_op jit(solution)/shard_map/ppermute | solution.py:382
  59.4 10.4 %collective-permute-start.28 = (bf16[64,768]{1,0:T(8,128)(2,1)S(1)}, bf16[64,768]{1,0:T(8,128)(2,1)S(1)}, u32[]{:S(2)}, u32[]{:S(2)}) collective-permute-start(bf16[64,768]{1,0:T(8,128)(2,1)S(1)} %get-tuple-element.61), channel_id=1, source_target_pairs={{0,24},{4,28},{8,16},{12,20},{16,8},{20,12},{24,0},{28,4},{1,25},{... | collective-permute-start | bytes 294920 | tf_op jit(solution)/shard_map/ppermute | solution.py:382
  71.1 14.7 %collective-permute-start.29 = (bf16[2,144,768]{2,1,0:T(8,128)(2,1)S(1)}, bf16[2,144,768]{2,1,0:T(8,128)(2,1)S(1)}, u32[]{:S(2)}, u32[]{:S(2)}) collective-permute-start(bf16[2,144,768]{2,1,0:T(8,128)(2,1)S(1)} %get-tuple-element.62.refs_3_), channel_id=1, source_target_pairs={{0,4},{4,0},{8,12},{12,8},{16,20},{20,16},{24,28},{28,24},{1,5},{5... | collective-permute-start | bytes 1327112 | tf_op jit(solution)/shard_map/ppermute | solution.py:379
  71.2 7.2 %collective-permute-start.30 = (bf16[112,768]{1,0:T(8,128)(2,1)S(1)}, bf16[112,768]{1,0:T(8,128)(2,1)S(1)}, u32[]{:S(2)}, u32[]{:S(2)}) collective-permute-start(bf16[112,768]{1,0:T(8,128)(2,1)S(1)} %get-tuple-element.63), channel_id=1, source_target_pairs={{0,8},{4,12},{8,0},{12,4},{16,24},{20,28},{24,16},{28,20},{1,9},{5... | collective-permute-start | bytes 516104 | tf_op jit(solution)/shard_map/ppermute | solution.py:382
  71.8 10.1 %collective-permute-start.31 = (bf16[112,768]{1,0:T(8,128)(2,1)S(1)}, bf16[112,768]{1,0:T(8,128)(2,1)S(1)}, u32[]{:S(2)}, u32[]{:S(2)}) collective-permute-start(bf16[112,768]{1,0:T(8,128)(2,1)S(1)} %get-tuple-element.64), channel_id=1, source_target_pairs={{0,16},{4,20},{8,24},{12,28},{16,0},{20,4},{24,8},{28,12},{1,17},{... | collective-permute-start | bytes 516104 | tf_op jit(solution)/shard_map/ppermute | solution.py:382
  73.0 9.0 %collective-permute-start.32 = (bf16[112,768]{1,0:T(8,128)(2,1)S(1)}, bf16[112,768]{1,0:T(8,128)(2,1)S(1)}, u32[]{:S(2)}, u32[]{:S(2)}) collective-permute-start(bf16[112,768]{1,0:T(8,128)(2,1)S(1)} %get-tuple-element.65), channel_id=1, source_target_pairs={{0,24},{4,28},{8,16},{12,20},{16,8},{20,12},{24,0},{28,4},{1,25},{... | collective-permute-start | bytes 516104 | tf_op jit(solution)/shard_map/ppermute | solution.py:382
  76.0 6.5 %collective-permute-start.24 = (bf16[2,96,384]{2,1,0:T(8,128)(2,1)S(1)}, bf16[2,96,384]{2,1,0:T(8,128)(2,1)S(1)}, u32[]{:S(2)}, u32[]{:S(2)}) collective-permute-start(bf16[2,96,384]{2,1,0:T(8,128)(2,1)S(1)} %collective-permute-done.22.refs_22_.refs_2_), channel_id=1, source_target_pairs={{0,4},{4,0},{8,12},{12,8},{16,20},{20,16},{24,28},{28,24},{1,5},{5... | collective-permute-start | bytes 442376 | tf_op jit(solution)/shard_map/ppermute | solution.py:379
  78.4 5.4 %collective-permute-start.33 = (bf16[112,768]{1,0:T(8,128)(2,1)S(1)}, bf16[112,768]{1,0:T(8,128)(2,1)S(1)}, u32[]{:S(2)}, u32[]{:S(2)}) collective-permute-start(bf16[112,768]{1,0:T(8,128)(2,1)S(1)} %collective-permute-done.30.refs_5_.refs_2_), channel_id=1, source_target_pairs={{0,4},{4,0},{8,12},{12,8},{16,20},{20,16},{24,28},{28,24},{1,5},{5... | collective-permute-start | bytes 516104 | tf_op jit(solution)/shard_map/ppermute | solution.py:379
  82.0 1.8 %collective-permute-start.34 = (bf16[112,768]{1,0:T(8,128)(2,1)S(1)}, bf16[112,768]{1,0:T(8,128)(2,1)S(1)}, u32[]{:S(2)}, u32[]{:S(2)}) collective-permute-start(bf16[112,768]{1,0:T(8,128)(2,1)S(1)} %collective-permute-done.31.refs_6_.refs_3_), channel_id=1, source_target_pairs={{0,4},{4,0},{8,12},{12,8},{16,20},{20,16},{24,28},{28,24},{1,5},{5... | collective-permute-start | bytes 516104 | tf_op jit(solution)/shard_map/ppermute | solution.py:379
  82.0 1.8 %collective-permute-start.35 = (bf16[112,768]{1,0:T(8,128)(2,1)S(1)}, bf16[112,768]{1,0:T(8,128)(2,1)S(1)}, u32[]{:S(2)}, u32[]{:S(2)}) collective-permute-start(bf16[112,768]{1,0:T(8,128)(2,1)S(1)} %collective-permute-done.32.refs_7_.refs_4_), channel_id=1, source_target_pairs={{0,4},{4,0},{8,12},{12,8},{16,20},{20,16},{24,28},{28,24},{1,5},{5... | collective-permute-start | bytes 516104 | tf_op jit(solution)/shard_map/ppermute | solution.py:379
  (6 other events, 8.3 us)
